TPU v7x, 32 devices: a whole 2x2x4 slice. The times are simulated.
32 devices in a mesh: shard: 2 (over core), replica: 16 (over z, y, x).
Axes of the slice: x: 2, y: 2, z: 4, core: 2. Of those that a mesh axis runs over, the one named last changes fastest.
Arguments:
- tokens: bfloat16 [16, 1024, 1088], P('replica', 'shard'), may hold values from -6 to 6
- documents: int32 [16, 1024], P('replica', 'shard'), may hold values from 0 to 2, as said below
- cotangent: bfloat16 [16, 1024, 1088], P('replica', 'shard'), may hold values from -6 to 6
- w_qkv: bfloat16 [1088, 3264], P('shard'), may hold values from -0.1875 to 0.1875
- w_out: bfloat16 [1088, 1088], P('shard'), may hold values from -1.5 to 1.5
- w_up: bfloat16 [1088, 4352], P('shard'), may hold values from -0.1875 to 0.1875
- w_down: bfloat16 [4352, 1088], P('shard'), may hold values from -0.09375 to 0.09375
- gain_one: bfloat16 [1088], P('shard'), may hold values from 0.25 to 1.75
- shift_one: bfloat16 [1088], P('shard'), may hold values from -4 to 4
- bias_query: bfloat16 [1088], P('shard'), may hold values from -4 to 4
- bias_value: bfloat16 [1088], P('shard'), may hold values from -4 to 4
- bias_out: bfloat16 [1088], P('shard'), may hold values from -4 to 4
- gain_two: bfloat16 [1088], P('shard'), may hold values from 0.25 to 1.75
- shift_two: bfloat16 [1088], P('shard'), may hold values from -4 to 4
- bias_up: bfloat16 [4352], P('shard'), may hold values from -4 to 4
- bias_down: bfloat16 [1088], P('shard'), may hold values from -4 to 4
Outputs:
- output: bfloat16 [16, 1024, 1088], P('replica', 'shard')
- input_grad: bfloat16 [16, 1024, 1088], P('replica', 'shard')
- grad_w_qkv: float32 [1088, 3264], P('shard')
- grad_w_out: float32 [1088, 1088], P('shard')
- grad_w_up: float32 [1088, 4352], P('shard')
- grad_w_down: float32 [4352, 1088], P('shard')
- grad_gain_one: float32 [1088], P('shard')
- grad_shift_one: float32 [1088], P('shard')
- grad_bias_query: float32 [1088], P('shard')
- grad_bias_value: float32 [1088], P('shard')
- grad_bias_out: float32 [1088], P('shard')
- grad_gain_two: float32 [1088], P('shard')
- grad_shift_two: float32 [1088], P('shard')
- grad_bias_up: float32 [4352], P('shard')
- grad_bias_down: float32 [1088], P('shard')
Inputs may be any that keep to these rules, and one draw needn't show every extreme that they name: Each sequence holds three documents whose numbers never fall; each has 128 tokens or more, and document 1 covers positions 511 and 512.
All inputs are finite; a program needn't handle non-finite values.
Results may differ from a plain program's by a relative error of at most 0.012.
Values may be sent and summed in bfloat16 or wider, within the bound.
No kernel may reach another device: no remote copies, remote signals or barrier semaphores. Data moves between devices by JAX's collectives and lax.ppermute only.
A program may use at most 320 MiB of HBM per device.

v0:
```python
import jax
import jax.numpy as jnp
from jax import lax
from jax.sharding import PartitionSpec as P

HDIM = 64


epsilon = 1e-05


def passed_along(block, axis, distance):
    devices = range(lax.axis_size(axis))
    route = [(i - distance, i) for i in devices if i - distance in devices]
    return lax.ppermute(block, axis, route)


def layer_norm(values, gain_row, shift_row):
    center = values - jnp.mean(values, axis=-1, keepdims=True)
    spread = jnp.mean(center * center, axis=-1, keepdims=True)
    return center * lax.rsqrt(spread + epsilon) * gain_row + shift_row


def tanh_gelu(values):
    return jax.nn.gelu(values, approximate=True)


def over_rows(former, latter):
    return lax.dot_general(
        former, latter, (((0,), (0,)), ((), ())), preferred_element_type=jnp.float32
    )


def by_transpose(former, latter):
    return lax.dot_general(
        former, latter, (((1,), (1,)), ((), ())), preferred_element_type=jnp.float32
    )


def shards(
    tokens,
    documents,
    cotangent,
    w_qkv,
    w_out,
    w_up,
    w_down,
    gain_one,
    shift_one,
    bias_query,
    bias_value,
    bias_out,
    gain_two,
    shift_two,
    bias_up,
    bias_down,
):
    bfloat = jnp.bfloat16
    single = jnp.float32
    gathered = (
        lax.all_gather(w_qkv, "shard", axis=0, tiled=True),
        lax.all_gather(w_out, "shard", axis=0, tiled=True),
        lax.all_gather(w_up, "shard", axis=0, tiled=True),
        lax.all_gather(w_down, "shard", axis=0, tiled=True),
        lax.all_gather(gain_one, "shard", axis=0, tiled=True),
        lax.all_gather(shift_one, "shard", axis=0, tiled=True),
        lax.all_gather(bias_query, "shard", axis=0, tiled=True),
        lax.all_gather(bias_value, "shard", axis=0, tiled=True),
        lax.all_gather(bias_out, "shard", axis=0, tiled=True),
        lax.all_gather(gain_two, "shard", axis=0, tiled=True),
        lax.all_gather(shift_two, "shard", axis=0, tiled=True),
        lax.all_gather(bias_up, "shard", axis=0, tiled=True),
        lax.all_gather(bias_down, "shard", axis=0, tiled=True),
    )
    full_qkv, full_out, full_up, full_down = (gathered[0], gathered[1], gathered[2], gathered[3])
    (
        vec_gain_one,
        vec_shift_one,
        vec_query,
        vec_value,
        vec_out,
        vec_gain_two,
        vec_shift_two,
        vec_up,
        vec_down,
    ) = [member.astype(single) for member in gathered[4:]]
    seq_count, length, model_width = tokens.shape
    head_count = model_width // HDIM
    scaling = HDIM ** (-0.5)
    flat_rows = tokens.reshape(seq_count * length, model_width).astype(single)
    normed_one, norm_pull_one = jax.vjp(layer_norm, flat_rows, vec_gain_one, vec_shift_one)
    normed_low = normed_one.astype(bfloat)
    project = jnp.dot(normed_low, full_qkv, preferred_element_type=single)
    query_low = (project[:, :model_width] + vec_query).astype(bfloat)
    key_low = project[:, model_width : 2 * model_width].astype(bfloat)
    value_low = (project[:, 2 * model_width :] + vec_value).astype(bfloat)
    seq_shape = (seq_count, length, model_width)
    earlier_key, earlier_value, earlier_doc = passed_along(
        (key_low.reshape(seq_shape), value_low.reshape(seq_shape), documents.astype(bfloat)),
        "shard",
        1,
    )
    head_shape = (seq_count, length, head_count, HDIM)
    wide_shape = (seq_count, 2 * length, head_count, HDIM)
    query_heads = query_low.reshape(head_shape)
    key_heads = jnp.concatenate([earlier_key, key_low.reshape(seq_shape)], axis=1).reshape(
        wide_shape
    )
    value_heads = jnp.concatenate([earlier_value, value_low.reshape(seq_shape)], axis=1).reshape(
        wide_shape
    )
    places = jnp.arange(length)
    causal = places[None, :] <= places[:, None]
    local_ok = causal[None] & (documents[:, None, :] == documents[:, :, None])
    has_earlier = lax.axis_index("shard") > 0
    earlier_ok = (earlier_doc.astype(jnp.int32)[:, None, :] == documents[:, :, None]) & has_earlier
    allowed = jnp.concatenate([earlier_ok, local_ok], axis=2)[:, None]

    def score_block():
        raw_scores = (
            jnp.einsum("bqhd,bkhd->bhqk", query_heads, key_heads, preferred_element_type=single)
            * scaling
        )
        return jnp.where(allowed, raw_scores, -1e30)

    scores = score_block()
    row_max = jnp.max(scores, axis=-1, keepdims=True)
    exponent = jnp.exp(scores - row_max)
    row_total = jnp.sum(exponent, axis=-1, keepdims=True)
    log_total = row_max + jnp.log(row_total)
    probs_low = (exponent / row_total).astype(bfloat)
    attended = jnp.einsum("bhqk,bkhd->bqhd", probs_low, value_heads, preferred_element_type=single)
    heads_low = attended.reshape(seq_count * length, model_width).astype(bfloat)
    middle = flat_rows + jnp.dot(heads_low, full_out, preferred_element_type=single) + vec_out
    normed_two, norm_pull_two = jax.vjp(layer_norm, middle, vec_gain_two, vec_shift_two)
    normed_two_low = normed_two.astype(bfloat)
    pre_active = jnp.dot(normed_two_low, full_up, preferred_element_type=single) + vec_up
    active, gelu_pull = jax.vjp(tanh_gelu, pre_active)
    active_low = active.astype(bfloat)
    final_rows = middle + jnp.dot(active_low, full_down, preferred_element_type=single) + vec_down
    output = final_rows.astype(bfloat).reshape(tokens.shape)
    back_qkv, back_out, back_up, back_down = (
        lax.all_gather(w_qkv, "shard", axis=0, tiled=True),
        lax.all_gather(w_out, "shard", axis=0, tiled=True),
        lax.all_gather(w_up, "shard", axis=0, tiled=True),
        lax.all_gather(w_down, "shard", axis=0, tiled=True),
    )
    grad_rows = cotangent.reshape(seq_count * length, model_width)
    grad_w_down = over_rows(active_low, grad_rows)
    grad_bias_down = jnp.sum(grad_rows.astype(single), axis=0)
    grad_active = by_transpose(grad_rows, back_down)
    grad_pre = gelu_pull(grad_active)[0].astype(bfloat)
    grad_w_up = over_rows(normed_two_low, grad_pre)
    grad_bias_up = jnp.sum(grad_pre.astype(single), axis=0)
    grad_normed_two = by_transpose(grad_pre, back_up)
    grad_mid_part, grad_gain_two, grad_shift_two = norm_pull_two(grad_normed_two)
    grad_middle = grad_rows.astype(single) + grad_mid_part
    grad_branch = grad_middle.astype(bfloat)
    grad_w_out = over_rows(heads_low, grad_branch)
    grad_bias_out = jnp.sum(grad_branch.astype(single), axis=0)
    grad_heads = by_transpose(grad_branch, back_out).astype(bfloat).reshape(head_shape)
    attn_probs = jnp.exp(score_block() - log_total)
    again_low = attn_probs.astype(bfloat)
    grad_value_all = jnp.einsum(
        "bhqk,bqhd->bkhd", again_low, grad_heads, preferred_element_type=single
    )
    grad_probs = jnp.einsum(
        "bqhd,bkhd->bhqk", grad_heads, value_heads, preferred_element_type=single
    )
    inner_sum = jnp.sum(attn_probs * grad_probs, axis=-1, keepdims=True)
    grad_scores = (attn_probs * (grad_probs - inner_sum)).astype(bfloat)
    grad_query = (
        jnp.einsum("bhqk,bkhd->bqhd", grad_scores, key_heads, preferred_element_type=single)
        * scaling
    )
    grad_key_all = (
        jnp.einsum("bhqk,bqhd->bkhd", grad_scores, query_heads, preferred_element_type=single)
        * scaling
    )
    back_key, back_value = passed_along(
        (grad_key_all[:, :length], grad_value_all[:, :length]), "shard", -1
    )
    row_shape = (seq_count * length, model_width)
    grad_query_low = grad_query.reshape(row_shape).astype(bfloat)
    grad_key_low = (grad_key_all[:, length:] + back_key).reshape(row_shape).astype(bfloat)
    grad_value_low = (grad_value_all[:, length:] + back_value).reshape(row_shape).astype(bfloat)
    grad_project = jnp.concatenate([grad_query_low, grad_key_low, grad_value_low], axis=1)
    grad_w_qkv = over_rows(normed_low, grad_project)
    grad_bias_query = jnp.sum(grad_query_low.astype(single), axis=0)
    grad_bias_value = jnp.sum(grad_value_low.astype(single), axis=0)
    grad_normed_one = by_transpose(grad_project, back_qkv)
    grad_in_part, grad_gain_one, grad_shift_one = norm_pull_one(grad_normed_one)
    input_grad = (grad_middle + grad_in_part).astype(bfloat).reshape(tokens.shape)
    shard_count = lax.axis_size("shard")
    replica_count = lax.axis_size("replica")
    small_grads = [
        grad_gain_one,
        grad_shift_one,
        grad_bias_query,
        grad_bias_value,
        grad_bias_out,
        grad_gain_two,
        grad_shift_two,
        grad_bias_up,
        grad_bias_down,
    ]
    packed = jnp.concatenate([member.reshape(shard_count, -1) for member in small_grads], axis=1)
    matrices = [grad_w_qkv, grad_w_out, grad_w_up, grad_w_down]
    halves = (
        lax.psum_scatter(grad_w_qkv, "shard", scatter_dimension=0, tiled=True),
        lax.psum_scatter(grad_w_out, "shard", scatter_dimension=0, tiled=True),
        lax.psum_scatter(grad_w_up, "shard", scatter_dimension=0, tiled=True),
        lax.psum_scatter(grad_w_down, "shard", scatter_dimension=0, tiled=True),
        lax.psum_scatter(packed, "shard", scatter_dimension=0, tiled=True),
    )
    flat_terms = [member.reshape(replica_count, -1) for member in halves]
    owned_part = (
        lax.psum_scatter(flat_terms[0], "replica", scatter_dimension=0, tiled=True),
        lax.psum_scatter(flat_terms[1], "replica", scatter_dimension=0, tiled=True),
        lax.psum_scatter(flat_terms[2], "replica", scatter_dimension=0, tiled=True),
        lax.psum_scatter(flat_terms[3], "replica", scatter_dimension=0, tiled=True),
        lax.psum_scatter(flat_terms[4], "replica", scatter_dimension=0, tiled=True),
    )
    summed = (
        lax.all_gather(owned_part[0], "replica", axis=0, tiled=True),
        lax.all_gather(owned_part[1], "replica", axis=0, tiled=True),
        lax.all_gather(owned_part[2], "replica", axis=0, tiled=True),
        lax.all_gather(owned_part[3], "replica", axis=0, tiled=True),
        lax.all_gather(owned_part[4], "replica", axis=0, tiled=True),
    )
    owned_mats = [
        summed[position].reshape(
            matrices[position].shape[0] // shard_count, matrices[position].shape[1]
        )
        for position in range(4)
    ]
    small_flat = summed[4].reshape(-1)
    owned_small = []
    offset = 0
    for member in small_grads:
        piece_len = member.shape[0] // shard_count
        owned_small.append(small_flat[offset : offset + piece_len])
        offset = offset + piece_len
    return (
        output,
        input_grad,
        owned_mats[0],
        owned_mats[1],
        owned_mats[2],
        owned_mats[3],
        owned_small[0],
        owned_small[1],
        owned_small[2],
        owned_small[3],
        owned_small[4],
        owned_small[5],
        owned_small[6],
        owned_small[7],
        owned_small[8],
    )


def solution(mesh):
    placed = (
        P("replica", "shard", None),
        P("replica", "shard"),
        P("replica", "shard", None),
        P("shard", None),
        P("shard", None),
        P("shard", None),
        P("shard", None),
        P("shard"),
        P("shard"),
        P("shard"),
        P("shard"),
        P("shard"),
        P("shard"),
        P("shard"),
        P("shard"),
        P("shard"),
    )
    return jax.shard_map(
        shards,
        mesh=mesh,
        in_specs=placed,
        out_specs=(
            P("replica", "shard", None),
            P("replica", "shard", None),
            P("shard", None),
            P("shard", None),
            P("shard", None),
            P("shard", None),
            P("shard"),
            P("shard"),
            P("shard"),
            P("shard"),
            P("shard"),
            P("shard"),
            P("shard"),
            P("shard"),
            P("shard"),
        ),
        check_vma=False,
    )
```

profile of v0, /device:TPU:0, one launch (start us, length us, event | category | flops | bytes accessed | tf_op | source)
XLA Modules:
  0.0 1661.6 jit_solution(17667897794083296566)
XLA Ops:
  15.4 4.0 all-reduce.15
  22.5 8.0 all-gather.15.cloned.1.call-done
  30.4 7.2 fusion.70
  46.4 4.0 fusion.33
  52.9 18.0 %fusion.6 = (f32[17,512]{1,0:T(8,128)S(1)}, f32[17,512,1024]{2,1,0:T(8,128)}) fusion(pred[512,1024]{1,0:T(8,128)(4,1)S(1)} %add_bitcast_fusion, bf16[512,17,64]{0,2,1:T(8,128)(2,1)S(1)} %bitcast.134, bf16[1,512,17,64]{1,3,2,0:T(8,128)(2,1)S(1)} %bitcast.136, bf16[1,512,17,64]{1,3,2,0:T(8,128)(2,1)S(1)} %bitcast.138), kind=kOutput, calls=%fused_computation.11 | convolution fusion | flops 1172037120 | bytes 39553024 | tf_op jit(solution)/shard_map/bqhd,bkhd->bhqk/dot_general | solution.py:121
  70.9 17.6 %fusion = f32[17,512]{1,0:T(8,128)S(1)} fusion(f32[17,512]{1,0:T(8,128)S(1)} %get-tuple-element.86, f32[17,512,1024]{2,1,0:T(8,128)} %get-tuple-element.87, pred[512,1024]{1,0:T(8,128)(4,1)S(1)} %add_bitcast_fusion), kind=kLoop, calls=%fused_computation.6 | loop fusion | flops 35642880 | bytes 36245504 | tf_op jit(solution)/shard_map/reduce_sum | solution.py:129
  88.6 17.3 %fusion.43 = bf16[17,64,512]{2,1,0:T(8,128)(2,1)} fusion(f32[17,512]{1,0:T(8,128)S(1)} %fusion, f32[17,512]{1,0:T(8,128)S(1)} %get-tuple-element.86, f32[17,512,1024]{2,1,0:T(8,128)} %get-tuple-element.87, pred[512,1024]{1,0:T(8,128)(4,1)S(1)} %add_bitcast_fusion, bf16[1,512,17,64]{1,3,2,0:T(8,128)(2,1)} %bitcast.4, bf16[1,512,17,64]{1,3,2,0:T(8,128)(2,1)} %bitcast.3), kind=kOutput, calls=%fused_computation.78 | convolution fusion | flops 1190428672 | bytes 39587840 | tf_op jit(solution)/shard_map/bhqk,bkhd->bqhd/dot_general | solution.py:132
  105.9 4.1 fusion.80
  110.4 12.7 fusion.73
  123.0 17.2 %convert_reduce_fusion = (f32[4352]{0:T(1024)}, bf16[512,4352]{1,0:T(8,128)(2,1)S(1)}) fusion(f32[512,4352]{1,0:T(8,128)} %fusion.73, f32[4352]{0:T(1024)S(1)} %reshape.495, bf16[4352,1088]{0,1:T(8,128)(2,1)} %all-gather.21.cloned.1.call-done, bf16[1,512,1088]{1,2,0:T(8,128)(2,1)} %param.18), kind=kOutput, calls=%fused_computation.21 | convolution fusion | flops 4899860480 | bytes 23988224 | tf_op jit(solution)/shard_map/dot_general | solution.py:35
  140.3 6.3 multiply_reduce_fusion.1
  149.9 3.9 fusion.81
  153.8 4.6 convolution_convert_fusion
  158.4 18.1 %fusion.40 = f32[1,1024,17,64]{1,3,2,0:T(8,128)} fusion(bf16[512,17,64]{0,2,1:T(8,128)(2,1)} %bitcast.142, f32[17,512]{1,0:T(8,128)S(1)} %log_add_fusion, f32[17,512,1024]{2,1,0:T(8,128)} %get-tuple-element.87, pred[512,1024]{1,0:T(8,128)(4,1)S(1)} %add_bitcast_fusion), kind=kOutput, calls=%fused_computation.76 | convolution fusion | flops 1176502272 | bytes 41781248 | tf_op jit(solution)/shard_map/bhqk,bqhd->bkhd/dot_general | solution.py:164
  181.1 27.4 %multiply_reduce_fusion = (f32[17,512]{1,0:T(8,128)S(1)}, f32[17,512,1024]{2,1,0:T(8,128)}) fusion(f32[17,512]{1,0:T(8,128)S(1)} %log_add_fusion, f32[17,512,1024]{2,1,0:T(8,128)} %get-tuple-element.87, pred[512,1024]{1,0:T(8,128)(4,1)S(1)} %add_bitcast_fusion, bf16[512,17,64]{0,2,1:T(8,128)(2,1)} %bitcast.143, bf16[512,17,64]{0,2,1:T(8,128)(2,1)} %bitcast.21, ...), kind=kOutput, calls=%fused_computation.1 | convolution fusion | flops 1189862912 | bytes 75239424 | tf_op jit(solution)/shard_map/bqhd,bkhd->bhqk/dot_general | solution.py:167
  208.5 29.5 %multiply_convert_fusion = bf16[17,512,1024]{2,1,0:T(8,128)(2,1)} fusion(f32[17,512,1024]{2,1,0:T(8,128)} %get-tuple-element.92, f32[17,512]{1,0:T(8,128)S(1)} %get-tuple-element.91, f32[17,512]{1,0:T(8,128)S(1)} %log_add_fusion, f32[17,512,1024]{2,1,0:T(8,128)} %get-tuple-element.87, pred[512,1024]{1,0:T(8,128)(4,1)S(1)} %add_bitcast_fusion), kind=kLoop, calls=%fused_computation | loop fusion | flops 53477376 | bytes 89722880 | tf_op jit(solution)/shard_map/convert_element_type | solution.py:171
  238.1 9.6 multiply_bitcast_fusion
  250.6 10.8 convert_reduce_fusion.5
  267.7 10.2 fusion.46
  278.0 19.9 %fusion.49 = f32[4352,1088]{0,1:T(8,128)} fusion(bf16[1,512,1088]{1,2,0:T(8,128)(2,1)} %param.18, f32[512,4352]{1,0:T(8,128)} %fusion.73, f32[4352]{0:T(1024)S(1)} %reshape.495), kind=kOutput, calls=%fused_computation.84 | convolution fusion | flops 4870897664 | bytes 28984320 | tf_op jit(solution)/shard_map/dot_general | solution.py:29
  298.6 12.8 fusion.72
  311.5 3.8 reshape.441
  315.3 9.4 reshape.439
  324.7 13.7 reduce-scatter.11.cloned.1.call-done
  338.3 11.8 copy.33
  350.2 16.3 reshape.445
  366.5 3.9 reduce-scatter.9.cloned.1.call-done
  370.4 12.1 reshape.443
  383.7 741.3 %all-reduce.18.cloned.1.call-done = (f32[16,110976]{1,0:T(8,128)}, f32[16,36992]{1,0:T(8,128)}, f32[16,147968]{1,0:T(8,128)}, f32[16,147968]{1,0:T(8,128)}) async-done(((f32[16,110976]{1,0:T(8,128)}, f32[16,36992]{1,0:T(8,128)}, f32[16,147968]{1,0:T(8,128)}, f32[16,147968]{1,0:T(8,128)}), (f32[16,110976]{1,0:T(8,128)}, f32[16,36992]{1,0:T(8,128)}, f32[16,147968]{1,0:T(8,128)}, ...) | async-done | bytes 28409872
  1127.8 3.7 dynamic-slice_bitcast_fusion.2
  1131.6 4.0 dynamic-slice_bitcast_fusion.1
  1135.6 4.4 dynamic-slice_bitcast_fusion
  1140.4 12.7 fusion.22
  1153.1 7.3 fusion.74
  1163.1 4.0 convert_reduce_fusion.1
  1167.4 3.6 all-reduce.12
  1171.8 74.3 %all-reduce.13 = f32[16,408]{1,0:T(8,128)S(1)} all-reduce(f32[16,408]{1,0:T(8,128)S(1)} %reshape.456), channel_id=11, replica_groups=mesh['shard'=2,'replica'=16] {'replica'}, use_global_device_ids=true, to_apply=%region_29.30.clone | all-reduce | flops 6528 | bytes 52224
  1246.7 37.1 %all-gather.5 = f32[16,1,408]{2,1,0:T(1,128)S(1)} all-gather(f32[1,1,408]{2,1,0:T(1,128)S(1)} %dynamic-slice_bitcast_fusion.4), channel_id=1, replica_groups=mesh['shard'=2,'replica'=16] {'replica'}, dimensions={0}, use_global_device_ids=true | all-gather | bytes 27744 | tf_op jit(solution)/shard_map/all_gather | solution.py:229
  1285.4 7.3 reduce.13
  1295.3 76.0 %reduce.12 = f32[16,110976]{1,0:T(8,128)} reduce(f32[16,1,110976]{2,1,0:T(1,128)} %all-gather.23.cloned.1.call-done, f32[]{:T(128)} %constant.119), dimensions={1}, to_apply=%all-gather.1.reduce_sub_computation | reduce | bytes 14204932 | tf_op jit(solution)/shard_map/all_gather | solution.py:225
  1371.3 6.4 reshape.440
  1377.7 42.1 %all-gather.27.cloned.1.call-done = f32[16,1,147968]{2,1,0:T(1,128)} async-done(((f32[1,1,147968]{2,1,0:T(1,128)}), f32[16,1,147968]{2,1,0:T(1,128)}) %all-gather.27.cloned.1.call-update) | async-done | bytes 9469968 | tf_op jit(solution)/shard_map/all_gather | solution.py:227
  1419.8 86.2 %reduce.14 = f32[16,147968]{1,0:T(8,128)} reduce(f32[16,1,147968]{2,1,0:T(1,128)} %all-gather.27.cloned.1.call-done, f32[]{:T(128)} %constant.119), dimensions={1}, to_apply=%all-gather.3.reduce_sub_computation | reduce | bytes 18939908 | tf_op jit(solution)/shard_map/all_gather | solution.py:227
  1506.0 11.1 reshape.444
  1517.2 26.7 %all-gather.29.cloned.1.call-done = f32[16,1,147968]{2,1,0:T(1,128)} async-done(((f32[1,1,147968]{2,1,0:T(1,128)}), f32[16,1,147968]{2,1,0:T(1,128)}) %all-gather.29.cloned.1.call-update) | async-done | bytes 9469968 | tf_op jit(solution)/shard_map/all_gather | solution.py:228
  1543.9 86.2 %reduce.15 = f32[16,147968]{1,0:T(8,128)} reduce(f32[16,1,147968]{2,1,0:T(1,128)} %all-gather.29.cloned.1.call-done, f32[]{:T(128)} %constant.119), dimensions={1}, to_apply=%all-gather.4.reduce_sub_computation | reduce | bytes 18939908 | tf_op jit(solution)/shard_map/all_gather | solution.py:228
  1630.1 12.7 reshape.446
  1642.7 12.1 copy.34
  (223 shorter events, 52.4 us)
Async XLA Ops:
  7.2 23.3 %all-gather.15.cloned.1.call-start = ((), (), s32[]{:S(2)}) async-start(), calls=%async_computation.4 | async-start | bytes 10862592 | tf_op jit(solution)/shard_map/all_gather | solution.py:61
  7.9 98.0 %all-gather.17.cloned.1.call-start = ((), (), s32[]{:S(2)}) async-start(), calls=%async_computation.5 | async-start | bytes 3760128 | tf_op jit(solution)/shard_map/all_gather | solution.py:62
  8.7 101.7 %all-gather.19.cloned.1.call-start = ((), (), s32[]{:S(2)}) async-start(), calls=%async_computation.6 | async-start | bytes 14204928 | tf_op jit(solution)/shard_map/all_gather | solution.py:63
  9.4 113.6 %all-gather.21.cloned.1.call-start = ((), (), s32[]{:S(2)}) async-start(), calls=%async_computation.7 | async-start | bytes 14204928 | tf_op jit(solution)/shard_map/all_gather | solution.py:64
  9.5 4.0 copy-start.42
  9.5 4.2 copy-start.43
  9.5 4.4 copy-start.44
  9.5 4.7 copy-start.45
  9.5 4.9 copy-start.46
  9.5 5.1 copy-start.47
  9.6 5.4 copy-start.48
  9.6 5.6 copy-start.49
  9.6 9.8 copy-start.2
  9.6 34.5 %collective-permute-start.1 = (bf16[1,512]{1,0:T(2,128)(2,1)S(1)}, bf16[1,512]{1,0:T(2,128)(2,1)S(1)}, u32[]{:S(2)}, u32[]{:S(2)}) collective-permute-start(bf16[1,512]{1,0:T(2,128)(2,1)S(1)} %convert_element_type.147), channel_id=1, source_target_pairs={{0,16},{1,17},{2,18},{3,19},{4,20},{5,21},{6,22},{7,23},{8,24},{9,... | collective-permute-start | bytes 3080 | tf_op jit(solution)/shard_map/ppermute | solution.py:15
  12.1 8.5 copy-start.39
  12.1 299.4 %reduce-scatter.7.cloned.1.call-start = ((), (), s32[]{:S(2)}) async-start(), calls=%async_computation.9 | async-start | bytes 7520256 | tf_op jit(solution)/shard_map/reduce_scatter | solution.py:211
  19.4 18.3 %copy-start.35 = (f32[1088]{0:T(1024)}, f32[1088]{0:T(1024)S(1)}, u32[]{:S(2)}) copy-start(f32[1088]{0:T(1024)S(1)} %convert_element_type.143) | copy-start | bytes 13060
  19.4 18.3 %copy-start.22 = (f32[1088]{0:T(1024)}, f32[1088]{0:T(1024)S(1)}, u32[]{:S(2)}) copy-start(f32[1088]{0:T(1024)S(1)} %convert_element_type.142) | copy-start | bytes 13060
  19.7 18.0 %copy-start.24 = (f32[512]{0:T(512)}, f32[512]{0:T(512)S(1)}, u32[]{:S(2)}) copy-start(f32[512]{0:T(512)S(1)} %broadcast_multiply_fusion.1) | copy-start | bytes 6148
  20.6 17.1 %copy-start.29 = (f32[512]{0:T(512)}, f32[512]{0:T(512)S(1)}, u32[]{:S(2)}) copy-start(f32[512]{0:T(512)S(1)} %fusion.57) | copy-start | bytes 6148
  41.8 11.1 collective-permute-start.2
  44.1 66.3 %copy-start.20 = (f32[1088]{0:T(1024)}, f32[1088]{0:T(1024)S(1)}, u32[]{:S(2)}) copy-start(f32[1088]{0:T(1024)S(1)} %convert_element_type.157) | copy-start | bytes 13060
  46.3 6.6 copy-start.6
  50.4 20.5 %copy-start.4 = (bf16[512,1088]{0,1:T(8,128)(2,1)}, bf16[512,1088]{0,1:T(8,128)(2,1)S(1)}, u32[]{:S(2)}) copy-start(bf16[512,1088]{0,1:T(8,128)(2,1)S(1)} %get-tuple-element.71) | copy-start | bytes 3342340
  50.4 38.2 %collective-permute-start = (bf16[1,512,1088]{1,2,0:T(8,128)(2,1)}, bf16[1,512,1088]{1,2,0:T(8,128)(2,1)}, u32[]{:S(2)}, u32[]{:S(2)}) collective-permute-start(bf16[1,512,1088]{1,2,0:T(8,128)(2,1)} %bitcast.2), channel_id=1, source_target_pairs={{0,16},{1,17},{2,18},{3,19},{4,20},{5,21},{6,22},{7,23},{8,24},{9,... | collective-permute-start | bytes 3342344 | tf_op jit(solution)/shard_map/ppermute | solution.py:15
  52.9 18.0 %copy-start.11 = (bf16[1,512,1088]{1,2,0:T(8,128)(2,1)}, bf16[1,512,1088]{1,2,0:T(8,128)(2,1)S(1)}, u32[]{:S(2)}) copy-start(bf16[1,512,1088]{1,2,0:T(8,128)(2,1)S(1)} %collective-permute-done.2) | copy-start | bytes 3342340
  123.0 17.2 %copy-start.5 = (bf16[1088,4352]{1,0:T(8,128)(2,1)S(1)}, bf16[1088,4352]{1,0:T(8,128)(2,1)}, u32[]{:S(2)}) copy-start(bf16[1088,4352]{1,0:T(8,128)(2,1)} %all-gather.19.cloned.1.call-done) | copy-start | bytes 28409860
  140.3 6.3 copy-start.52
  179.7 81.7 %collective-permute-start.4 = (f32[1,512,17,64]{1,3,2,0:T(8,128)}, f32[1,512,17,64]{1,3,2,0:T(8,128)}, u32[]{:S(2)}, u32[]{:S(2)}) collective-permute-start(f32[1,512,17,64]{1,3,2,0:T(8,128)} %slice.71), channel_id=1, source_target_pairs={{16,0},{17,1},{18,2},{19,3},{20,4},{21,5},{22,6},{23,7},{24,8},{25... | collective-permute-start | bytes 6684680 | tf_op jit(solution)/shard_map/ppermute | solution.py:15
  181.0 134.3 %reduce-scatter.5.cloned.1.call-start = ((), (), s32[]{:S(2)}) async-start(), calls=%async_computation.8 | async-start | bytes 21725184 | tf_op jit(solution)/shard_map/reduce_scatter | solution.py:210
  249.3 14.8 collective-permute-start.3
  264.1 3.6 copy-start.3
  278.0 60.4 %reduce-scatter.11.cloned.1.call-start = ((), (), s32[]{:S(2)}) async-start(), calls=%async_computation.11 | async-start | bytes 28409856 | tf_op jit(solution)/shard_map/reduce_scatter | solution.py:213
  297.9 72.5 %reduce-scatter.9.cloned.1.call-start = ((), (), s32[]{:S(2)}) async-start(), calls=%async_computation.10 | async-start | bytes 28409856 | tf_op jit(solution)/shard_map/reduce_scatter | solution.py:212
  311.4 813.6 %all-reduce.18.cloned.1.call-start = ((), (), s32[]{:S(2)}) async-start(), calls=%async_computation.16 | async-start | bytes 56819712
  382.5 902.9 %all-gather.25.cloned.1.call-start = ((), (), s32[]{:S(2)}) async-start(), calls=%async_computation.13 | async-start | bytes 2515456 | tf_op jit(solution)/shard_map/all_gather | solution.py:226
  1127.7 167.6 %all-gather.23.cloned.1.call-start = ((), (), s32[]{:S(2)}) async-start(), calls=%async_computation.12 | async-start | bytes 7546368 | tf_op jit(solution)/shard_map/all_gather | solution.py:225
  1131.5 8.5 copy-start.40
  1131.5 8.6 copy-start.26
  1131.5 8.7 copy-start.38
  1131.5 8.8 copy-start.37
  1131.5 8.9 copy-start.27
  1131.6 288.3 %all-gather.27.cloned.1.call-start = ((), (), s32[]{:S(2)}) async-start(), calls=%async_computation.14 | async-start | bytes 10061824 | tf_op jit(solution)/shard_map/all_gather | solution.py:227
  1135.6 408.3 %all-gather.29.cloned.1.call-start = ((), (), s32[]{:S(2)}) async-start(), calls=%async_computation.15 | async-start | bytes 10061824 | tf_op jit(solution)/shard_map/all_gather | solution.py:228
  1140.4 12.7 copy-start.14
  1140.4 12.7 copy-start.16
  1140.4 12.7 copy-start.18
  1153.1 7.3 copy-start.34
  (23 other events, 50.1 us)
Sparse Core Ops, SparseCore 0:
  9.6 20.8 all-gather.14
  32.0 12.3 all-gather.16
  45.9 23.0 all-gather.18
  70.4 23.0 all-gather.20
  181.2 16.3 reduce-scatter.6
  278.1 28.4 reduce-scatter.4
  308.9 29.4 reduce-scatter.10
  340.6 29.6 reduce-scatter.8
  382.6 742.3 all-reduce.17
  1128.6 61.8 all-gather.24
  1194.2 101.0 all-gather.22
  1298.8 121.0 all-gather.26
  1422.9 120.9 all-gather.28
where the time goes:
time: 1670 us; the launch traced here: 1660 us
  waiting for transfers between devices  839 us (50%)
  other arithmetic  320 us (19%)
  matrix products  220 us (13%)
  local copies, waits for them, and re-layouts  136 us (8%)
  blocking collectives  121 us (7%)
    unnamed x14, waiting for transfers between devices  744 us
    all_gather x1, other arithmetic, shards(): lax.all_gather(owned_part[2], 'replica', axis=0, tiled=True)  86.2 us
    all_gather x1, other arithmetic, shards(): lax.all_gather(owned_part[3], 'replica', axis=0, tiled=True)  86.2 us
    unnamed x3, blocking collectives  81.9 us
    all_gather x1, other arithmetic, shards(): lax.all_gather(owned_part[0], 'replica', axis=0, tiled=True)  76 us
    dot_general x4, matrix products, over_rows(): lax.dot_general(former, latter, (((0,), (0,)), ((), ())), preferred_eleme...  46.8 us
    all_gather x1, waiting for transfers between devices, shards(): lax.all_gather(owned_part[2], 'replica', axis=0, tiled=True)  42.1 us
    reshape x5, local copies, waits for them, and re-layouts, shards(): flat_terms = [member.reshape(replica_count, -1) for member in halves]  41.6 us
  transfers between devices with their start and end apart: 18, of which 7 were waited for; matrix products, arithmetic and copies ran while one was open for 29% of the time, Pallas kernels for 0%

commit v1 on v0

v1 whole, which is shorter than its diff:
```python
import jax
import jax.numpy as jnp
from jax import lax
from jax.experimental import pallas as pl
from jax.experimental.pallas import tpu as pltpu
from jax.sharding import PartitionSpec as P

HDIM = 64
SCALE = HDIM ** (-0.5)
SKIP = 128
epsilon = 1e-05
bfloat = jnp.bfloat16
single = jnp.float32


def dot(former, latter, former_axis, latter_axis):
    return lax.dot_general(
        former,
        latter,
        (((former_axis,), (latter_axis,)), ((), ())),
        preferred_element_type=single,
    )


def query_chunks(length):
    early = length - SKIP
    half = length // 2
    cuts = [(0, half, 0), (half, early, 0), (early, length, early)]
    return [(a, b, first, early + b) for a, b, first in cuts]


def fill_bias(bias_ref, doc_row_ref, doc_col_ref, early_col_ref, flag_ref):
    length = doc_row_ref.shape[1]
    early = length - SKIP
    row = doc_row_ref[...]
    ok = (early_col_ref[SKIP:, :] == row) & (flag_ref[0] > 0)
    bias_ref[:early, :] = jnp.where(ok, 0.0, -1e30)
    key_at = lax.broadcasted_iota(jnp.int32, (length, length), 0)
    query_at = lax.broadcasted_iota(jnp.int32, (length, length), 1)
    ok = (doc_col_ref[...] == row) & (key_at <= query_at)
    bias_ref[early:, :] = jnp.where(ok, 0.0, -1e30)


def attend_kernel(
    flag_ref,
    doc_row_ref,
    doc_col_ref,
    early_col_ref,
    q_ref,
    k_ref,
    v_ref,
    ek_ref,
    ev_ref,
    o_ref,
    lse_ref,
    bias_ref,
    kk_ref,
    vv_ref,
):
    length = q_ref.shape[1]
    early = length - SKIP

    @pl.when(pl.program_id(0) == 0)
    def _():
        fill_bias(bias_ref, doc_row_ref, doc_col_ref, early_col_ref, flag_ref)

    kk_ref[:, :early] = ek_ref[...]
    kk_ref[:, early:] = k_ref[...]
    vv_ref[:, :early] = ev_ref[...]
    vv_ref[:, early:] = v_ref[...]
    for a, b, first, last in query_chunks(length):
        scores = dot(kk_ref[:, first:last], q_ref[:, a:b], 0, 0) * SCALE
        scores = scores + bias_ref[first:last, a:b]
        top = jnp.max(scores, axis=0, keepdims=True)
        exponent = jnp.exp(scores - top)
        norm = jnp.sum(exponent, axis=0, keepdims=True)
        out = dot(vv_ref[:, first:last], exponent.astype(bfloat), 1, 0) / norm
        o_ref[:, a:b] = out.astype(bfloat)
        lse_ref[0, :, a:b] = top + jnp.log(norm)


def attend_back_kernel(
    flag_ref,
    doc_row_ref,
    doc_col_ref,
    early_col_ref,
    q_ref,
    k_ref,
    v_ref,
    ek_ref,
    ev_ref,
    g_ref,
    o_ref,
    lse_ref,
    dq_ref,
    dk_ref,
    dv_ref,
    dek_ref,
    dev_ref,
    bias_ref,
    kk_ref,
    vv_ref,
    dkk_ref,
    dvv_ref,
):
    length = q_ref.shape[1]
    early = length - SKIP

    @pl.when(pl.program_id(0) == 0)
    def _():
        fill_bias(bias_ref, doc_row_ref, doc_col_ref, early_col_ref, flag_ref)

    kk_ref[:, :early] = ek_ref[...]
    kk_ref[:, early:] = k_ref[...]
    vv_ref[:, :early] = ev_ref[...]
    vv_ref[:, early:] = v_ref[...]
    dkk_ref[...] = jnp.zeros_like(dkk_ref)
    dvv_ref[...] = jnp.zeros_like(dvv_ref)
    for a, b, first, last in query_chunks(length):
        queries = q_ref[:, a:b]
        grads = g_ref[:, a:b]
        keys = kk_ref[:, first:last]
        values = vv_ref[:, first:last]
        inner = jnp.sum(
            grads.astype(single) * o_ref[:, a:b].astype(single), axis=0, keepdims=True
        )
        scores = dot(keys, queries, 0, 0) * SCALE + bias_ref[first:last, a:b]
        probs = jnp.exp(scores - lse_ref[0, :, a:b])
        grad_probs = dot(values, grads, 0, 0)
        grad_scores = (probs * (grad_probs - inner)).astype(bfloat)
        dvv_ref[:, first:last] += dot(grads, probs.astype(bfloat), 1, 1)
        dkk_ref[:, first:last] += dot(queries, grad_scores, 1, 1)
        dq_ref[:, a:b] = (dot(keys, grad_scores, 1, 0) * SCALE).astype(bfloat)
    dk_ref[...] = dkk_ref[:, early:] * SCALE
    dv_ref[...] = dvv_ref[:, early:]
    dek_ref[...] = (dkk_ref[:, :early] * SCALE).astype(bfloat)
    dev_ref[...] = dvv_ref[:, :early].astype(bfloat)


def attention_specs(length, heads):
    early = length - SKIP
    block = lambda skip: pl.BlockSpec((HDIM, length), lambda h: (h + skip, 0))
    early_block = lambda skip: pl.BlockSpec((HDIM, early), lambda h: (h + skip, 0))
    whole = lambda shape: pl.BlockSpec(shape, lambda h: (0, 0))
    row_block = pl.BlockSpec((1, 1, length), lambda h: (h, 0, 0))
    inputs = [
        pl.BlockSpec(memory_space=pltpu.SMEM),
        whole((1, length)),
        whole((length, 1)),
        whole((length, 1)),
        block(0),
        block(heads),
        block(2 * heads),
        early_block(0),
        early_block(heads),
    ]
    scratch = [
        pltpu.VMEM((length + early, length), single),
        pltpu.VMEM((HDIM, length + early), bfloat),
        pltpu.VMEM((HDIM, length + early), bfloat),
    ]
    return block(0), early_block(0), row_block, inputs, scratch


def attend(flag, documents, early_docs, qkv, early_kv):
    width, length = qkv.shape[0] // 3, qkv.shape[1]
    heads = width // HDIM
    block, _, row_block, inputs, scratch = attention_specs(length, heads)
    return pl.pallas_call(
        attend_kernel,
        grid=(heads,),
        in_specs=inputs,
        out_specs=[block, row_block],
        out_shape=[
            jax.ShapeDtypeStruct((width, length), bfloat),
            jax.ShapeDtypeStruct((heads, 1, length), single),
        ],
        scratch_shapes=scratch,
        compiler_params=pltpu.CompilerParams(vmem_limit_bytes=32 * 2**20),
        cost_estimate=pl.CostEstimate(
            flops=12 * 10**9, bytes_accessed=6 * 10**6, transcendentals=0
        ),
        name="attend",
    )(
        flag,
        documents.reshape(1, length),
        documents.reshape(length, 1),
        early_docs.reshape(length, 1),
        qkv,
        qkv,
        qkv,
        early_kv,
        early_kv,
    )


def attend_back(flag, documents, early_docs, qkv, early_kv, grads, outs, lse):
    width, length = qkv.shape[0] // 3, qkv.shape[1]
    heads = width // HDIM
    early = length - SKIP
    block, early_block, row_block, inputs, scratch = attention_specs(length, heads)
    return pl.pallas_call(
        attend_back_kernel,
        grid=(heads,),
        in_specs=inputs + [block, block, row_block],
        out_specs=[block, block, block, early_block, early_block],
        out_shape=[
            jax.ShapeDtypeStruct((width, length), bfloat),
            jax.ShapeDtypeStruct((width, length), single),
            jax.ShapeDtypeStruct((width, length), single),
            jax.ShapeDtypeStruct((width, early), bfloat),
            jax.ShapeDtypeStruct((width, early), bfloat),
        ],
        scratch_shapes=scratch
        + [
            pltpu.VMEM((HDIM, length + early), single),
            pltpu.VMEM((HDIM, length + early), single),
        ],
        compiler_params=pltpu.CompilerParams(vmem_limit_bytes=32 * 2**20),
        cost_estimate=pl.CostEstimate(
            flops=30 * 10**9, bytes_accessed=12 * 10**6, transcendentals=0
        ),
        name="attend_back",
    )(
        flag,
        documents.reshape(1, length),
        documents.reshape(length, 1),
        early_docs.reshape(length, 1),
        qkv,
        qkv,
        qkv,
        early_kv,
        early_kv,
        grads,
        outs,
        lse,
    )


def swapped(block):
    return lax.ppermute(block, "shard", [(0, 1), (1, 0)])


def halves(block, at):
    middle = block.shape[0] // 2
    lower, upper = block[:middle], block[middle:]
    first = at == 0
    return jnp.where(first, lower, upper), jnp.where(first, upper, lower)


def both_tokens(mine, arrived):
    return jnp.concatenate([mine, arrived], axis=1)


def partners(count, bit):
    return [(i, i ^ (1 << bit)) for i in range(count)]


def window(rows):
    return -(-rows // 16) * 8


def summed_product(former, latter, order):
    count = lax.axis_size("replica")
    at = lax.axis_index("replica")
    if not order:
        return lax.psum(dot(former, latter, 1, 1), "replica")
    sizes = []
    total = None
    for bit in order:
        source = former if total is None else total
        rows = source.shape[0]
        size = window(rows)
        low = ((at >> bit) & 1) == 0
        lower, upper = source[:size], source[rows - size :]
        sent, kept = jnp.where(low, upper, lower), jnp.where(low, lower, upper)
        if total is None:
            sent = dot(sent, latter, 1, 1)
            kept = dot(kept, latter, 1, 1)
        arrived = lax.ppermute(sent.astype(bfloat), "replica", partners(count, bit))
        total = kept + arrived.astype(single)
        sizes.append(rows)
    whole = total.astype(bfloat)
    for bit, rows in zip(order[::-1], sizes[::-1]):
        low = ((at >> bit) & 1) == 0
        arrived = lax.ppermute(whole, "replica", partners(count, bit))
        lower, upper = jnp.where(low, whole, arrived), jnp.where(low, arrived, whole)
        whole = jnp.concatenate([lower, upper[2 * window(rows) - rows :]], axis=0)
    return whole.astype(single)


def summed_small(values):
    count = lax.axis_size("replica")
    if count & (count - 1):
        return lax.psum(values, "replica")
    for bit in range(count.bit_length() - 1):
        values = values + lax.ppermute(values, "replica", partners(count, bit))
    return values


def orders():
    count = lax.axis_size("replica")
    if count & (count - 1):
        return (), ()
    bits = tuple(range(count.bit_length() - 1))
    return bits, bits[1:2] + bits[:1] + bits[2:]


def normalize(values):
    center = values - jnp.mean(values, axis=0, keepdims=True)
    spread = jnp.mean(center * center, axis=0, keepdims=True)
    scale = lax.rsqrt(spread + epsilon)
    return center * scale, scale


def normalize_back(grad, normal, scale, gain):
    z = grad * gain
    z_mean = jnp.mean(z, axis=0, keepdims=True)
    zn_mean = jnp.mean(z * normal, axis=0, keepdims=True)
    part = (z - z_mean - normal * zn_mean) * scale
    return part, jnp.sum(grad * normal, axis=1), jnp.sum(grad, axis=1)


def tanh_gelu(values):
    return jax.nn.gelu(values, approximate=True)


def shards(
    tokens,
    documents,
    cotangent,
    w_qkv,
    w_out,
    w_up,
    w_down,
    gain_one,
    shift_one,
    bias_query,
    bias_value,
    bias_out,
    gain_two,
    shift_two,
    bias_up,
    bias_down,
):
    at = lax.axis_index("shard")
    first = at == 0
    flag = at.astype(jnp.int32).reshape(1)
    order_one, order_two = orders()
    docs = documents[0]
    early_docs = lax.ppermute(docs, "shard", [(0, 1)])

    other_qkv = swapped(w_qkv)
    vectors = jnp.stack(
        [
            gain_one,
            shift_one,
            bias_query,
            bias_value,
            bias_out,
            gain_two,
            shift_two,
            bias_down,
        ]
    )
    other_vectors, other_up_bias = swapped((vectors, bias_up))
    full_out = lax.all_gather(w_out, "shard", axis=0, tiled=True)
    full_up = lax.all_gather(w_up, "shard", axis=0, tiled=True)
    full_down = lax.all_gather(w_down.T, "shard", axis=1, tiled=True)

    def ordered(mine, other, axis):
        return jnp.concatenate(
            [jnp.where(first, mine, other), jnp.where(first, other, mine)], axis=axis
        )

    columns = ordered(vectors, other_vectors, 1).T.astype(single)
    (
        col_gain_one,
        col_shift_one,
        col_query,
        col_value,
        col_out,
        col_gain_two,
        col_shift_two,
        col_down,
    ) = [columns[:, i : i + 1] for i in range(8)]
    col_up = ordered(bias_up, other_up_bias, 0).astype(single)[:, None]

    grad_rows = cotangent[0].T
    other_grad_rows = swapped(grad_rows)
    width = grad_rows.shape[0]

    rows = tokens[0].T.astype(single)
    normal_one, scale_one = normalize(rows)
    normed_one = (normal_one * col_gain_one + col_shift_one).astype(bfloat)
    normed_one_mine, normed_one_theirs = halves(normed_one, at)
    project = dot(w_qkv, normed_one_mine, 0, 0) + dot(other_qkv, normed_one_theirs, 0, 0)
    col_qkv = jnp.concatenate([col_query, jnp.zeros_like(col_query), col_value], axis=0)
    qkv = (project + col_qkv).astype(bfloat)
    early_kv = lax.ppermute(qkv[width:, SKIP:], "shard", [(0, 1)])
    normed_one_arrived = swapped(normed_one_theirs)

    heads, lse = attend(flag, docs, early_docs, qkv, early_kv)
    heads_mine, heads_theirs = halves(heads, at)
    heads_arrived = swapped(heads_theirs)
    middle = rows + dot(full_out, heads, 0, 0) + col_out
    normal_two, scale_two = normalize(middle)
    normed_two = (normal_two * col_gain_two + col_shift_two).astype(bfloat)
    normed_two_mine, normed_two_theirs = halves(normed_two, at)
    normed_two_arrived = swapped(normed_two_theirs)
    pre_active = dot(full_up, normed_two, 0, 0) + col_up
    active, gelu_pull = jax.vjp(tanh_gelu, pre_active)
    active = active.astype(bfloat)
    active_mine, active_theirs = halves(active, at)
    active_arrived = swapped(active_theirs)
    output = (middle + dot(full_down, active, 1, 0) + col_down).astype(bfloat)

    all_grad_rows = both_tokens(grad_rows, other_grad_rows)
    all_active = both_tokens(active_mine, active_arrived)
    middle_row = width // 2
    grad_w_down = jnp.concatenate(
        [
            summed_product(all_grad_rows[:middle_row], all_active, order_one),
            summed_product(all_grad_rows[middle_row:], all_active, order_two),
        ],
        axis=0,
    ).T
    grad_bias_down = jnp.sum(grad_rows.astype(single), axis=1)
    grad_active = dot(full_down, grad_rows, 0, 0)
    grad_pre = gelu_pull(grad_active)[0].astype(bfloat)
    all_grad_pre = both_tokens(grad_pre, swapped(grad_pre))
    grad_bias_up = jnp.sum(grad_pre.astype(single), axis=1)
    all_normed_two = both_tokens(normed_two_mine, normed_two_arrived)
    ff = grad_pre.shape[0]
    grad_w_up = jnp.concatenate(
        [
            summed_product(all_normed_two, all_grad_pre[: ff // 2], order_one),
            summed_product(all_normed_two, all_grad_pre[ff // 2 :], order_two),
        ],
        axis=1,
    )
    grad_normed_two = dot(full_up, grad_pre, 1, 0)
    part_two, grad_gain_two, grad_shift_two = normalize_back(
        grad_normed_two, normal_two, scale_two, col_gain_two
    )
    grad_middle = grad_rows.astype(single) + part_two
    grad_branch = grad_middle.astype(bfloat)
    grad_bias_out = jnp.sum(grad_branch.astype(single), axis=1)
    grad_w_out = summed_product(
        both_tokens(heads_mine, heads_arrived),
        both_tokens(grad_branch, swapped(grad_branch)),
        order_one,
    )
    grad_heads = dot(full_out, grad_branch, 1, 0).astype(bfloat)
    grad_query, grad_key, grad_value, early_key, early_value = attend_back(
        flag, docs, early_docs, qkv, early_kv, grad_heads, heads, lse
    )
    back_key, back_value = lax.ppermute((early_key, early_value), "shard", [(1, 0)])

    def joined(own, back):
        return (own + jnp.pad(back.astype(single), ((0, 0), (SKIP, 0)))).astype(bfloat)

    grad_value = joined(grad_value, back_value)
    grad_project = jnp.concatenate(
        [grad_query, joined(grad_key, back_key), grad_value], axis=0
    )
    grad_bias_query = jnp.sum(grad_query.astype(single), axis=1)
    grad_bias_value = jnp.sum(grad_value.astype(single), axis=1)
    all_grad_project = both_tokens(grad_project, swapped(grad_project))
    all_normed_one = both_tokens(normed_one_mine, normed_one_arrived)
    cut = (all_grad_project.shape[0] // 256 + 1) * 128
    grad_w_qkv = jnp.concatenate(
        [
            summed_product(all_normed_one, all_grad_project[:cut], order_two),
            summed_product(all_normed_one, all_grad_project[cut:], order_one),
        ],
        axis=1,
    )
    grad_normed_one = ordered(
        dot(w_qkv, grad_project, 1, 0), dot(other_qkv, grad_project, 1, 0), 0
    )
    part_one, grad_gain_one, grad_shift_one = normalize_back(
        grad_normed_one, normal_one, scale_one, col_gain_one
    )
    input_grad = (grad_middle + part_one).astype(bfloat)

    small = jnp.stack(
        [
            grad_gain_one,
            grad_shift_one,
            grad_bias_query,
            grad_bias_value,
            grad_bias_out,
            grad_gain_two,
            grad_shift_two,
            grad_bias_down,
        ]
    )
    half = width // 2
    lanes = grad_bias_up.shape[0] // 2 // half
    up_parts = grad_bias_up.reshape(2, lanes, half)
    lower = jnp.concatenate([small[:, :half], up_parts[0]], axis=0)
    upper = jnp.concatenate([small[:, half:], up_parts[1]], axis=0)
    mine, theirs = jnp.where(first, lower, upper), jnp.where(first, upper, lower)
    mine = summed_small(mine + swapped(theirs))
    return (
        output.T[None],
        input_grad.T[None],
        grad_w_qkv,
        grad_w_out,
        grad_w_up,
        grad_w_down,
        mine[0],
        mine[1],
        mine[2],
        mine[3],
        mine[4],
        mine[5],
        mine[6],
        mine[8:].reshape(-1),
        mine[7],
    )


def solution(mesh):
    sequences = P("replica", "shard", None)
    matrix = P("shard", None)
    vector = P("shard")
    return jax.shard_map(
        shards,
        mesh=mesh,
        in_specs=(sequences, P("replica", "shard"), sequences) + (matrix,) * 4 + (vector,) * 9,
        out_specs=(sequences, sequences) + (matrix,) * 4 + (vector,) * 9,
        check_vma=False,
    )
```

time: 1670 us -> 587 us (0.35)
  waiting for transfers between devices: 839 us -> 208 us
  other arithmetic: 320 us -> 113 us
  local copies, waits for them, and re-layouts: 136 us -> 10.2 us
  blocking collectives: 121 us -> 0 us
  matrix products: 220 us -> 108 us
  starting transfers between devices: 10.2 us -> 82.7 us
  Pallas kernels: 0 us -> 42.7 us
    unnamed x14 -> x3, waiting for transfers between devices: 744 us -> 1.39 us
    all_gather x5 -> x0, other arithmetic: 256 us -> none  [the longest x1 86.2 us: shards(): lax.all_gather(owned_part[2], 'replica', axis=0, tiled=True)]
    ppermute x5 -> x76, waiting for transfers between devices: 0.01 us -> 206 us  [the longest x28 113 us: summed_product(): arrived = lax.ppermute(sent.astype(bfloat), 'replica', partners(count, bit))]
    dot_general x18 -> x24, matrix products: 220 us -> 108 us  [dot(): lax.dot_general(former, latter, (((former_axis,), (latter_axis,)), ((), (...]
    unnamed x3 -> x0, blocking collectives: 81.9 us -> none
    all_gather x8 -> x3, waiting for transfers between devices: 77.4 us -> 0.02 us  [the longest x1 0.02 us: shards(): full_out = lax.all_gather(w_out, 'shard', axis=0, tiled=True)]
    reshape x20 -> x2, local copies, waits for them, and re-layouts: 75.8 us -> 1.52 us  [the longest x1 1.38 us: shards(): mine[8:].reshape(-1)]
    ppermute x5 -> x76, starting transfers between devices: 9.64 us -> 82.6 us  [the longest x28 36.5 us: summed_product(): arrived = lax.ppermute(sent.astype(bfloat), 'replica', partners(count, bit))]
  transfers between devices with their start and end apart: 18 -> 79, of which waited for: 7 -> 34; matrix products, arithmetic and copies ran while one was open for 29% -> 31% of each run, Pallas kernels for 0% -> 4%
where the time goes in v1:
time: 587 us; the launch traced here: 580 us
  waiting for transfers between devices  208 us (35%)
  other arithmetic  113 us (19%)
  matrix products  108 us (18%)
  starting transfers between devices  82.7 us (14%)
  Pallas kernels  42.7 us (7%)
  between operations  15.8 us (3%)
  local copies, waits for them, and re-layouts  10.2 us (2%)
    ppermute x28, waiting for transfers between devices, summed_product(): arrived = lax.ppermute(sent.astype(bfloat), 'replica', partners(count, bit))  113 us
    dot_general x24, matrix products, dot(): lax.dot_general(former, latter, (((former_axis,), (latter_axis,)), ((), (...  108 us
    ppermute x28, waiting for transfers between devices, summed_product(): arrived = lax.ppermute(whole, 'replica', partners(count, bit))  88.3 us
    ppermute x28, starting transfers between devices, summed_product(): arrived = lax.ppermute(sent.astype(bfloat), 'replica', partners(count, bit))  36.5 us
    concatenate x4, other arithmetic, both_tokens(): return jnp.concatenate([mine, arrived], axis=1)  29.6 us
    ppermute x28, starting transfers between devices, summed_product(): arrived = lax.ppermute(whole, 'replica', partners(count, bit))  26.6 us
    pallas_call x1, Pallas kernels, attend_back(): pl.pallas_call(attend_back_kernel, grid=(heads,), in_specs=inputs + [bloc...  22.2 us
    concatenate x1, other arithmetic, shards(): jnp.concatenate([summed_product(all_normed_two, all_grad_pre[:ff // 2], o...  21.2 us
  transfers between devices with their start and end apart: 79, of which 34 were waited for; matrix products, arithmetic and copies ran while one was open for 31% of the time, Pallas kernels for 4%

profile of v1, /device:TPU:0, one launch (start us, length us, event | category | flops | bytes accessed | tf_op | source)
XLA Modules:
  0.0 580.5 jit_solution(11838533726505556056)
XLA Ops:
  11.5 3.7 collective-permute-done.1
  20.6 5.4 fusion.10.q_ref.k_ref.v_ref
  41.3 20.5 %attend.1 = (bf16[1088,512]{1,0:T(8,128)(2,1)S(1)}, f32[17,1,512]{2,1,0:T(1,128)S(1)}) custom-call(s32[1]{0:T(128)} %bitcast.1.flag_ref, s32[1,512]{1,0:T(1,128)S(1)} %copy-done.10, s32[512,1]{1,0:T(8,128)S(1)} %copy.31.doc_col_ref, s32[512,1]{1,0:T(8,128)S(1)} %copy.32.early_col_ref, bf16[3264,512]{1,0:T(8,128)(2,1)S(1)} %copy-done.4, ...), custom_call_target="tpu_custom_call" | custom-call | flops 12000000000 | bytes 6000000 | tf_op jit(solution)/shard_map/attend/pallas_call | solution.py:169
  61.9 4.6 fusion.127
  68.2 15.4 %fusion.9 = (bf16[4352,512]{0,1:T(8,128)(2,1)}, f32[512,4352]{1,0:T(8,128)}) fusion(f32[4352]{0:T(1024)S(1)} %maximum_convert_fusion.3, bf16[1088,512]{1,0:T(8,128)(2,1)} %fusion.46, bf16[1088,4352]{1,0:T(8,128)(2,1)} %all-gather.6.cloned.1.call-done), kind=kOutput, calls=%fused_computation.16 | convolution fusion | flops 4870897664 | bytes 23970816 | tf_op jit(solution)/shard_map/dot_general | solution.py:17
  83.6 16.6 %convert_reduce_fusion = (f32[4352]{0:T(1024)S(1)}, bf16[4352,512]{0,1:T(8,128)(2,1)S(1)}) fusion(f32[512,4352]{1,0:T(8,128)} %get-tuple-element.117, f32[4352]{0:T(1024)S(1)} %maximum_convert_fusion.3, bf16[1088,4352]{1,0:T(8,128)(2,1)} %all-gather.8.cloned.1.call-done, bf16[1,512,1088]{1,2,0:T(8,128)(2,1)S(1)} %copy-done.25), kind=kOutput, calls=%fused_computation.17 | convolution fusion | flops 4899860480 | bytes 23988224 | tf_op jit(solution)/shard_map/dot_general | solution.py:17
  100.2 5.7 fusion.44
  112.1 22.2 %attend_back.1 = (bf16[1088,512]{1,0:T(8,128)(2,1)S(1)}, f32[1088,512]{1,0:T(8,128)S(1)}, f32[1088,512]{1,0:T(8,128)S(1)}, bf16[1088,384]{1,0:T(8,128)(2,1)}, bf16[1088,384]{1,0:T(8,128)(2,1)}) custom-call(s32[1]{0:T(128)} %bitcast.1.flag_ref, s32[1,512]{1,0:T(1,128)S(1)} %copy-done.10, s32[512,1]{1,0:T(8,128)S(1)} %copy-done.7, s32[512,1]{1,0:T(8,128)S(1)} %copy-done.9, ...), custom_call_target="tpu_custom_call" | custom-call | flops 30000001024 | bytes 12000000 | tf_op jit(solution)/shard_map/attend_back/pallas_call | solution.py:202
  150.1 4.5 fusion.122
  157.8 3.7 convolution_convert_fusion.5
  166.9 12.3 %collective-permute-done.27 = bf16[272,1088]{1,0:T(8,128)(2,1)} collective-permute-done((bf16[272,1088]{1,0:T(8,128)(2,1)}, bf16[272,1088]{1,0:T(8,128)(2,1)}, u32[]{:S(2)}, u32[]{:S(2)}) %collective-permute-start.27) | collective-permute-done | bytes 591904 | tf_op jit(solution)/shard_map/ppermute | solution.py:280
  179.2 3.2 convolution_add_fusion.6
  184.4 7.3 %collective-permute-done.28 = bf16[136,1088]{1,0:T(8,128)(2,1)S(1)} collective-permute-done((bf16[136,1088]{1,0:T(8,128)(2,1)S(1)}, bf16[136,1088]{1,0:T(8,128)(2,1)S(1)}, u32[]{:S(2)}, u32[]{:S(2)}) %collective-permute-start.28) | collective-permute-done | bytes 295968 | tf_op jit(solution)/shard_map/ppermute | solution.py:280
  205.7 4.9 broadcast_select_fusion.1
  213.2 6.5 %fusion.23 = bf16[1,512,1088]{1,2,0:T(8,128)(2,1)} fusion(f32[512,1088]{0,1:T(8,128)S(1)} %copy-done.14, bf16[4352,512]{0,1:T(8,128)(2,1)S(1)} %bitcast.191, bf16[1088,4352]{1,0:T(8,128)(2,1)S(1)} %bitcast.194, f32[1088]{0:T(1024)S(1)} %get-tuple-element.107), kind=kOutput, calls=%fused_computation.60 | convolution fusion | flops 4850286592 | bytes 17273088 | tf_op jit(solution)/shard_map/dot_general | solution.py:17
  227.4 3.4 collective-permute-done.33
  233.6 4.0 convolution_convert_fusion
  239.0 3.3 convolution_convert_fusion.1
  242.9 6.3 %collective-permute-done.34 = bf16[272,1088]{1,0:T(8,128)(2,1)S(1)} collective-permute-done((bf16[272,1088]{1,0:T(8,128)(2,1)S(1)}, bf16[272,1088]{1,0:T(8,128)(2,1)S(1)}, u32[]{:S(2)}, u32[]{:S(2)}) %collective-permute-start.34) | collective-permute-done | bytes 591904 | tf_op jit(solution)/shard_map/ppermute | solution.py:286
  251.0 13.2 %collective-permute-done.63 = bf16[272,2176]{1,0:T(8,128)(2,1)S(1)} collective-permute-done((bf16[272,2176]{1,0:T(8,128)(2,1)S(1)}, bf16[272,2176]{1,0:T(8,128)(2,1)S(1)}, u32[]{:S(2)}, u32[]{:S(2)}) %collective-permute-start.63) | collective-permute-done | bytes 1183776 | tf_op jit(solution)/shard_map/ppermute | solution.py:280
  264.2 3.2 convolution_add_fusion
  268.1 6.4 %collective-permute-done.55 = bf16[272,2176]{1,0:T(8,128)(2,1)S(1)} collective-permute-done((bf16[272,2176]{1,0:T(8,128)(2,1)S(1)}, bf16[272,2176]{1,0:T(8,128)(2,1)S(1)}, u32[]{:S(2)}, u32[]{:S(2)}) %collective-permute-start.55) | collective-permute-done | bytes 1183776 | tf_op jit(solution)/shard_map/ppermute | solution.py:280
  274.5 3.3 convolution_add_fusion.1
  279.3 5.7 collective-permute-done.64
  295.3 22.8 %pad_maximum_fusion = bf16[3264,1024]{1,0:T(8,128)(2,1)S(1)} fusion(bf16[3264,512]{1,0:T(8,128)(2,1)} %collective-permute-done.8, bf16[1088,512]{1,0:T(8,128)(2,1)S(1)} %copy-done.20, bf16[1088,512]{1,0:T(8,128)(2,1)S(1)} %copy-done.23, bf16[1088,512]{1,0:T(8,128)(2,1)S(1)} %get-tuple-element.24), kind=kLoop, calls=%fused_computation.18 | loop fusion | flops 26738688 | bytes 13369344 | tf_op jit(solution)/shard_map/concatenate | solution.py:252
  334.3 7.9 %collective-permute-done.67 = bf16[40,2176]{1,0:T(8,128)(2,1)S(1)} collective-permute-done((bf16[40,2176]{1,0:T(8,128)(2,1)S(1)}, bf16[40,2176]{1,0:T(8,128)(2,1)S(1)}, u32[]{:S(2)}, u32[]{:S(2)}) %collective-permute-start.67) | collective-permute-done | bytes 174112 | tf_op jit(solution)/shard_map/ppermute | solution.py:286
  342.4 9.0 %collective-permute-done.59 = bf16[40,2176]{1,0:T(8,128)(2,1)S(1)} collective-permute-done((bf16[40,2176]{1,0:T(8,128)(2,1)S(1)}, bf16[40,2176]{1,0:T(8,128)(2,1)S(1)}, u32[]{:S(2)}, u32[]{:S(2)}) %collective-permute-start.59) | collective-permute-done | bytes 174112 | tf_op jit(solution)/shard_map/ppermute | solution.py:286
  351.4 9.2 %collective-permute-done.68 = bf16[72,2176]{1,0:T(8,128)(2,1)S(1)} collective-permute-done((bf16[72,2176]{1,0:T(8,128)(2,1)S(1)}, bf16[72,2176]{1,0:T(8,128)(2,1)S(1)}, u32[]{:S(2)}, u32[]{:S(2)}) %collective-permute-start.68) | collective-permute-done | bytes 313376 | tf_op jit(solution)/shard_map/ppermute | solution.py:286
  361.2 8.0 %collective-permute-done.60 = bf16[72,2176]{1,0:T(8,128)(2,1)S(1)} collective-permute-done((bf16[72,2176]{1,0:T(8,128)(2,1)S(1)}, bf16[72,2176]{1,0:T(8,128)(2,1)S(1)}, u32[]{:S(2)}, u32[]{:S(2)}) %collective-permute-start.60) | collective-permute-done | bytes 313376 | tf_op jit(solution)/shard_map/ppermute | solution.py:286
  375.7 17.0 %collective-permute-done.18 = bf16[136,1600]{1,0:T(8,128)(2,1)S(1)} collective-permute-done((bf16[136,1600]{1,0:T(8,128)(2,1)S(1)}, bf16[136,1600]{1,0:T(8,128)(2,1)S(1)}, u32[]{:S(2)}, u32[]{:S(2)}) %collective-permute-start.18) | collective-permute-done | bytes 435232 | tf_op jit(solution)/shard_map/ppermute | solution.py:280
  394.6 7.7 %collective-permute-done.10 = bf16[136,1664]{1,0:T(8,128)(2,1)S(1)} collective-permute-done((bf16[136,1664]{1,0:T(8,128)(2,1)S(1)}, bf16[136,1664]{1,0:T(8,128)(2,1)S(1)}, u32[]{:S(2)}, u32[]{:S(2)}) %collective-permute-start.10) | collective-permute-done | bytes 452640 | tf_op jit(solution)/shard_map/ppermute | solution.py:280
  406.8 3.1 convolution_add_fusion.2
  410.7 3.6 convolution_add_fusion.3
  416.9 9.6 %collective-permute-done.20 = bf16[40,1600]{1,0:T(8,128)(2,1)S(1)} collective-permute-done((bf16[40,1600]{1,0:T(8,128)(2,1)S(1)}, bf16[40,1600]{1,0:T(8,128)(2,1)S(1)}, u32[]{:S(2)}, u32[]{:S(2)}) %collective-permute-start.20) | collective-permute-done | bytes 128032 | tf_op jit(solution)/shard_map/ppermute | solution.py:280
  426.6 7.4 %collective-permute-done.12 = bf16[40,1664]{1,0:T(8,128)(2,1)S(1)} collective-permute-done((bf16[40,1664]{1,0:T(8,128)(2,1)S(1)}, bf16[40,1664]{1,0:T(8,128)(2,1)S(1)}, u32[]{:S(2)}, u32[]{:S(2)}) %collective-permute-start.12) | collective-permute-done | bytes 133152 | tf_op jit(solution)/shard_map/ppermute | solution.py:280
  434.0 8.8 %collective-permute-done.21 = bf16[40,1600]{1,0:T(8,128)(2,1)S(1)} collective-permute-done((bf16[40,1600]{1,0:T(8,128)(2,1)S(1)}, bf16[40,1600]{1,0:T(8,128)(2,1)S(1)}, u32[]{:S(2)}, u32[]{:S(2)}) %collective-permute-start.21) | collective-permute-done | bytes 128032 | tf_op jit(solution)/shard_map/ppermute | solution.py:286
  442.9 6.5 %collective-permute-done.13 = bf16[40,1664]{1,0:T(8,128)(2,1)S(1)} collective-permute-done((bf16[40,1664]{1,0:T(8,128)(2,1)S(1)}, bf16[40,1664]{1,0:T(8,128)(2,1)S(1)}, u32[]{:S(2)}, u32[]{:S(2)}) %collective-permute-start.13) | collective-permute-done | bytes 133152 | tf_op jit(solution)/shard_map/ppermute | solution.py:286
  449.6 8.7 %collective-permute-done.22 = bf16[72,1600]{1,0:T(8,128)(2,1)S(1)} collective-permute-done((bf16[72,1600]{1,0:T(8,128)(2,1)S(1)}, bf16[72,1600]{1,0:T(8,128)(2,1)S(1)}, u32[]{:S(2)}, u32[]{:S(2)}) %collective-permute-start.22) | collective-permute-done | bytes 230432 | tf_op jit(solution)/shard_map/ppermute | solution.py:286
  461.1 4.8 collective-permute-done.14
  466.8 4.2 collective-permute-done.47
  473.0 3.3 collective-permute-done.39
  479.7 11.7 %collective-permute-done.48 = bf16[40,2176]{1,0:T(8,128)(2,1)S(1)} collective-permute-done((bf16[40,2176]{1,0:T(8,128)(2,1)S(1)}, bf16[40,2176]{1,0:T(8,128)(2,1)S(1)}, u32[]{:S(2)}, u32[]{:S(2)}) %collective-permute-start.48) | collective-permute-done | bytes 174112 | tf_op jit(solution)/shard_map/ppermute | solution.py:280
  497.7 8.5 %convert_bitcast_fusion = f32[2176,1088]{0,1:T(8,128)} fusion(bf16[272,2176]{1,0:T(8,128)(2,1)S(1)} %get-tuple-element.59, bf16[272,2176]{1,0:T(8,128)(2,1)S(1)} %get-tuple-element.58, bf16[272,2176]{1,0:T(8,128)(2,1)S(1)} %get-tuple-element.57, bf16[272,2176]{1,0:T(8,128)(2,1)S(1)} %get-tuple-element.56), kind=kLoop, calls=%fused_computation.2 | loop fusion | flops 18939904 | bytes 14204928 | tf_op jit(solution)/shard_map/transpose | solution.py:427
  508.5 4.7 collective-permute-done.50
  519.5 7.9 %collective-permute-done.51 = bf16[136,2176]{1,0:T(8,128)(2,1)S(1)} collective-permute-done((bf16[136,2176]{1,0:T(8,128)(2,1)S(1)}, bf16[136,2176]{1,0:T(8,128)(2,1)S(1)}, u32[]{:S(2)}, u32[]{:S(2)}) %collective-permute-start.51) | collective-permute-done | bytes 591904 | tf_op jit(solution)/shard_map/ppermute | solution.py:286
  527.7 4.0 collective-permute-start.52
  535.3 16.5 %maximum_convert_fusion.1 = f32[544,3264]{1,0:T(8,128)} fusion(bf16[272,1600]{1,0:T(8,128)(2,1)S(1)} %get-tuple-element.69, bf16[272,1600]{1,0:T(8,128)(2,1)S(1)} %get-tuple-element.68, bf16[272,1664]{1,0:T(8,128)(2,1)S(1)} %get-tuple-element.67, bf16[272,1664]{1,0:T(8,128)(2,1)S(1)} %get-tuple-element.66), kind=kLoop, calls=%fused_computation.33 | loop fusion | flops 14204928 | bytes 10653696 | tf_op jit(solution)/shard_map/concatenate | solution.py:472
  552.6 21.2 %maximum_convert_fusion = f32[544,4352]{1,0:T(8,128)} fusion(bf16[272,2176]{1,0:T(8,128)(2,1)S(1)} %get-tuple-element.63, bf16[272,2176]{1,0:T(8,128)(2,1)S(1)} %get-tuple-element.62, bf16[272,2176]{1,0:T(8,128)(2,1)S(1)} %get-tuple-element.61, bf16[272,2176]{1,0:T(8,128)(2,1)S(1)} %get-tuple-element.60), kind=kLoop, calls=%fused_computation.21 | loop fusion | flops 18939904 | bytes 14204928 | tf_op jit(solution)/shard_map/concatenate | solution.py:435
  (441 shorter events, 163.1 us)
Async XLA Ops:
  7.2 54.7 %all-gather.4.cloned.1.call-start = ((), (), s32[]{:S(2)}) async-start(), calls=%async_computation | async-start | bytes 3760128 | tf_op jit(solution)/shard_map/all_gather | solution.py:367
  8.0 60.2 %all-gather.6.cloned.1.call-start = ((), (), s32[]{:S(2)}) async-start(), calls=%async_computation.1 | async-start | bytes 14204928 | tf_op jit(solution)/shard_map/all_gather | solution.py:368
  8.7 74.8 %all-gather.8.cloned.1.call-start = ((), (), s32[]{:S(2)}) async-start(), calls=%async_computation.2 | async-start | bytes 14204928 | tf_op jit(solution)/shard_map/all_gather | solution.py:369
  8.8 11.8 %collective-permute-start.2 = (bf16[544,3264]{1,0:T(8,128)(2,1)}, bf16[544,3264]{1,0:T(8,128)(2,1)}, u32[]{:S(2)}, u32[]{:S(2)}) collective-permute-start(bf16[544,3264]{1,0:T(8,128)(2,1)} %param.19), channel_id=1, source_target_pairs={{0,16},{16,0},{1,17},{17,1},{2,18},{18,2},{3,19},{19,3},{4,20},{20... | collective-permute-start | bytes 10653704 | tf_op jit(solution)/shard_map/ppermute | solution.py:241
  29.1 12.1 %collective-permute-start.3 = (bf16[2176,384]{1,0:T(8,128)(2,1)}, bf16[2176,384]{1,0:T(8,128)(2,1)S(1)}, u32[]{:S(2)}, u32[]{:S(2)}) collective-permute-start(bf16[2176,384]{1,0:T(8,128)(2,1)} %slice.434), channel_id=1, source_target_pairs={{0,16},{1,17},{2,18},{3,19},{4,20},{5,21},{6,22},{7,23},{8,24},{9,... | collective-permute-start | bytes 5013512 | tf_op jit(solution)/shard_map/ppermute | solution.py:400
  134.3 11.7 %collective-permute-start.6 = (bf16[1088,384]{1,0:T(8,128)(2,1)}, bf16[1088,384]{1,0:T(8,128)(2,1)}, u32[]{:S(2)}, u32[]{:S(2)}) collective-permute-start(bf16[1088,384]{1,0:T(8,128)(2,1)} %get-tuple-element.28), channel_id=1, source_target_pairs={{16,0},{17,1},{18,2},{19,3},{20,4},{21,5},{22,6},{23,7},{24,8},{25... | collective-permute-start | bytes 2506760 | tf_op jit(solution)/shard_map/ppermute | solution.py:458
  137.0 20.8 %collective-permute-start.25 = (bf16[544,512]{1,0:T(8,128)(2,1)}, bf16[544,512]{1,0:T(8,128)(2,1)}, u32[]{:S(2)}, u32[]{:S(2)}) collective-permute-start(bf16[544,512]{1,0:T(8,128)(2,1)} %get-tuple-element.87), channel_id=1, source_target_pairs={{0,16},{16,0},{1,17},{17,1},{2,18},{18,2},{3,19},{19,3},{4,20},{20... | collective-permute-start | bytes 1671176 | tf_op jit(solution)/shard_map/ppermute | solution.py:241
  141.6 58.4 %collective-permute-start.35 = (bf16[544,512]{1,0:T(8,128)(2,1)}, bf16[544,512]{1,0:T(8,128)(2,1)}, u32[]{:S(2)}, u32[]{:S(2)}) collective-permute-start(bf16[544,512]{1,0:T(8,128)(2,1)} %get-tuple-element.85), channel_id=1, source_target_pairs={{0,16},{16,0},{1,17},{17,1},{2,18},{18,2},{3,19},{19,3},{4,20},{20... | collective-permute-start | bytes 1671176 | tf_op jit(solution)/shard_map/ppermute | solution.py:241
  143.6 14.1 %collective-permute-start.26 = (bf16[1088,512]{1,0:T(8,128)(2,1)}, bf16[1088,512]{1,0:T(8,128)(2,1)}, u32[]{:S(2)}, u32[]{:S(2)}) collective-permute-start(bf16[1088,512]{1,0:T(8,128)(2,1)} %get-tuple-element.51), channel_id=1, source_target_pairs={{0,16},{16,0},{1,17},{17,1},{2,18},{18,2},{3,19},{19,3},{4,20},{20... | collective-permute-start | bytes 3342344 | tf_op jit(solution)/shard_map/ppermute | solution.py:241
  161.5 17.6 %collective-permute-start.27 = (bf16[272,1088]{1,0:T(8,128)(2,1)}, bf16[272,1088]{1,0:T(8,128)(2,1)}, u32[]{:S(2)}, u32[]{:S(2)}) collective-permute-start(bf16[272,1088]{1,0:T(8,128)(2,1)} %convolution_convert_fusion.5), channel_id=1, source_target_pairs={{0,1},{1,0},{2,3},{3,2},{4,5},{5,4},{6,7},{7,6},{8,9},{9,8},{10,11... | collective-permute-start | bytes 1775624 | tf_op jit(solution)/shard_map/ppermute | solution.py:280
  202.3 122.3 %collective-permute-start.36 = (bf16[4352,512]{0,1:T(8,128)(2,1)}, bf16[4352,512]{0,1:T(8,128)(2,1)}, u32[]{:S(2)}, u32[]{:S(2)}) collective-permute-start(bf16[4352,512]{0,1:T(8,128)(2,1)} %copy-done.29), channel_id=1, source_target_pairs={{0,16},{16,0},{1,17},{17,1},{2,18},{18,2},{3,19},{19,3},{4,20},{20... | collective-permute-start | bytes 13369352 | tf_op jit(solution)/shard_map/ppermute | solution.py:241
  210.6 23.0 %collective-permute-start.54 = (bf16[2176,512]{0,1:T(8,128)(2,1)}, bf16[2176,512]{0,1:T(8,128)(2,1)}, u32[]{:S(2)}, u32[]{:S(2)}) collective-permute-start(bf16[2176,512]{0,1:T(8,128)(2,1)} %get-tuple-element.55), channel_id=1, source_target_pairs={{0,16},{16,0},{1,17},{17,1},{2,18},{18,2},{3,19},{19,3},{4,20},{20... | collective-permute-start | bytes 6684680 | tf_op jit(solution)/shard_map/ppermute | solution.py:241
  224.6 66.4 %collective-permute-start.8 = (bf16[3264,512]{1,0:T(8,128)(2,1)}, bf16[3264,512]{1,0:T(8,128)(2,1)}, u32[]{:S(2)}, u32[]{:S(2)}) collective-permute-start(bf16[3264,512]{1,0:T(8,128)(2,1)} %pad_maximum_fusion.3), channel_id=1, source_target_pairs={{0,16},{16,0},{1,17},{17,1},{2,18},{18,2},{3,19},{19,3},{4,20},{20... | collective-permute-start | bytes 10027016 | tf_op jit(solution)/shard_map/ppermute | solution.py:241
  232.0 17.1 %collective-permute-start.34 = (bf16[272,1088]{1,0:T(8,128)(2,1)S(1)}, bf16[272,1088]{1,0:T(8,128)(2,1)S(1)}, u32[]{:S(2)}, u32[]{:S(2)}) collective-permute-start(bf16[272,1088]{1,0:T(8,128)(2,1)S(1)} %pad_maximum_fusion.17), channel_id=1, source_target_pairs={{0,1},{1,0},{2,3},{3,2},{4,5},{5,4},{6,7},{7,6},{8,9},{9,8},{10,11... | collective-permute-start | bytes 1775624 | tf_op jit(solution)/shard_map/ppermute | solution.py:286
  237.6 26.5 %collective-permute-start.63 = (bf16[272,2176]{1,0:T(8,128)(2,1)S(1)}, bf16[272,2176]{1,0:T(8,128)(2,1)S(1)}, u32[]{:S(2)}, u32[]{:S(2)}) collective-permute-start(bf16[272,2176]{1,0:T(8,128)(2,1)S(1)} %convolution_convert_fusion), channel_id=1, source_target_pairs={{0,2},{1,3},{2,0},{3,1},{4,6},{5,7},{6,4},{7,5},{8,10},{9,11},{10,... | collective-permute-start | bytes 3551240 | tf_op jit(solution)/shard_map/ppermute | solution.py:280
  242.3 32.2 %collective-permute-start.55 = (bf16[272,2176]{1,0:T(8,128)(2,1)S(1)}, bf16[272,2176]{1,0:T(8,128)(2,1)S(1)}, u32[]{:S(2)}, u32[]{:S(2)}) collective-permute-start(bf16[272,2176]{1,0:T(8,128)(2,1)S(1)} %convolution_convert_fusion.1), channel_id=1, source_target_pairs={{0,1},{1,0},{2,3},{3,2},{4,5},{5,4},{6,7},{7,6},{8,9},{9,8},{10,11... | collective-permute-start | bytes 3551240 | tf_op jit(solution)/shard_map/ppermute | solution.py:280
  267.5 17.4 %collective-permute-start.64 = (bf16[136,2176]{1,0:T(8,128)(2,1)S(1)}, bf16[136,2176]{1,0:T(8,128)(2,1)S(1)}, u32[]{:S(2)}, u32[]{:S(2)}) collective-permute-start(bf16[136,2176]{1,0:T(8,128)(2,1)S(1)} %select_convert_fusion), channel_id=1, source_target_pairs={{0,1},{1,0},{2,3},{3,2},{4,5},{5,4},{6,7},{7,6},{8,9},{9,8},{10,11... | collective-permute-start | bytes 1775624 | tf_op jit(solution)/shard_map/ppermute | solution.py:280
  277.9 10.9 %collective-permute-start.56 = (bf16[136,2176]{1,0:T(8,128)(2,1)S(1)}, bf16[136,2176]{1,0:T(8,128)(2,1)S(1)}, u32[]{:S(2)}, u32[]{:S(2)}) collective-permute-start(bf16[136,2176]{1,0:T(8,128)(2,1)S(1)} %select_convert_fusion.1), channel_id=1, source_target_pairs={{0,2},{1,3},{2,0},{3,1},{4,6},{5,7},{6,4},{7,5},{8,10},{9,11},{10,... | collective-permute-start | bytes 1775624 | tf_op jit(solution)/shard_map/ppermute | solution.py:280
  285.2 36.0 %collective-permute-start.65 = (bf16[72,2176]{1,0:T(8,128)(2,1)S(1)}, bf16[72,2176]{1,0:T(8,128)(2,1)S(1)}, u32[]{:S(2)}, u32[]{:S(2)}) collective-permute-start(bf16[72,2176]{1,0:T(8,128)(2,1)S(1)} %select_convert_fusion.6), channel_id=1, source_target_pairs={{0,4},{1,5},{2,6},{3,7},{4,0},{5,1},{6,2},{7,3},{8,12},{9,13},{10,... | collective-permute-start | bytes 940040 | tf_op jit(solution)/shard_map/ppermute | solution.py:280
  289.1 34.3 %collective-permute-start.57 = (bf16[72,2176]{1,0:T(8,128)(2,1)S(1)}, bf16[72,2176]{1,0:T(8,128)(2,1)S(1)}, u32[]{:S(2)}, u32[]{:S(2)}) collective-permute-start(bf16[72,2176]{1,0:T(8,128)(2,1)S(1)} %select_convert_fusion.7), channel_id=1, source_target_pairs={{0,4},{1,5},{2,6},{3,7},{4,0},{5,1},{6,2},{7,3},{8,12},{9,13},{10,... | collective-permute-start | bytes 940040 | tf_op jit(solution)/shard_map/ppermute | solution.py:280
  293.8 75.6 %collective-permute-start.17 = (bf16[272,1600]{1,0:T(8,128)(2,1)S(1)}, bf16[272,1600]{1,0:T(8,128)(2,1)S(1)}, u32[]{:S(2)}, u32[]{:S(2)}) collective-permute-start(bf16[272,1600]{1,0:T(8,128)(2,1)S(1)} %convolution_convert_fusion.6), channel_id=1, source_target_pairs={{0,1},{1,0},{2,3},{3,2},{4,5},{5,4},{6,7},{7,6},{8,9},{9,8},{10,11... | collective-permute-start | bytes 2611208 | tf_op jit(solution)/shard_map/ppermute | solution.py:280
  319.4 54.3 %collective-permute-start.9 = (bf16[272,1664]{1,0:T(8,128)(2,1)S(1)}, bf16[272,1664]{1,0:T(8,128)(2,1)S(1)}, u32[]{:S(2)}, u32[]{:S(2)}) collective-permute-start(bf16[272,1664]{1,0:T(8,128)(2,1)S(1)} %fusion.27), channel_id=1, source_target_pairs={{0,2},{1,3},{2,0},{3,1},{4,6},{5,7},{6,4},{7,5},{8,10},{9,11},{10,... | collective-permute-start | bytes 2715656 | tf_op jit(solution)/shard_map/ppermute | solution.py:280
  321.4 11.1 %collective-permute-start.66 = (bf16[40,2176]{1,0:T(8,128)(2,1)S(1)}, bf16[40,2176]{1,0:T(8,128)(2,1)S(1)}, u32[]{:S(2)}, u32[]{:S(2)}) collective-permute-start(bf16[40,2176]{1,0:T(8,128)(2,1)S(1)} %select_convert_fusion.13), channel_id=1, source_target_pairs={{0,8},{1,9},{2,10},{3,11},{4,12},{5,13},{6,14},{7,15},{8,0},{9,1},... | collective-permute-start | bytes 522248 | tf_op jit(solution)/shard_map/ppermute | solution.py:280
  323.6 10.7 %collective-permute-start.58 = (bf16[40,2176]{1,0:T(8,128)(2,1)S(1)}, bf16[40,2176]{1,0:T(8,128)(2,1)S(1)}, u32[]{:S(2)}, u32[]{:S(2)}) collective-permute-start(bf16[40,2176]{1,0:T(8,128)(2,1)S(1)} %select_convert_fusion.14), channel_id=1, source_target_pairs={{0,8},{1,9},{2,10},{3,11},{4,12},{5,13},{6,14},{7,15},{8,0},{9,1},... | collective-permute-start | bytes 522248 | tf_op jit(solution)/shard_map/ppermute | solution.py:280
  327.7 77.6 %collective-permute-start.45 = (bf16[272,2176]{1,0:T(8,128)(2,1)S(1)}, bf16[272,2176]{1,0:T(8,128)(2,1)S(1)}, u32[]{:S(2)}, u32[]{:S(2)}) collective-permute-start(bf16[272,2176]{1,0:T(8,128)(2,1)S(1)} %convolution_convert_fusion.2), channel_id=1, source_target_pairs={{0,2},{1,3},{2,0},{3,1},{4,6},{5,7},{6,4},{7,5},{8,10},{9,11},{10,... | collective-permute-start | bytes 3551240 | tf_op jit(solution)/shard_map/ppermute | solution.py:280
  332.4 77.7 %collective-permute-start.37 = (bf16[272,2176]{1,0:T(8,128)(2,1)S(1)}, bf16[272,2176]{1,0:T(8,128)(2,1)S(1)}, u32[]{:S(2)}, u32[]{:S(2)}) collective-permute-start(bf16[272,2176]{1,0:T(8,128)(2,1)S(1)} %convolution_convert_fusion.3), channel_id=1, source_target_pairs={{0,1},{1,0},{2,3},{3,2},{4,5},{5,4},{6,7},{7,6},{8,9},{9,8},{10,11... | collective-permute-start | bytes 3551240 | tf_op jit(solution)/shard_map/ppermute | solution.py:280
  369.2 34.6 %collective-permute-start.69 = (bf16[136,2176]{1,0:T(8,128)(2,1)S(1)}, bf16[136,2176]{1,0:T(8,128)(2,1)S(1)}, u32[]{:S(2)}, u32[]{:S(2)}) collective-permute-start(bf16[136,2176]{1,0:T(8,128)(2,1)S(1)} %pad_maximum_fusion.21), channel_id=1, source_target_pairs={{0,1},{1,0},{2,3},{3,2},{4,5},{5,4},{6,7},{7,6},{8,9},{9,8},{10,11... | collective-permute-start | bytes 1775624 | tf_op jit(solution)/shard_map/ppermute | solution.py:286
  369.4 35.5 %collective-permute-start.61 = (bf16[136,2176]{1,0:T(8,128)(2,1)S(1)}, bf16[136,2176]{1,0:T(8,128)(2,1)S(1)}, u32[]{:S(2)}, u32[]{:S(2)}) collective-permute-start(bf16[136,2176]{1,0:T(8,128)(2,1)S(1)} %pad_maximum_fusion.20), channel_id=1, source_target_pairs={{0,2},{1,3},{2,0},{3,1},{4,6},{5,7},{6,4},{7,5},{8,10},{9,11},{10,... | collective-permute-start | bytes 1775624 | tf_op jit(solution)/shard_map/ppermute | solution.py:286
  373.7 19.0 %collective-permute-start.18 = (bf16[136,1600]{1,0:T(8,128)(2,1)S(1)}, bf16[136,1600]{1,0:T(8,128)(2,1)S(1)}, u32[]{:S(2)}, u32[]{:S(2)}) collective-permute-start(bf16[136,1600]{1,0:T(8,128)(2,1)S(1)} %select_convert_fusion.4), channel_id=1, source_target_pairs={{0,2},{1,3},{2,0},{3,1},{4,6},{5,7},{6,4},{7,5},{8,10},{9,11},{10,... | collective-permute-start | bytes 1305608 | tf_op jit(solution)/shard_map/ppermute | solution.py:280
  402.3 12.2 %collective-permute-start.19 = (bf16[72,1600]{1,0:T(8,128)(2,1)S(1)}, bf16[72,1600]{1,0:T(8,128)(2,1)S(1)}, u32[]{:S(2)}, u32[]{:S(2)}) collective-permute-start(bf16[72,1600]{1,0:T(8,128)(2,1)S(1)} %select_convert_fusion.11), channel_id=1, source_target_pairs={{0,4},{1,5},{2,6},{3,7},{4,0},{5,1},{6,2},{7,3},{8,12},{9,13},{10,... | collective-permute-start | bytes 691208 | tf_op jit(solution)/shard_map/ppermute | solution.py:280
  403.8 12.9 %collective-permute-start.11 = (bf16[72,1664]{1,0:T(8,128)(2,1)S(1)}, bf16[72,1664]{1,0:T(8,128)(2,1)S(1)}, u32[]{:S(2)}, u32[]{:S(2)}) collective-permute-start(bf16[72,1664]{1,0:T(8,128)(2,1)S(1)} %select_convert_fusion.12), channel_id=1, source_target_pairs={{0,4},{1,5},{2,6},{3,7},{4,0},{5,1},{6,2},{7,3},{8,12},{9,13},{10,... | collective-permute-start | bytes 718856 | tf_op jit(solution)/shard_map/ppermute | solution.py:280
  404.9 91.7 %collective-permute-start.70 = (bf16[272,2176]{1,0:T(8,128)(2,1)S(1)}, bf16[272,2176]{1,0:T(8,128)(2,1)S(1)}, u32[]{:S(2)}, u32[]{:S(2)}) collective-permute-start(bf16[272,2176]{1,0:T(8,128)(2,1)S(1)} %pad_maximum_fusion.12), channel_id=1, source_target_pairs={{0,2},{1,3},{2,0},{3,1},{4,6},{5,7},{6,4},{7,5},{8,10},{9,11},{10,... | collective-permute-start | bytes 3551240 | tf_op jit(solution)/shard_map/ppermute | solution.py:286
  405.3 91.9 %collective-permute-start.62 = (bf16[272,2176]{1,0:T(8,128)(2,1)S(1)}, bf16[272,2176]{1,0:T(8,128)(2,1)S(1)}, u32[]{:S(2)}, u32[]{:S(2)}) collective-permute-start(bf16[272,2176]{1,0:T(8,128)(2,1)S(1)} %pad_maximum_fusion.11), channel_id=1, source_target_pairs={{0,1},{1,0},{2,3},{3,2},{4,5},{5,4},{6,7},{7,6},{8,9},{9,8},{10,11... | collective-permute-start | bytes 3551240 | tf_op jit(solution)/shard_map/ppermute | solution.py:286
  410.1 48.3 %collective-permute-start.46 = (bf16[136,2176]{1,0:T(8,128)(2,1)S(1)}, bf16[136,2176]{1,0:T(8,128)(2,1)S(1)}, u32[]{:S(2)}, u32[]{:S(2)}) collective-permute-start(bf16[136,2176]{1,0:T(8,128)(2,1)S(1)} %select_convert_fusion.2), channel_id=1, source_target_pairs={{0,1},{1,0},{2,3},{3,2},{4,5},{5,4},{6,7},{7,6},{8,9},{9,8},{10,11... | collective-permute-start | bytes 1775624 | tf_op jit(solution)/shard_map/ppermute | solution.py:280
  414.5 44.3 %collective-permute-start.38 = (bf16[136,2176]{1,0:T(8,128)(2,1)S(1)}, bf16[136,2176]{1,0:T(8,128)(2,1)S(1)}, u32[]{:S(2)}, u32[]{:S(2)}) collective-permute-start(bf16[136,2176]{1,0:T(8,128)(2,1)S(1)} %select_convert_fusion.3), channel_id=1, source_target_pairs={{0,2},{1,3},{2,0},{3,1},{4,6},{5,7},{6,4},{7,5},{8,10},{9,11},{10,... | collective-permute-start | bytes 1775624 | tf_op jit(solution)/shard_map/ppermute | solution.py:280
  458.4 19.1 %collective-permute-start.23 = (bf16[136,1600]{1,0:T(8,128)(2,1)S(1)}, bf16[136,1600]{1,0:T(8,128)(2,1)S(1)}, u32[]{:S(2)}, u32[]{:S(2)}) collective-permute-start(bf16[136,1600]{1,0:T(8,128)(2,1)S(1)} %pad_maximum_fusion.27), channel_id=1, source_target_pairs={{0,2},{1,3},{2,0},{3,1},{4,6},{5,7},{6,4},{7,5},{8,10},{9,11},{10,... | collective-permute-start | bytes 1305608 | tf_op jit(solution)/shard_map/ppermute | solution.py:286
  458.8 12.2 %collective-permute-start.47 = (bf16[72,2176]{1,0:T(8,128)(2,1)S(1)}, bf16[72,2176]{1,0:T(8,128)(2,1)S(1)}, u32[]{:S(2)}, u32[]{:S(2)}) collective-permute-start(bf16[72,2176]{1,0:T(8,128)(2,1)S(1)} %select_convert_fusion.8), channel_id=1, source_target_pairs={{0,4},{1,5},{2,6},{3,7},{4,0},{5,1},{6,2},{7,3},{8,12},{9,13},{10,... | collective-permute-start | bytes 940040 | tf_op jit(solution)/shard_map/ppermute | solution.py:280
  471.0 22.4 %collective-permute-start.15 = (bf16[136,1664]{1,0:T(8,128)(2,1)S(1)}, bf16[136,1664]{1,0:T(8,128)(2,1)S(1)}, u32[]{:S(2)}, u32[]{:S(2)}) collective-permute-start(bf16[136,1664]{1,0:T(8,128)(2,1)S(1)} %pad_maximum_fusion.26), channel_id=1, source_target_pairs={{0,1},{1,0},{2,3},{3,2},{4,5},{5,4},{6,7},{7,6},{8,9},{9,8},{10,11... | collective-permute-start | bytes 1357832 | tf_op jit(solution)/shard_map/ppermute | solution.py:286
  476.3 15.1 %collective-permute-start.48 = (bf16[40,2176]{1,0:T(8,128)(2,1)S(1)}, bf16[40,2176]{1,0:T(8,128)(2,1)S(1)}, u32[]{:S(2)}, u32[]{:S(2)}) collective-permute-start(bf16[40,2176]{1,0:T(8,128)(2,1)S(1)} %select_convert_fusion.15), channel_id=1, source_target_pairs={{0,8},{1,9},{2,10},{3,11},{4,12},{5,13},{6,14},{7,15},{8,0},{9,1},... | collective-permute-start | bytes 522248 | tf_op jit(solution)/shard_map/ppermute | solution.py:280
  477.5 15.8 %collective-permute-start.40 = (bf16[40,2176]{1,0:T(8,128)(2,1)S(1)}, bf16[40,2176]{1,0:T(8,128)(2,1)S(1)}, u32[]{:S(2)}, u32[]{:S(2)}) collective-permute-start(bf16[40,2176]{1,0:T(8,128)(2,1)S(1)} %select_convert_fusion.16), channel_id=1, source_target_pairs={{0,8},{1,9},{2,10},{3,11},{4,12},{5,13},{6,14},{7,15},{8,0},{9,1},... | collective-permute-start | bytes 522248 | tf_op jit(solution)/shard_map/ppermute | solution.py:280
  491.4 27.4 %collective-permute-start.24 = (bf16[272,1600]{1,0:T(8,128)(2,1)S(1)}, bf16[272,1600]{1,0:T(8,128)(2,1)S(1)}, u32[]{:S(2)}, u32[]{:S(2)}) collective-permute-start(bf16[272,1600]{1,0:T(8,128)(2,1)S(1)} %pad_maximum_fusion.14), channel_id=1, source_target_pairs={{0,1},{1,0},{2,3},{3,2},{4,5},{5,4},{6,7},{7,6},{8,9},{9,8},{10,11... | collective-permute-start | bytes 2611208 | tf_op jit(solution)/shard_map/ppermute | solution.py:286
  493.3 12.9 %collective-permute-start.49 = (bf16[40,2176]{1,0:T(8,128)(2,1)S(1)}, bf16[40,2176]{1,0:T(8,128)(2,1)S(1)}, u32[]{:S(2)}, u32[]{:S(2)}) collective-permute-start(bf16[40,2176]{1,0:T(8,128)(2,1)S(1)} %add_convert_fusion.5), channel_id=1, source_target_pairs={{0,8},{1,9},{2,10},{3,11},{4,12},{5,13},{6,14},{7,15},{8,0},{9,1},... | collective-permute-start | bytes 522248 | tf_op jit(solution)/shard_map/ppermute | solution.py:286
  493.4 12.9 %collective-permute-start.41 = (bf16[40,2176]{1,0:T(8,128)(2,1)S(1)}, bf16[40,2176]{1,0:T(8,128)(2,1)S(1)}, u32[]{:S(2)}, u32[]{:S(2)}) collective-permute-start(bf16[40,2176]{1,0:T(8,128)(2,1)S(1)} %add_convert_fusion.6), channel_id=1, source_target_pairs={{0,8},{1,9},{2,10},{3,11},{4,12},{5,13},{6,14},{7,15},{8,0},{9,1},... | collective-permute-start | bytes 522248 | tf_op jit(solution)/shard_map/ppermute | solution.py:286
  496.7 22.5 %collective-permute-start.16 = (bf16[272,1664]{1,0:T(8,128)(2,1)S(1)}, bf16[272,1664]{1,0:T(8,128)(2,1)S(1)}, u32[]{:S(2)}, u32[]{:S(2)}) collective-permute-start(bf16[272,1664]{1,0:T(8,128)(2,1)S(1)} %pad_maximum_fusion.13), channel_id=1, source_target_pairs={{0,2},{1,3},{2,0},{3,1},{4,6},{5,7},{6,4},{7,5},{8,10},{9,11},{10,... | collective-permute-start | bytes 2715656 | tf_op jit(solution)/shard_map/ppermute | solution.py:286
  513.5 13.9 %collective-permute-start.51 = (bf16[136,2176]{1,0:T(8,128)(2,1)S(1)}, bf16[136,2176]{1,0:T(8,128)(2,1)S(1)}, u32[]{:S(2)}, u32[]{:S(2)}) collective-permute-start(bf16[136,2176]{1,0:T(8,128)(2,1)S(1)} %pad_maximum_fusion.19), channel_id=1, source_target_pairs={{0,1},{1,0},{2,3},{3,2},{4,5},{5,4},{6,7},{7,6},{8,9},{9,8},{10,11... | collective-permute-start | bytes 1775624 | tf_op jit(solution)/shard_map/ppermute | solution.py:286
  516.9 16.4 %collective-permute-start.43 = (bf16[136,2176]{1,0:T(8,128)(2,1)S(1)}, bf16[136,2176]{1,0:T(8,128)(2,1)S(1)}, u32[]{:S(2)}, u32[]{:S(2)}) collective-permute-start(bf16[136,2176]{1,0:T(8,128)(2,1)S(1)} %pad_maximum_fusion.18), channel_id=1, source_target_pairs={{0,2},{1,3},{2,0},{3,1},{4,6},{5,7},{6,4},{7,5},{8,10},{9,11},{10,... | collective-permute-start | bytes 1775624 | tf_op jit(solution)/shard_map/ppermute | solution.py:286
  527.7 24.0 %collective-permute-start.52 = (bf16[272,2176]{1,0:T(8,128)(2,1)S(1)}, bf16[272,2176]{1,0:T(8,128)(2,1)S(1)}, u32[]{:S(2)}, u32[]{:S(2)}) collective-permute-start(bf16[272,2176]{1,0:T(8,128)(2,1)S(1)} %pad_maximum_fusion.10), channel_id=1, source_target_pairs={{0,2},{1,3},{2,0},{3,1},{4,6},{5,7},{6,4},{7,5},{8,10},{9,11},{10,... | collective-permute-start | bytes 3551240 | tf_op jit(solution)/shard_map/ppermute | solution.py:286
  533.5 18.6 %collective-permute-start.44 = (bf16[272,2176]{1,0:T(8,128)(2,1)S(1)}, bf16[272,2176]{1,0:T(8,128)(2,1)S(1)}, u32[]{:S(2)}, u32[]{:S(2)}) collective-permute-start(bf16[272,2176]{1,0:T(8,128)(2,1)S(1)} %pad_maximum_fusion.9), channel_id=1, source_target_pairs={{0,1},{1,0},{2,3},{3,2},{4,5},{5,4},{6,7},{7,6},{8,9},{9,8},{10,11... | collective-permute-start | bytes 3551240 | tf_op jit(solution)/shard_map/ppermute | solution.py:286
  (91 other events, 689.2 us)
Sparse Core Ops, SparseCore 0:
  9.6 13.8 all-gather.3
  25.0 23.0 all-gather.5
  49.7 22.9 all-gather.7

commit v2 on v1

--- a/solution.py
+++ b/solution.py
@@ -137,12 +137,12 @@
     dev_ref[...] = dvv_ref[:, :early].astype(bfloat)
 
 
-def attention_specs(length, heads):
+def attention_specs(length, heads, begin=0):
     early = length - SKIP
-    block = lambda skip: pl.BlockSpec((HDIM, length), lambda h: (h + skip, 0))
-    early_block = lambda skip: pl.BlockSpec((HDIM, early), lambda h: (h + skip, 0))
+    block = lambda skip: pl.BlockSpec((HDIM, length), lambda h: (h + begin + skip, 0))
+    early_block = lambda skip: pl.BlockSpec((HDIM, early), lambda h: (h + begin + skip, 0))
     whole = lambda shape: pl.BlockSpec(shape, lambda h: (0, 0))
-    row_block = pl.BlockSpec((1, 1, length), lambda h: (h, 0, 0))
+    row_block = pl.BlockSpec((1, 1, length), lambda h: (h + begin, 0, 0))
     inputs = [
         pl.BlockSpec(memory_space=pltpu.SMEM),
         whole((1, length)),
@@ -194,16 +194,18 @@
     )
 
 
-def attend_back(flag, documents, early_docs, qkv, early_kv, grads, outs, lse):
-    width, length = qkv.shape[0] // 3, qkv.shape[1]
-    heads = width // HDIM
+def attend_back(flag, documents, early_docs, qkv, early_kv, grads, outs, lse, begin, end):
+    length = qkv.shape[1]
     early = length - SKIP
-    block, early_block, row_block, inputs, scratch = attention_specs(length, heads)
+    heads = qkv.shape[0] // 3 // HDIM
+    block, early_block, row_block, inputs, scratch = attention_specs(length, heads, begin)
+    width = (end - begin) * HDIM
+    out_block, early_block, *_ = attention_specs(length, heads)
     return pl.pallas_call(
         attend_back_kernel,
-        grid=(heads,),
+        grid=(end - begin,),
         in_specs=inputs + [block, block, row_block],
-        out_specs=[block, block, block, early_block, early_block],
+        out_specs=[out_block, out_block, out_block, early_block, early_block],
         out_shape=[
             jax.ShapeDtypeStruct((width, length), bfloat),
             jax.ShapeDtypeStruct((width, length), single),
@@ -217,9 +219,7 @@
             pltpu.VMEM((HDIM, length + early), single),
         ],
         compiler_params=pltpu.CompilerParams(vmem_limit_bytes=32 * 2**20),
-        cost_estimate=pl.CostEstimate(
-            flops=30 * 10**9, bytes_accessed=12 * 10**6, transcendentals=0
-        ),
+        cost_estimate=NO_COST,
         name="attend_back",
     )(
         flag,
@@ -248,62 +248,319 @@
     return jnp.where(first, lower, upper), jnp.where(first, upper, lower)
 
 
-def both_tokens(mine, arrived):
-    return jnp.concatenate([mine, arrived], axis=1)
-
-
-def partners(count, bit):
-    return [(i, i ^ (1 << bit)) for i in range(count)]
+class Line:
+    def __init__(self):
+        self.standing = []
+
+    def enter(self, *values):
+        standing = tuple(holder[key] for holder, key in self.standing)
+        passed = lax.optimization_barrier(values + standing)
+        for (holder, key), value in zip(self.standing, passed[len(values) :]):
+            holder[key] = value
+        self.standing = []
+        return passed[: len(values)]
+
+    def leave(self, holder, sent=(), **values):
+        passed = lax.optimization_barrier(tuple(sent) + tuple(values.values()))
+        holder.update(zip(values, passed[len(sent) :]))
+        self.standing += [(holder, key) for key in values]
+        return passed[: len(sent)]
 
 
 def window(rows):
     return -(-rows // 16) * 8
 
 
-def summed_product(former, latter, order):
-    count = lax.axis_size("replica")
-    at = lax.axis_index("replica")
-    if not order:
-        return lax.psum(dot(former, latter, 1, 1), "replica")
-    sizes = []
-    total = None
-    for bit in order:
-        source = former if total is None else total
-        rows = source.shape[0]
+class Sum:
+    def __init__(self, line, order):
+        count = lax.axis_size("replica")
+        bits = count.bit_length() - 1
+        self.line = line
+        self.plain = count != 1 << bits
+        self.order = list(order) if len(order) <= bits else []
+        self.order += [(i, i) for i in range(len(self.order), bits)]
+        self.place = 0
+        self.sizes = []
+
+    def low(self, bit):
+        at = jnp.where(lax.axis_index("shard") == 0, bit[0], bit[1])
+        return ((lax.axis_index("replica") >> at) & 1) == 0
+
+    def pass_on(self, block, bit):
+        count = lax.axis_size("replica")
+        route = [
+            (core * count + i, core * count + (i ^ (1 << bit[core])))
+            for core in range(2)
+            for i in range(count)
+        ]
+        self.arrived = lax.ppermute(block, ("shard", "replica"), route)
+
+    def split(self, block, bit):
+        rows = block.shape[0]
         size = window(rows)
-        low = ((at >> bit) & 1) == 0
-        lower, upper = source[:size], source[rows - size :]
-        sent, kept = jnp.where(low, upper, lower), jnp.where(low, lower, upper)
-        if total is None:
-            sent = dot(sent, latter, 1, 1)
-            kept = dot(kept, latter, 1, 1)
-        arrived = lax.ppermute(sent.astype(bfloat), "replica", partners(count, bit))
-        total = kept + arrived.astype(single)
-        sizes.append(rows)
-    whole = total.astype(bfloat)
-    for bit, rows in zip(order[::-1], sizes[::-1]):
-        low = ((at >> bit) & 1) == 0
-        arrived = lax.ppermute(whole, "replica", partners(count, bit))
-        lower, upper = jnp.where(low, whole, arrived), jnp.where(low, arrived, whole)
-        whole = jnp.concatenate([lower, upper[2 * window(rows) - rows :]], axis=0)
-    return whole.astype(single)
-
-
-def summed_small(values):
-    count = lax.axis_size("replica")
-    if count & (count - 1):
-        return lax.psum(values, "replica")
-    for bit in range(count.bit_length() - 1):
-        values = values + lax.ppermute(values, "replica", partners(count, bit))
-    return values
-
-
-def orders():
-    count = lax.axis_size("replica")
-    if count & (count - 1):
-        return (), ()
-    bits = tuple(range(count.bit_length() - 1))
-    return bits, bits[1:2] + bits[:1] + bits[2:]
+        low = self.low(bit)
+        lower, upper = block[:size], block[rows - size :]
+        return jnp.where(low, upper, lower), jnp.where(low, lower, upper)
+
+    def send(self, pairs):
+        if self.plain:
+            self.pairs = pairs
+            return pairs[0][0]
+        bit = self.order[0]
+        self.sizes.append(pairs[0][0].shape[0])
+        sent = sum(dot(self.split(former, bit)[0], latter, 1, 1) for former, latter in pairs)
+        return sent.astype(bfloat)
+
+    def keep(self, pairs):
+        bit = self.order[0]
+        return sum(dot(self.split(former, bit)[1], latter, 1, 1) for former, latter in pairs)
+
+    def finished(self):
+        return self.place == (0 if self.plain else 2 * len(self.order) - 1)
+
+    def step(self):
+        if self.finished():
+            return
+        bits = len(self.order)
+        if self.place < bits:
+            arrived, total = self.line.enter(self.arrived, self.total)
+            total = total + arrived.astype(single)
+            if self.place == bits - 1:
+                self.line.leave(self.__dict__, whole=total.astype(bfloat))
+                self.pass_on(self.whole, self.order[-1])
+            else:
+                bit = self.order[self.place + 1]
+                self.sizes.append(total.shape[0])
+                sent, kept = self.split(total, bit)
+                (sent,) = self.line.leave(self.__dict__, [sent.astype(bfloat)], total=kept)
+                self.pass_on(sent, bit)
+        else:
+            arrived, whole = self.line.enter(self.arrived, self.whole)
+            at = 2 * bits - 1 - self.place
+            rows = self.sizes[at]
+            low = self.low(self.order[at])
+            lower, upper = jnp.where(low, whole, arrived), jnp.where(low, arrived, whole)
+            whole = jnp.concatenate([lower, upper[2 * window(rows) - rows :]], axis=0)
+            self.line.leave(self.__dict__, whole=whole)
+            self.pass_on(self.whole, self.order[at - 1])
+        self.place += 1
+
+
+def assemble_kernel(groups, low_ref, *refs):
+    out_ref = refs[-1]
+    step = pl.program_id(0)
+    at = 0
+    for row, lanes in enumerate(groups):
+        lane = 0
+        for width in lanes:
+            whole_ref, arrived_ref = refs[2 * at], refs[2 * at + 1]
+            for half in range(2):
+                for low, source in ((1 - half, whole_ref), (half, arrived_ref)):
+
+                    @pl.when((step == 2 * row + half) & (low_ref[at] == low))
+                    def _(lane=lane, width=width, source=source):
+                        out_ref[:, lane : lane + width] = source[...].astype(single)
+
+            lane += width
+            at += 1
+
+
+def assembled(line, groups):
+    sums = [one for row in groups for one in row]
+    if sums[0].plain:
+        blocks = [
+            [lax.psum(sum(dot(a, b, 1, 1) for a, b in one.pairs), "replica") for one in row]
+            for row in groups
+        ]
+        return jnp.concatenate([jnp.concatenate(row, axis=1) for row in blocks], axis=0)
+    blocks = line.enter(*[block for one in sums for block in (one.whole, one.arrived)])
+    lows = jnp.stack([one.low(one.order[0]) for one in sums]).astype(jnp.int32)
+    rows = blocks[0].shape[0]
+    lanes = [[one.whole.shape[1] for one in row] for row in groups]
+    out = pl.pallas_call(
+        lambda *refs: assemble_kernel(lanes, *refs),
+        grid=(2 * len(groups),),
+        in_specs=[pl.BlockSpec(memory_space=pltpu.SMEM)]
+        + [pl.BlockSpec(block.shape, lambda i: (0, 0)) for block in blocks],
+        out_specs=pl.BlockSpec((rows, sum(lanes[0])), lambda i: (i, 0)),
+        out_shape=jax.ShapeDtypeStruct((2 * rows * len(groups), sum(lanes[0])), single),
+        compiler_params=pltpu.CompilerParams(vmem_limit_bytes=40 * 2**20),
+        cost_estimate=NO_COST,
+        name="assemble",
+    )(lows, *blocks)
+    return out
+
+
+class SmallSum:
+    def __init__(self, line):
+        self.line = line
+        self.place = 0
+        count = lax.axis_size("replica")
+        self.plain = count & (count - 1) != 0
+        self.steps = 1 if self.plain else count.bit_length()
+
+    def send(self, mine, theirs):
+        (theirs,) = self.line.leave(self.__dict__, [theirs], total=mine)
+        self.arrived = swapped(theirs)
+
+    def finished(self):
+        return self.place == self.steps
+
+    def step(self):
+        if self.finished():
+            return
+        count = lax.axis_size("replica")
+        total, arrived = self.line.enter(self.total, self.arrived)
+        self.line.leave(self.__dict__, total=total + arrived)
+        if self.plain:
+            self.total = lax.psum(self.total, "replica")
+        elif self.place < self.steps - 1:
+            route = [(i, i ^ (1 << self.place)) for i in range(count)]
+            self.arrived = lax.ppermute(self.total, "replica", route)
+        self.place += 1
+
+
+NO_COST = pl.CostEstimate(flops=0, bytes_accessed=0, transcendentals=0)
+
+
+def gelu_slope(values):
+    root = (2 / 3.141592653589793) ** 0.5
+    square = values * values
+    curve = jnp.tanh(root * values * (1.0 + 0.044715 * square))
+    return 0.5 * (1.0 + curve) + 0.5 * root * values * (1.0 - curve * curve) * (
+        1.0 + 3 * 0.044715 * square
+    )
+
+
+def grad_pre_kernel(w_ref, cot_ref, pre_ref, out_ref, sum_ref):
+    grad = dot(w_ref[...], cot_ref[...], 0, 0)
+    grad = (grad * gelu_slope(pre_ref[...])).astype(bfloat)
+    out_ref[...] = grad
+    sum_ref[...] = jnp.sum(grad.astype(single), axis=1, keepdims=True)
+
+
+def grad_pre_of(full_down, cotangent, pre_active):
+    width, ff = full_down.shape
+    length = cotangent.shape[1]
+    tile = 256
+    return pl.pallas_call(
+        grad_pre_kernel,
+        grid=(ff // tile,),
+        in_specs=[
+            pl.BlockSpec((width, tile), lambda i: (0, i)),
+            pl.BlockSpec((width, length), lambda i: (0, 0)),
+            pl.BlockSpec((tile, length), lambda i: (i, 0)),
+        ],
+        out_specs=[
+            pl.BlockSpec((tile, length), lambda i: (i, 0)),
+            pl.BlockSpec((tile, 1), lambda i: (i, 0)),
+        ],
+        out_shape=[
+            jax.ShapeDtypeStruct((ff, length), bfloat),
+            jax.ShapeDtypeStruct((ff, 1), single),
+        ],
+        compiler_params=pltpu.CompilerParams(vmem_limit_bytes=24 * 2**20),
+        cost_estimate=NO_COST,
+        name="grad_pre",
+    )(full_down, cotangent, pre_active)
+
+
+def grad_middle_kernel(
+    w_ref, grad_ref, normal_ref, scale_ref, gain_ref, cot_ref,
+    middle_ref, branch_ref, gain_sum_ref, shift_sum_ref, branch_sum_ref, total_ref,
+):
+    step = pl.program_id(0)
+    tile = w_ref.shape[0]
+    place = pl.ds(pl.multiple_of(step * tile, tile), tile)
+    total_ref[place, :] = dot(w_ref[...], grad_ref[...], 1, 0)
+
+    @pl.when(step == pl.num_programs(0) - 1)
+    def _():
+        width, length = total_ref.shape
+        rows = width // 4
+        z_sum = jnp.zeros((1, length), single)
+        zn_sum = jnp.zeros((1, length), single)
+        for start in range(0, width, rows):
+            at = slice(start, start + rows)
+            grad = total_ref[at]
+            normal = normal_ref[at]
+            product = grad * normal
+            gain = gain_ref[at]
+            gain_sum_ref[at] = jnp.sum(product, axis=1, keepdims=True)
+            shift_sum_ref[at] = jnp.sum(grad, axis=1, keepdims=True)
+            z_sum += jnp.sum(grad * gain, axis=0, keepdims=True)
+            zn_sum += jnp.sum(product * gain, axis=0, keepdims=True)
+        z_mean = z_sum / width
+        zn_mean = zn_sum / width
+        for start in range(0, width, rows):
+            at = slice(start, start + rows)
+            z = total_ref[at] * gain_ref[at]
+            middle = cot_ref[at].astype(single) + (
+                z - z_mean - normal_ref[at] * zn_mean
+            ) * scale_ref[...]
+            branch = middle.astype(bfloat)
+            middle_ref[at] = middle
+            branch_ref[at] = branch
+            branch_sum_ref[at] = jnp.sum(branch.astype(single), axis=1, keepdims=True)
+
+
+def grad_middle_of(full_up, grad_pre, normal, scale, gain, cotangent):
+    width, ff = full_up.shape
+    length = cotangent.shape[1]
+    tile = width // 4
+    whole = lambda rows, lanes: pl.BlockSpec((rows, lanes), lambda i: (0, 0))
+    return pl.pallas_call(
+        grad_middle_kernel,
+        grid=(width // tile,),
+        in_specs=[
+            pl.BlockSpec((tile, ff), lambda i: (i, 0)),
+            whole(ff, length),
+            whole(width, length),
+            whole(1, length),
+            whole(width, 1),
+            whole(width, length),
+        ],
+        out_specs=[whole(width, length), whole(width, length)] + [whole(width, 1)] * 3,
+        out_shape=[
+            jax.ShapeDtypeStruct((width, length), single),
+            jax.ShapeDtypeStruct((width, length), bfloat),
+        ]
+        + [jax.ShapeDtypeStruct((width, 1), single)] * 3,
+        scratch_shapes=[pltpu.VMEM((width, length), single)],
+        compiler_params=pltpu.CompilerParams(vmem_limit_bytes=40 * 2**20),
+        cost_estimate=NO_COST,
+        name="grad_middle",
+    )(full_up, grad_pre, normal, scale, gain, cotangent)
+
+
+ORDER = (
+    "out", "Dsend", "Dkeep", "gact", "gn2", "DA", "Usend", "Ukeep", "DA", "gheads", "Osend",
+    "Okeep", "abackA", "DA", "OA", "abackB", "UA", "OA", "DA", "joinA", "joinB", "gproj",
+    "OA", "gn1", "UA", "DA", "OA", "Qsend", "Qkeep", "OA", "smalls", "S", "UA", "S", "DA",
+    "QA", "S", "OA", "S", "UA", "S", "OA", "QA", "DA", "UA", "OA", "QA", "UA", "DA", "QA",
+    "UA", "QA", "QA", "UA", "QA", "QA",
+)
+
+ROUTES = {
+    "DA": ((0, 1), (1, 0), (2, 2), (3, 3)),
+    "UA": ((1, 0), (0, 1), (2, 2), (3, 3)),
+    "OA": ((1, 0), (0, 1), (2, 2), (3, 3)),
+    "QA": ((1, 0), (0, 1), (2, 2), (3, 3)),
+}
+
+CUTS = {
+    "DA": ((0, 1088), (0, 2176)),
+    "UA": ((0, 544), (0, 4352)),
+    "OA": ((0, 544), (0, 1088)),
+    "QA": ((0, 544), (0, 3264)),
+}
+
+LAYOUTS = {
+    "D": [['DA']],
+    "U": [['UA']],
+    "O": [['OA']],
+    "Q": [['QA']],
+}
 
 
 def normalize(values):
@@ -346,7 +603,6 @@
     at = lax.axis_index("shard")
     first = at == 0
     flag = at.astype(jnp.int32).reshape(1)
-    order_one, order_two = orders()
     docs = documents[0]
     early_docs = lax.ppermute(docs, "shard", [(0, 1)])
 
@@ -400,6 +656,9 @@
     early_kv = lax.ppermute(qkv[width:, SKIP:], "shard", [(0, 1)])
     normed_one_arrived = swapped(normed_one_theirs)
 
+    qkv, early_kv, early_docs, normed_one_arrived, other_grad_rows = lax.optimization_barrier(
+        (qkv, early_kv, early_docs, normed_one_arrived, other_grad_rows)
+    )
     heads, lse = attend(flag, docs, early_docs, qkv, early_kv)
     heads_mine, heads_theirs = halves(heads, at)
     heads_arrived = swapped(heads_theirs)
@@ -408,117 +667,224 @@
     normed_two = (normal_two * col_gain_two + col_shift_two).astype(bfloat)
     normed_two_mine, normed_two_theirs = halves(normed_two, at)
     normed_two_arrived = swapped(normed_two_theirs)
+    normed_two, heads_arrived = lax.optimization_barrier((normed_two, heads_arrived))
     pre_active = dot(full_up, normed_two, 0, 0) + col_up
-    active, gelu_pull = jax.vjp(tanh_gelu, pre_active)
-    active = active.astype(bfloat)
+    active = tanh_gelu(pre_active).astype(bfloat)
     active_mine, active_theirs = halves(active, at)
     active_arrived = swapped(active_theirs)
-    output = (middle + dot(full_down, active, 1, 0) + col_down).astype(bfloat)
-
-    all_grad_rows = both_tokens(grad_rows, other_grad_rows)
-    all_active = both_tokens(active_mine, active_arrived)
-    middle_row = width // 2
-    grad_w_down = jnp.concatenate(
-        [
-            summed_product(all_grad_rows[:middle_row], all_active, order_one),
-            summed_product(all_grad_rows[middle_row:], all_active, order_two),
-        ],
-        axis=0,
-    ).T
-    grad_bias_down = jnp.sum(grad_rows.astype(single), axis=1)
-    grad_active = dot(full_down, grad_rows, 0, 0)
-    grad_pre = gelu_pull(grad_active)[0].astype(bfloat)
-    all_grad_pre = both_tokens(grad_pre, swapped(grad_pre))
-    grad_bias_up = jnp.sum(grad_pre.astype(single), axis=1)
-    all_normed_two = both_tokens(normed_two_mine, normed_two_arrived)
-    ff = grad_pre.shape[0]
-    grad_w_up = jnp.concatenate(
-        [
-            summed_product(all_normed_two, all_grad_pre[: ff // 2], order_one),
-            summed_product(all_normed_two, all_grad_pre[ff // 2 :], order_two),
-        ],
-        axis=1,
-    )
-    grad_normed_two = dot(full_up, grad_pre, 1, 0)
-    part_two, grad_gain_two, grad_shift_two = normalize_back(
-        grad_normed_two, normal_two, scale_two, col_gain_two
-    )
-    grad_middle = grad_rows.astype(single) + part_two
-    grad_branch = grad_middle.astype(bfloat)
-    grad_bias_out = jnp.sum(grad_branch.astype(single), axis=1)
-    grad_w_out = summed_product(
-        both_tokens(heads_mine, heads_arrived),
-        both_tokens(grad_branch, swapped(grad_branch)),
-        order_one,
-    )
-    grad_heads = dot(full_out, grad_branch, 1, 0).astype(bfloat)
-    grad_query, grad_key, grad_value, early_key, early_value = attend_back(
-        flag, docs, early_docs, qkv, early_kv, grad_heads, heads, lse
-    )
-    back_key, back_value = lax.ppermute((early_key, early_value), "shard", [(1, 0)])
+    line = Line()
+    sums = {name: Sum(line, order) for name, order in ROUTES.items()}
+    sums["S"] = SmallSum(line)
+    s = {}
+    half = width // 2
+    ff = pre_active.shape[0]
+
+    def stage_out():
+        active_now, middle_now = line.enter(active, middle)
+        out = (middle_now + dot(full_down, active_now, 1, 0) + col_down).astype(bfloat)
+        line.leave(s, output=out)
+
+    def send_matrix(matrix, pairs):
+        names = [name for row in LAYOUTS[matrix] for name in row]
+        sent = []
+        for name in names:
+            rows, lanes = [slice(*at) for at in CUTS[name]]
+            sent.append(
+                sums[name].send([(former[rows], latter[lanes]) for former, latter in pairs])
+            )
+        formers, latters = zip(*pairs)
+        sent = line.leave(
+            s, sent, **{matrix + str(i): one for i, one in enumerate(formers + latters)}
+        )
+        for name, value in zip(names, sent):
+            if not sums[name].plain:
+                sums[name].pass_on(value, sums[name].order[0])
+
+    def keep(matrix):
+        names = [name for row in LAYOUTS[matrix] for name in row]
+        if sums[names[0]].plain:
+            return
+        count = 2
+        values = line.enter(*[s[matrix + str(i)] for i in range(2 * count)])
+        for name in names:
+            rows, lanes = [slice(*at) for at in CUTS[name]]
+            pairs = [(a[rows], b[lanes]) for a, b in zip(values[:count], values[count:])]
+            line.leave(sums[name].__dict__, total=sums[name].keep(pairs))
+
+    def stage_down_send():
+        mine, arrived, s["normed_two_arrived"], own, other = line.enter(
+            active_mine, active_arrived, normed_two_arrived, grad_rows, other_grad_rows
+        )
+        send_matrix("D", [(own, mine), (other, arrived)])
+
+    def stage_grad_active():
+        (cot,) = line.enter(grad_rows)
+        grad_pre, bias_sum = grad_pre_of(full_down, cot, pre_active)
+        line.leave(s, grad_pre=grad_pre, grad_bias_up=bias_sum)
+        s["grad_pre_other"] = swapped(s["grad_pre"])
+
+    def stage_normed_two():
+        (grad_pre,) = line.enter(s["grad_pre"])
+        names = "grad_middle", "grad_branch", "grad_gain_two", "grad_shift_two", "grad_bias_out"
+        results = grad_middle_of(
+            full_up, grad_pre, normal_two, scale_two, col_gain_two, grad_rows
+        )
+        line.leave(s, **dict(zip(names, results)))
+        s["grad_branch_other"] = swapped(s["grad_branch"])
+
+    def stage_up_send():
+        mine, arrived, own, other = line.enter(
+            normed_two_mine, s["normed_two_arrived"], s["grad_pre"], s["grad_pre_other"]
+        )
+        send_matrix("U", [(mine, own), (arrived, other)])
+
+    def stage_out_send():
+        mine, arrived, own, other = line.enter(
+            heads_mine, heads_arrived, s["grad_branch"], s["grad_branch_other"]
+        )
+        send_matrix("O", [(mine, own), (arrived, other)])
+
+    def stage_grad_heads():
+        grad_branch, s["grad_branch_other"] = line.enter(s["grad_branch"], s["grad_branch_other"])
+        line.leave(s, grad_heads=dot(full_out, grad_branch, 1, 0).astype(bfloat))
+
+    heads_count = width // HDIM
+    ranges = {"A": (0, heads_count // 2), "B": (heads_count // 2, heads_count)}
+
+    def stage_attend_back(name):
+        (grad_heads,) = line.enter(s["grad_heads"])
+        results = attend_back(
+            flag, docs, early_docs, qkv, early_kv, grad_heads, heads, lse, *ranges[name]
+        )
+        back = jnp.concatenate(results[3:], axis=0)
+        kept = {name + str(i): one for i, one in enumerate(results[:3])}
+        (back,) = line.leave(s, [back], **kept)
+        s["back" + name] = lax.ppermute(back, "shard", [(1, 0)])
 
     def joined(own, back):
         return (own + jnp.pad(back.astype(single), ((0, 0), (SKIP, 0)))).astype(bfloat)
 
-    grad_value = joined(grad_value, back_value)
-    grad_project = jnp.concatenate(
-        [grad_query, joined(grad_key, back_key), grad_value], axis=0
-    )
-    grad_bias_query = jnp.sum(grad_query.astype(single), axis=1)
-    grad_bias_value = jnp.sum(grad_value.astype(single), axis=1)
-    all_grad_project = both_tokens(grad_project, swapped(grad_project))
-    all_normed_one = both_tokens(normed_one_mine, normed_one_arrived)
-    cut = (all_grad_project.shape[0] // 256 + 1) * 128
-    grad_w_qkv = jnp.concatenate(
-        [
-            summed_product(all_normed_one, all_grad_project[:cut], order_two),
-            summed_product(all_normed_one, all_grad_project[cut:], order_one),
-        ],
-        axis=1,
-    )
-    grad_normed_one = ordered(
-        dot(w_qkv, grad_project, 1, 0), dot(other_qkv, grad_project, 1, 0), 0
-    )
-    part_one, grad_gain_one, grad_shift_one = normalize_back(
-        grad_normed_one, normal_one, scale_one, col_gain_one
-    )
-    input_grad = (grad_middle + part_one).astype(bfloat)
-
-    small = jnp.stack(
-        [
-            grad_gain_one,
-            grad_shift_one,
-            grad_bias_query,
-            grad_bias_value,
-            grad_bias_out,
-            grad_gain_two,
-            grad_shift_two,
-            grad_bias_down,
-        ]
-    )
-    half = width // 2
-    lanes = grad_bias_up.shape[0] // 2 // half
-    up_parts = grad_bias_up.reshape(2, lanes, half)
-    lower = jnp.concatenate([small[:, :half], up_parts[0]], axis=0)
-    upper = jnp.concatenate([small[:, half:], up_parts[1]], axis=0)
-    mine, theirs = jnp.where(first, lower, upper), jnp.where(first, upper, lower)
-    mine = summed_small(mine + swapped(theirs))
+    def stage_join(name):
+        query, key, value, back = line.enter(*[s[name + str(i)] for i in range(3)], s["back" + name])
+        middle_row = back.shape[0] // 2
+        key, value = joined(key, back[:middle_row]), joined(value, back[middle_row:])
+        line.leave(s, **{name + "q": query, name + "k": key, name + "v": value})
+
+    def stage_project():
+        pieces = line.enter(*[s[name + part] for part in "qkv" for name in "AB"])
+        line.leave(s, grad_project=jnp.concatenate(pieces, axis=0))
+        s["grad_project_other"] = swapped(s["grad_project"])
+
+    def stage_normed_one():
+        (grad_project,) = line.enter(s["grad_project"])
+        grad_normed_one = ordered(
+            dot(w_qkv, grad_project, 1, 0), dot(other_qkv, grad_project, 1, 0), 0
+        )
+        part_one, gain_sum, shift_sum = normalize_back(
+            grad_normed_one, normal_one, scale_one, col_gain_one
+        )
+        line.leave(
+            s,
+            input_grad=(s["grad_middle"] + part_one).astype(bfloat),
+            grad_gain_one=gain_sum,
+            grad_shift_one=shift_sum,
+        )
+
+    def stage_small():
+        bias_out, gain_two_sum, shift_two_sum, bias_up_sum, cot, grad_project = line.enter(
+            s["grad_bias_out"],
+            s["grad_gain_two"],
+            s["grad_shift_two"],
+            s["grad_bias_up"],
+            grad_rows,
+            s["grad_project"],
+        )
+        small = jnp.stack(
+            [
+                s["grad_gain_one"],
+                s["grad_shift_one"],
+                jnp.sum(grad_project[:width].astype(single), axis=1),
+                jnp.sum(grad_project[2 * width :].astype(single), axis=1),
+                bias_out[:, 0],
+                gain_two_sum[:, 0],
+                shift_two_sum[:, 0],
+                jnp.sum(cot.astype(single), axis=1),
+            ]
+        )
+        lanes = ff // 2 // half
+        up_parts = bias_up_sum[:, 0].reshape(2, lanes, half)
+        lower = jnp.concatenate([small[:, :half], up_parts[0]], axis=0)
+        upper = jnp.concatenate([small[:, half:], up_parts[1]], axis=0)
+        sums["S"].send(jnp.where(first, lower, upper), jnp.where(first, upper, lower))
+
+    def stage_qkv_send():
+        mine, arrived, own, other = line.enter(
+            normed_one_mine, normed_one_arrived, s["grad_project"], s["grad_project_other"]
+        )
+        send_matrix("Q", [(mine, own), (arrived, other)])
+
+    stages = {
+        "out": stage_out,
+        "Dsend": stage_down_send,
+        "Dkeep": lambda: keep("D"),
+        "gact": stage_grad_active,
+        "gn2": stage_normed_two,
+        "Usend": stage_up_send,
+        "Ukeep": lambda: keep("U"),
+        "Osend": stage_out_send,
+        "Okeep": lambda: keep("O"),
+        "gheads": stage_grad_heads,
+        "abackA": lambda: stage_attend_back("A"),
+        "abackB": lambda: stage_attend_back("B"),
+        "joinA": lambda: stage_join("A"),
+        "joinB": lambda: stage_join("B"),
+        "gproj": stage_project,
+        "gn1": stage_normed_one,
+        "smalls": stage_small,
+        "Qsend": stage_qkv_send,
+        "Qkeep": lambda: keep("Q"),
+    }
+    grads = {}
+
+    def gather():
+        for name, layout in LAYOUTS.items():
+            rows_of = [[sums[one] for one in row] for row in layout]
+            sent = not waiting or not rows_of[0][0].plain
+            if name not in grads and sent and all(
+                one.finished() for row in rows_of for one in row
+            ):
+                grads[name] = assembled(line, rows_of)
+
+    waiting = set(stages)
+    for name in ORDER:
+        if name in stages:
+            stages[name]()
+            waiting.remove(name)
+        else:
+            sums[name].step()
+        if name not in stages:
+            gather()
+    while len(grads) < len(LAYOUTS) or not sums["S"].finished():
+        for one in sums.values():
+            one.step()
+        gather()
+    small = sums["S"].total
     return (
-        output.T[None],
-        input_grad.T[None],
-        grad_w_qkv,
-        grad_w_out,
-        grad_w_up,
-        grad_w_down,
-        mine[0],
-        mine[1],
-        mine[2],
-        mine[3],
-        mine[4],
-        mine[5],
-        mine[6],
-        mine[8:].reshape(-1),
-        mine[7],
+        s["output"].T[None],
+        s["input_grad"].T[None],
+        grads["Q"],
+        grads["O"],
+        grads["U"],
+        grads["D"].T,
+        small[0],
+        small[1],
+        small[2],
+        small[3],
+        small[4],
+        small[5],
+        small[6],
+        small[8:].reshape(-1),
+        small[7],
     )
 
 

time: 587 us -> 513 us (0.87)
  other arithmetic: 113 us -> 33.2 us
  Pallas kernels: 42.7 us -> 93.1 us
  starting transfers between devices: 82.7 us -> 56.4 us
  matrix products: 108 us -> 89.6 us
  waiting for transfers between devices: 208 us -> 193 us
  local copies, waits for them, and re-layouts: 10.2 us -> 23.8 us
    concatenate x28 -> x14, other arithmetic: 70.9 us -> 5.25 us  [the longest x12 5.08 us: step(): whole = jnp.concatenate([lower, upper[2 * window(rows) - rows:]], axis=0)]
    pallas_call x1 -> x8, Pallas kernels: 22.2 us -> 71.5 us  [the longest x2 23.8 us: attend_back(): pl.pallas_call(attend_back_kernel, grid=(end - begin,), in_specs=inputs +...]
    ppermute x62 -> x38, starting transfers between devices: 72.5 us -> 47.7 us  [the longest x32 41.4 us: pass_on(): self.arrived = lax.ppermute(block, ('shard', 'replica'), route)]
    dot_general x24, matrix products: 108 us -> 89.6 us  [dot(): lax.dot_general(former, latter, (((former_axis,), (latter_axis,)), ((), (...]
    ppermute x62 -> x38, waiting for transfers between devices: 201 us -> 187 us  [the longest x32 167 us: pass_on(): self.arrived = lax.ppermute(block, ('shard', 'replica'), route)]
    unnamed x120 -> x119, local copies, waits for them, and re-layouts: 5.3 us -> 14.1 us
    transpose x1 -> x0, other arithmetic: 8.54 us -> none  [shards(): grad_w_down = jnp.concatenate([summed_product(all_grad_rows[:middle_row],...]
  transfers between devices with their start and end apart: 79 -> 55, of which waited for: 34 -> 23; matrix products, arithmetic and copies ran while one was open for 31% -> 25% of each run, Pallas kernels for 4% -> 17%
where the time goes in v2:
time: 513 us; the launch traced here: 504 us
  waiting for transfers between devices  193 us (38%)
  Pallas kernels  93.1 us (18%)
  matrix products  89.6 us (17%)
  starting transfers between devices  56.4 us (11%)
  other arithmetic  33.2 us (6%)
  local copies, waits for them, and re-layouts  23.8 us (5%)
  between operations  15.8 us (3%)
    ppermute x32, waiting for transfers between devices, pass_on(): self.arrived = lax.ppermute(block, ('shard', 'replica'), route)  167 us
    dot_general x24, matrix products, dot(): lax.dot_general(former, latter, (((former_axis,), (latter_axis,)), ((), (...  89.6 us
    ppermute x32, starting transfers between devices, pass_on(): self.arrived = lax.ppermute(block, ('shard', 'replica'), route)  41.4 us
    pallas_call x2, Pallas kernels, attend_back(): pl.pallas_call(attend_back_kernel, grid=(end - begin,), in_specs=inputs +...  23.8 us
    pallas_call x1, Pallas kernels, attend(): pl.pallas_call(attend_kernel, grid=(heads,), in_specs=inputs, out_specs=[...  21.6 us
    pallas_call x4, Pallas kernels, assembled(): pl.pallas_call(lambda *refs: assemble_kernel(lanes, *refs), grid=(2 * len...  20.1 us
    ppermute x4, waiting for transfers between devices, step(): self.arrived = lax.ppermute(self.total, 'replica', route)  19.6 us
    pallas_call x1, Pallas kernels, grad_pre_of(): pl.pallas_call(grad_pre_kernel, grid=(ff // tile,), in_specs=[pl.BlockSpe...  16.2 us
  transfers between devices with their start and end apart: 55, of which 23 were waited for; matrix products, arithmetic and copies ran while one was open for 25% of the time, Pallas kernels for 17%

profile of v2, /device:TPU:0, one launch (start us, length us, event | category | flops | bytes accessed | tf_op | source)
XLA Modules:
  0.0 504.4 jit_solution(2483893744094249210)
XLA Ops:
  11.5 3.7 collective-permute-done
  21.0 2.8 fusion.115
  23.8 5.0 %fusion.9.q_ref.k_ref.v_ref = bf16[3264,512]{1,0:T(8,128)(2,1)S(1)} fusion(f32[512,3264]{0,1:T(8,128)S(1)} %fusion.115, bf16[544,512]{1,0:T(8,128)(2,1)} %get-tuple-element.611, bf16[544,3264]{1,0:T(8,128)(2,1)} %collective-permute-done.1, f32[3264]{0:T(1024)S(1)} %reduce.6), kind=kOutput, calls=%fused_computation.16 | convolution fusion | flops 1823244288 | bytes 14148352 | tf_op jit(solution)/shard_map/dot_general | solution.py:17
  30.2 3.2 collective-permute-start.2
  34.0 2.6 collective-permute-start.3
  41.0 21.6 %attend.1 = (bf16[1088,512]{1,0:T(8,128)(2,1)S(1)}, f32[17,1,512]{2,1,0:T(1,128)S(1)}) custom-call(s32[1]{0:T(128)} %bitcast.1.flag_ref, s32[1,512]{1,0:T(1,128)S(1)} %copy-done.16, s32[512,1]{1,0:T(8,128)S(1)} %copy-done.3, s32[512,1]{1,0:T(8,128)S(1)} %copy-done.5, bf16[3264,512]{1,0:T(8,128)(2,1)S(1)} %fusion.9.q_ref.k_ref.v_ref, ...), custom_call_target="tpu_custom_call" | custom-call | flops 12000000000 | bytes 6000000 | tf_op jit(solution)/shard_map/attend/pallas_call | solution.py:169
  65.0 5.5 %fusion.114 = (f32[512]{0:T(512)S(1)}, f32[512,1088]{0,1:T(8,128)S(1)}) fusion(f32[1088]{0:T(1024)S(1)} %get-tuple-element.624, bf16[1088,512]{1,0:T(8,128)(2,1)} %copy-done, bf16[1088,1088]{1,0:T(8,128)(2,1)} %all-gather.4.cloned.1.call-done, bf16[1,512,1088]{1,2,0:T(8,128)(2,1)} %param.16), kind=kOutput, calls=%fused_computation.266 | convolution fusion | flops 1214381568 | bytes 6830336 | tf_op jit(solution)/shard_map/dot_general | solution.py:17
  73.0 13.3 %fusion.7 = (bf16[4352,512]{1,0:T(8,128)(2,1)S(1)}, f32[4352,512]{1,0:T(8,128)}) fusion(f32[4352]{0:T(1024)S(1)} %maximum_convert_fusion.1, bf16[1088,512]{1,0:T(8,128)(2,1)} %get-tuple-element.297, bf16[1088,4352]{1,0:T(8,128)(2,1)} %all-gather.6.cloned.1.call-done.w_ref), kind=kOutput, calls=%fused_computation.8 | convolution fusion | flops 4870897664 | bytes 23970816 | tf_op jit(solution)/shard_map/dot_general | solution.py:17
  86.3 2.5 broadcast_select_fusion
  89.8 2.3 broadcast_select_fusion.12
  92.6 10.5 %fusion.15 = bf16[1088,512]{1,0:T(8,128)(2,1)} fusion(f32[1088,512]{1,0:T(8,128)} %bitcast.146, bf16[1088,4352]{1,0:T(8,128)(2,1)} %all-gather.8.cloned.1.call-done.w_ref, bf16[4352,512]{1,0:T(8,128)(2,1)} %copy-done.24, f32[1088]{0:T(1024)S(1)} %get-tuple-element.627), kind=kOutput, calls=%fused_computation.29 | convolution fusion | flops 4850286592 | bytes 17273088 | tf_op jit(solution)/shard_map/dot_general | solution.py:17
  103.1 3.6 fusion.43
  106.7 4.1 fusion.11
  112.9 2.9 fusion.39
  115.8 5.8 %convolution_add_fusion.4 = f32[544,2176]{1,0:T(8,128)} fusion(f32[544,2176]{1,0:T(8,128)S(1)} %fusion.39, bf16[2176,512]{1,0:T(8,128)(2,1)} %collective-permute-done.8, bf16[1088,512]{1,0:T(8,128)(2,1)} %collective-permute-done.5, pred[]{:T(512)S(6)} %eq.11), kind=kOutput, calls=%fused_computation.18 | convolution fusion | flops 1213616128 | bytes 12812289 | tf_op jit(solution)/shard_map/dot_general | solution.py:17
  121.7 16.2 %grad_pre.1 = (bf16[4352,512]{1,0:T(8,128)(2,1)}, f32[4352,1]{1,0:T(8,128)S(1)}) custom-call(bf16[1088,4352]{1,0:T(8,128)(2,1)S(1)} %bitcast.138, bf16[1088,512]{1,0:T(8,128)(2,1)} %bitcast.8.cot_ref, f32[4352,512]{1,0:T(8,128)S(1)} %bitcast.140), custom_call_target="tpu_custom_call" | custom-call | tf_op jit(solution)/shard_map/grad_pre/pallas_call | solution.py:446
  142.0 11.4 %grad_middle.1 = (f32[1088,512]{1,0:T(8,128)S(1)}, bf16[1088,512]{1,0:T(8,128)(2,1)S(1)}, f32[1088,1]{1,0:T(8,128)S(1)}, f32[1088,1]{1,0:T(8,128)S(1)}, f32[1088,1]{1,0:T(8,128)S(1)}) custom-call(bf16[1088,4352]{1,0:T(8,128)(2,1)} %all-gather.6.cloned.1.call-done.w_ref, bf16[4352,512]{1,0:T(8,128)(2,1)} %get-tuple-element.342.grad_ref, ...), custom_call_target="tpu_custom_call" | custom-call | tf_op jit(solution)/shard_map/grad_middle/pallas_call | solution.py:512
  158.2 3.9 fusion.89
  162.1 3.7 fusion.8
  166.4 3.7 fusion.85
  170.1 3.9 convolution_add_fusion
  185.3 11.3 %attend_back.2 = (bf16[512,512]{1,0:T(8,128)(2,1)S(1)}, f32[512,512]{1,0:T(8,128)S(1)}, f32[512,512]{1,0:T(8,128)S(1)}, bf16[512,384]{1,0:T(8,128)(2,1)S(1)}, bf16[512,384]{1,0:T(8,128)(2,1)S(1)}) custom-call(s32[1]{0:T(128)} %bitcast.1.flag_ref, s32[1,512]{1,0:T(1,128)S(1)} %copy-done.16, s32[512,1]{1,0:T(8,128)S(1)} %copy-done.4, s32[512,1]{1,0:T(8,128)S(1)} %copy-done.6, ...), custom_call_target="tpu_custom_call" | custom-call | tf_op jit(solution)/shard_map/attend_back/pallas_call | solution.py:204
  198.3 6.7 %collective-permute-done.15 = bf16[272,1088]{1,0:T(8,128)(2,1)S(1)} collective-permute-done((bf16[272,1088]{1,0:T(8,128)(2,1)S(1)}, bf16[272,1088]{1,0:T(8,128)(2,1)S(1)}, u32[]{:S(2)}, u32[]{:S(2)}) %collective-permute-start.15) | collective-permute-done | bytes 591904 | tf_op jit(solution)/shard_map/ppermute | solution.py:296
  205.2 12.6 %attend_back.3 = (bf16[576,512]{1,0:T(8,128)(2,1)S(1)}, f32[576,512]{1,0:T(8,128)S(1)}, f32[576,512]{1,0:T(8,128)S(1)}, bf16[576,384]{1,0:T(8,128)(2,1)S(1)}, bf16[576,384]{1,0:T(8,128)(2,1)S(1)}) custom-call(s32[1]{0:T(128)} %bitcast.1.flag_ref, s32[1,512]{1,0:T(1,128)S(1)} %copy-done.16, s32[512,1]{1,0:T(8,128)S(1)} %copy-done.4, s32[512,1]{1,0:T(8,128)S(1)} %copy-done.6, ...), custom_call_target="tpu_custom_call" | custom-call | tf_op jit(solution)/shard_map/attend_back/pallas_call | solution.py:204
  219.5 2.4 collective-permute-start.20
  228.1 7.8 %collective-permute-done.20 = bf16[72,2176]{1,0:T(8,128)(2,1)S(1)} collective-permute-done((bf16[72,2176]{1,0:T(8,128)(2,1)S(1)}, bf16[72,2176]{1,0:T(8,128)(2,1)S(1)}, u32[]{:S(2)}, u32[]{:S(2)}) %collective-permute-start.20) | collective-permute-done | bytes 313376 | tf_op jit(solution)/shard_map/ppermute | solution.py:296
  241.1 4.1 select_bitcast_fusion.1
  248.2 2.9 collective-permute-start.24
  254.4 2.3 collective-permute-start.27
  263.4 4.0 convolution_add_fusion.2
  282.8 15.1 %collective-permute-done.28 = bf16[136,2176]{1,0:T(8,128)(2,1)S(1)} collective-permute-done((bf16[136,2176]{1,0:T(8,128)(2,1)}, bf16[136,2176]{1,0:T(8,128)(2,1)S(1)}, u32[]{:S(2)}, u32[]{:S(2)}) %collective-permute-start.28) | collective-permute-done | bytes 591904 | tf_op jit(solution)/shard_map/ppermute | solution.py:296
  301.2 2.7 collective-permute-done.38
  308.5 16.2 %collective-permute-done.40 = f32[12,544]{1,0:T(8,128)S(1)} collective-permute-done((f32[12,544]{1,0:T(8,128)S(1)}, f32[12,544]{1,0:T(8,128)S(1)}, u32[]{:S(2)}, u32[]{:S(2)}) %collective-permute-start.40) | collective-permute-done | bytes 26144 | tf_op jit(solution)/shard_map/ppermute | solution.py:419
  324.8 5.9 %collective-permute-done.32 = bf16[136,3264]{1,0:T(8,128)(2,1)S(1)} collective-permute-done((bf16[136,3264]{1,0:T(8,128)(2,1)S(1)}, bf16[136,3264]{1,0:T(8,128)(2,1)S(1)}, u32[]{:S(2)}, u32[]{:S(2)}) %collective-permute-start.32) | collective-permute-done | bytes 887840 | tf_op jit(solution)/shard_map/ppermute | solution.py:296
  333.3 11.8 %collective-permute-done.34 = bf16[72,3264]{1,0:T(8,128)(2,1)S(1)} collective-permute-done((bf16[72,3264]{1,0:T(8,128)(2,1)S(1)}, bf16[72,3264]{1,0:T(8,128)(2,1)S(1)}, u32[]{:S(2)}, u32[]{:S(2)}) %collective-permute-start.34) | collective-permute-done | bytes 470048 | tf_op jit(solution)/shard_map/ppermute | solution.py:296
  345.3 11.3 %collective-permute-done.42 = bf16[72,4352]{1,0:T(8,128)(2,1)S(1)} collective-permute-done((bf16[72,4352]{1,0:T(8,128)(2,1)S(1)}, bf16[72,4352]{1,0:T(8,128)(2,1)S(1)}, u32[]{:S(2)}, u32[]{:S(2)}) %collective-permute-start.42) | collective-permute-done | bytes 626720 | tf_op jit(solution)/shard_map/ppermute | solution.py:296
  360.0 9.8 %collective-permute-done.41 = bf16[40,3264]{1,0:T(8,128)(2,1)S(1)} collective-permute-done((bf16[40,3264]{1,0:T(8,128)(2,1)S(1)}, bf16[40,3264]{1,0:T(8,128)(2,1)S(1)}, u32[]{:S(2)}, u32[]{:S(2)}) %collective-permute-start.41) | collective-permute-done | bytes 261152 | tf_op jit(solution)/shard_map/ppermute | solution.py:296
  369.9 5.0 collective-permute-done.44
  374.9 9.2 %collective-permute-done.43 = bf16[40,3264]{1,0:T(8,128)(2,1)S(1)} collective-permute-done((bf16[40,3264]{1,0:T(8,128)(2,1)S(1)}, bf16[40,3264]{1,0:T(8,128)(2,1)S(1)}, u32[]{:S(2)}, u32[]{:S(2)}) %collective-permute-start.43) | collective-permute-done | bytes 261152 | tf_op jit(solution)/shard_map/ppermute | solution.py:296
  384.8 11.2 %collective-permute-done.45 = bf16[72,3264]{1,0:T(8,128)(2,1)S(1)} collective-permute-done((bf16[72,3264]{1,0:T(8,128)(2,1)S(1)}, bf16[72,3264]{1,0:T(8,128)(2,1)S(1)}, u32[]{:S(2)}, u32[]{:S(2)}) %collective-permute-start.45) | collective-permute-done | bytes 470048 | tf_op jit(solution)/shard_map/ppermute | solution.py:296
  399.9 45.7 %collective-permute-done.46 = bf16[136,3264]{1,0:T(8,128)(2,1)S(1)} collective-permute-done((bf16[136,3264]{1,0:T(8,128)(2,1)S(1)}, bf16[136,3264]{1,0:T(8,128)(2,1)S(1)}, u32[]{:S(2)}, u32[]{:S(2)}) %collective-permute-start.46) | collective-permute-done | bytes 887840 | tf_op jit(solution)/shard_map/ppermute | solution.py:296
  447.6 2.5 collective-permute-start.48
  450.1 8.3 %collective-permute-done.48 = bf16[136,1088]{1,0:T(8,128)(2,1)S(1)} collective-permute-done((bf16[136,1088]{1,0:T(8,128)(2,1)S(1)}, bf16[136,1088]{1,0:T(8,128)(2,1)S(1)}, u32[]{:S(2)}, u32[]{:S(2)}) %collective-permute-start.48) | collective-permute-done | bytes 295968 | tf_op jit(solution)/shard_map/ppermute | solution.py:296
  461.2 16.1 %collective-permute-done.49.refs_2_ = bf16[272,1088]{1,0:T(8,128)(2,1)} collective-permute-done((bf16[272,1088]{1,0:T(8,128)(2,1)S(1)}, bf16[272,1088]{1,0:T(8,128)(2,1)}, u32[]{:S(2)}, u32[]{:S(2)}) %collective-permute-start.49) | collective-permute-done | bytes 591904 | tf_op jit(solution)/shard_map/ppermute | solution.py:296
  477.3 2.6 assemble.5
  479.9 5.7 %assemble.7 = f32[1088,2176]{1,0:T(8,128)} custom-call(s32[1]{0:T(128)} %bitcast.24.refs_0_, bf16[544,2176]{1,0:T(8,128)(2,1)S(1)} %pad_maximum_fusion.1.refs_1_, bf16[544,2176]{1,0:T(8,128)(2,1)} %collective-permute-done.51.refs_2_), custom_call_target="tpu_custom_call" | custom-call | tf_op jit(solution)/shard_map/assemble/pallas_call | solution.py:380
  485.7 6.5 %assemble.6 = f32[544,4352]{1,0:T(8,128)} custom-call(s32[1]{0:T(128)} %bitcast.23.refs_0_, bf16[272,4352]{1,0:T(8,128)(2,1)} %pad_maximum_fusion.refs_1_, bf16[272,4352]{1,0:T(8,128)(2,1)} %collective-permute-done.50.refs_2_), custom_call_target="tpu_custom_call" | custom-call | tf_op jit(solution)/shard_map/assemble/pallas_call | solution.py:380
  492.1 5.3 %assemble.4 = f32[544,3264]{1,0:T(8,128)} custom-call(s32[1]{0:T(128)} %bitcast.23.refs_0_, bf16[272,3264]{1,0:T(8,128)(2,1)} %pad_maximum_fusion.3.refs_1_, bf16[272,3264]{1,0:T(8,128)(2,1)} %collective-permute-done.47.refs_2_), custom_call_target="tpu_custom_call" | custom-call | tf_op jit(solution)/shard_map/assemble/pallas_call | solution.py:380
  (365 shorter events, 111.1 us)
Async XLA Ops:
  7.2 57.8 %all-gather.4.cloned.1.call-start = ((), (), s32[]{:S(2)}) async-start(), calls=%async_computation | async-start | bytes 3760128 | tf_op jit(solution)/shard_map/all_gather | solution.py:623
  8.0 65.0 %all-gather.6.cloned.1.call-start = ((), (), s32[]{:S(2)}) async-start(), calls=%async_computation.1 | async-start | bytes 14204928 | tf_op jit(solution)/shard_map/all_gather | solution.py:624
  8.7 83.8 %all-gather.8.cloned.1.call-start = ((), (), s32[]{:S(2)}) async-start(), calls=%async_computation.2 | async-start | bytes 14204928 | tf_op jit(solution)/shard_map/all_gather | solution.py:625
  8.8 15.0 %collective-permute-start.1 = (bf16[544,3264]{1,0:T(8,128)(2,1)}, bf16[544,3264]{1,0:T(8,128)(2,1)}, u32[]{:S(2)}, u32[]{:S(2)}) collective-permute-start(bf16[544,3264]{1,0:T(8,128)(2,1)} %param.19), channel_id=1, source_target_pairs={{0,16},{16,0},{1,17},{17,1},{2,18},{18,2},{3,19},{19,3},{4,20},{20... | collective-permute-start | bytes 10653704 | tf_op jit(solution)/shard_map/ppermute | solution.py:241
  9.5 5.7 %collective-permute-start = (bf16[8,544]{1,0:T(8,128)(2,1)S(1)}, bf16[8,544]{1,0:T(8,128)(2,1)S(1)}, u32[]{:S(2)}, u32[]{:S(2)}) collective-permute-start(bf16[8,544]{1,0:T(8,128)(2,1)S(1)} %stack.57), channel_id=1, source_target_pairs={{0,16},{16,0},{1,17},{17,1},{2,18},{18,2},{3,19},{19,3},{4,20},{20... | collective-permute-start | bytes 26120 | tf_op jit(solution)/shard_map/ppermute | solution.py:241
  30.2 8.0 %collective-permute-start.2 = (bf16[2176,384]{1,0:T(8,128)(2,1)}, bf16[2176,384]{1,0:T(8,128)(2,1)}, u32[]{:S(2)}, u32[]{:S(2)}) collective-permute-start(bf16[2176,384]{1,0:T(8,128)(2,1)} %slice.404), channel_id=1, source_target_pairs={{0,16},{1,17},{2,18},{3,19},{4,20},{5,21},{6,22},{7,23},{8,24},{9,... | collective-permute-start | bytes 5013512 | tf_op jit(solution)/shard_map/ppermute | solution.py:656
  64.7 8.4 %collective-permute-start.6 = (bf16[544,512]{1,0:T(8,128)(2,1)}, bf16[544,512]{1,0:T(8,128)(2,1)}, u32[]{:S(2)}, u32[]{:S(2)}) collective-permute-start(bf16[544,512]{1,0:T(8,128)(2,1)} %get-tuple-element.608), channel_id=1, source_target_pairs={{0,16},{16,0},{1,17},{17,1},{2,18},{18,2},{3,19},{19,3},{4,20},{20... | collective-permute-start | bytes 1671176 | tf_op jit(solution)/shard_map/ppermute | solution.py:241
  89.8 13.3 %collective-permute-start.8 = (bf16[2176,512]{1,0:T(8,128)(2,1)}, bf16[2176,512]{1,0:T(8,128)(2,1)}, u32[]{:S(2)}, u32[]{:S(2)}) collective-permute-start(bf16[2176,512]{1,0:T(8,128)(2,1)} %get-tuple-element.595), channel_id=1, source_target_pairs={{0,16},{16,0},{1,17},{17,1},{2,18},{18,2},{3,19},{19,3},{4,20},{20... | collective-permute-start | bytes 6684680 | tf_op jit(solution)/shard_map/ppermute | solution.py:241
  92.2 10.9 %collective-permute-start.9 = (bf16[544,512]{1,0:T(8,128)(2,1)}, bf16[544,512]{1,0:T(8,128)(2,1)}, u32[]{:S(2)}, u32[]{:S(2)}) collective-permute-start(bf16[544,512]{1,0:T(8,128)(2,1)} %get-tuple-element.610), channel_id=1, source_target_pairs={{0,16},{16,0},{1,17},{17,1},{2,18},{18,2},{3,19},{19,3},{4,20},{20... | collective-permute-start | bytes 1671176 | tf_op jit(solution)/shard_map/ppermute | solution.py:241
  110.9 43.1 %collective-permute-start.11 = (bf16[544,2176]{1,0:T(8,128)(2,1)}, bf16[544,2176]{1,0:T(8,128)(2,1)}, u32[]{:S(2)}, u32[]{:S(2)}) collective-permute-start(bf16[544,2176]{1,0:T(8,128)(2,1)} %fusion.11), channel_id=1, source_target_pairs={{0,1},{1,0},{2,3},{3,2},{4,5},{5,4},{6,7},{7,6},{8,9},{9,8},{10,11... | collective-permute-start | bytes 7102472 | tf_op jit(solution)/shard_map/ppermute | solution.py:296
  139.2 18.9 %collective-permute-start.10 = (bf16[4352,512]{1,0:T(8,128)(2,1)}, bf16[4352,512]{1,0:T(8,128)(2,1)}, u32[]{:S(2)}, u32[]{:S(2)}) collective-permute-start(bf16[4352,512]{1,0:T(8,128)(2,1)} %get-tuple-element.342.grad_ref), channel_id=1, source_target_pairs={{0,16},{16,0},{1,17},{17,1},{2,18},{18,2},{3,19},{19,3},{4,20},{20... | collective-permute-start | bytes 13369352 | tf_op jit(solution)/shard_map/ppermute | solution.py:241
  153.5 21.1 %collective-permute-start.14 = (bf16[1088,512]{1,0:T(8,128)(2,1)S(1)}, bf16[1088,512]{1,0:T(8,128)(2,1)S(1)}, u32[]{:S(2)}, u32[]{:S(2)}) collective-permute-start(bf16[1088,512]{1,0:T(8,128)(2,1)S(1)} %get-tuple-element.364), channel_id=1, source_target_pairs={{0,16},{16,0},{1,17},{17,1},{2,18},{18,2},{3,19},{19,3},{4,20},{20... | collective-permute-start | bytes 3342344 | tf_op jit(solution)/shard_map/ppermute | solution.py:241
  156.6 17.4 %collective-permute-start.13 = (bf16[272,2176]{1,0:T(8,128)(2,1)S(1)}, bf16[272,2176]{1,0:T(8,128)(2,1)S(1)}, u32[]{:S(2)}, u32[]{:S(2)}) collective-permute-start(bf16[272,2176]{1,0:T(8,128)(2,1)S(1)} %select_convert_fusion.1), channel_id=1, source_target_pairs={{0,2},{1,3},{2,0},{3,1},{4,6},{5,7},{6,4},{7,5},{8,10},{9,11},{10,... | collective-permute-start | bytes 3551240 | tf_op jit(solution)/shard_map/ppermute | solution.py:296
  165.9 57.5 %collective-permute-start.12 = (bf16[272,4352]{1,0:T(8,128)(2,1)S(1)}, bf16[272,4352]{1,0:T(8,128)(2,1)S(1)}, u32[]{:S(2)}, u32[]{:S(2)}) collective-permute-start(bf16[272,4352]{1,0:T(8,128)(2,1)S(1)} %fusion.8), channel_id=1, source_target_pairs={{0,2},{1,3},{2,0},{3,1},{4,6},{5,7},{6,4},{7,5},{8,10},{9,11},{10,... | collective-permute-start | bytes 7102472 | tf_op jit(solution)/shard_map/ppermute | solution.py:296
  179.8 25.2 %collective-permute-start.15 = (bf16[272,1088]{1,0:T(8,128)(2,1)S(1)}, bf16[272,1088]{1,0:T(8,128)(2,1)S(1)}, u32[]{:S(2)}, u32[]{:S(2)}) collective-permute-start(bf16[272,1088]{1,0:T(8,128)(2,1)S(1)} %fusion.20), channel_id=1, source_target_pairs={{0,2},{1,3},{2,0},{3,1},{4,6},{5,7},{6,4},{7,5},{8,10},{9,11},{10,... | collective-permute-start | bytes 1775624 | tf_op jit(solution)/shard_map/ppermute | solution.py:296
  181.4 16.6 %collective-permute-start.16 = (bf16[136,2176]{1,0:T(8,128)(2,1)S(1)}, bf16[136,2176]{1,0:T(8,128)(2,1)S(1)}, u32[]{:S(2)}, u32[]{:S(2)}) collective-permute-start(bf16[136,2176]{1,0:T(8,128)(2,1)S(1)} %select_convert_fusion.4), channel_id=1, source_target_pairs={{0,4},{1,5},{2,6},{3,7},{4,0},{5,1},{6,2},{7,3},{8,12},{9,13},{10,... | collective-permute-start | bytes 1775624 | tf_op jit(solution)/shard_map/ppermute | solution.py:296
  196.7 39.4 %collective-permute-start.22 = (bf16[1024,384]{1,0:T(8,128)(2,1)S(1)}, bf16[1024,384]{1,0:T(8,128)(2,1)S(1)}, u32[]{:S(2)}, u32[]{:S(2)}) collective-permute-start(bf16[1024,384]{1,0:T(8,128)(2,1)S(1)} %pad_maximum_fusion.8), channel_id=1, source_target_pairs={{16,0},{17,1},{18,2},{19,3},{20,4},{21,5},{22,6},{23,7},{24,8},{25... | collective-permute-start | bytes 2359304 | tf_op jit(solution)/shard_map/ppermute | solution.py:762
  217.9 7.0 %collective-permute-start.18 = (bf16[136,1088]{1,0:T(8,128)(2,1)S(1)}, bf16[136,1088]{1,0:T(8,128)(2,1)S(1)}, u32[]{:S(2)}, u32[]{:S(2)}) collective-permute-start(bf16[136,1088]{1,0:T(8,128)(2,1)S(1)} %select_convert_fusion.7), channel_id=1, source_target_pairs={{0,1},{1,0},{2,3},{3,2},{4,5},{5,4},{6,7},{7,6},{8,9},{9,8},{10,11... | collective-permute-start | bytes 887816 | tf_op jit(solution)/shard_map/ppermute | solution.py:296
  219.5 16.4 %collective-permute-start.20 = (bf16[72,2176]{1,0:T(8,128)(2,1)S(1)}, bf16[72,2176]{1,0:T(8,128)(2,1)S(1)}, u32[]{:S(2)}, u32[]{:S(2)}) collective-permute-start(bf16[72,2176]{1,0:T(8,128)(2,1)S(1)} %select_convert_fusion.8), channel_id=1, source_target_pairs={{0,8},{1,9},{2,10},{3,11},{4,12},{5,13},{6,14},{7,15},{8,0},{9,1},... | collective-permute-start | bytes 940040 | tf_op jit(solution)/shard_map/ppermute | solution.py:296
  221.9 14.5 %collective-permute-start.21 = (bf16[1152,384]{1,0:T(8,128)(2,1)S(1)}, bf16[1152,384]{1,0:T(8,128)(2,1)S(1)}, u32[]{:S(2)}, u32[]{:S(2)}) collective-permute-start(bf16[1152,384]{1,0:T(8,128)(2,1)S(1)} %pad_maximum_fusion.7), channel_id=1, source_target_pairs={{16,0},{17,1},{18,2},{19,3},{20,4},{21,5},{22,6},{23,7},{24,8},{25... | collective-permute-start | bytes 2654216 | tf_op jit(solution)/shard_map/ppermute | solution.py:762
  225.0 26.0 %collective-permute-start.17 = (bf16[136,4352]{1,0:T(8,128)(2,1)S(1)}, bf16[136,4352]{1,0:T(8,128)(2,1)S(1)}, u32[]{:S(2)}, u32[]{:S(2)}) collective-permute-start(bf16[136,4352]{1,0:T(8,128)(2,1)S(1)} %select_convert_fusion), channel_id=1, source_target_pairs={{0,1},{1,0},{2,3},{3,2},{4,5},{5,4},{6,7},{7,6},{8,9},{9,8},{10,11... | collective-permute-start | bytes 3551240 | tf_op jit(solution)/shard_map/ppermute | solution.py:296
  226.6 11.3 %collective-permute-start.19 = (bf16[72,1088]{1,0:T(8,128)(2,1)S(1)}, bf16[72,1088]{1,0:T(8,128)(2,1)S(1)}, u32[]{:S(2)}, u32[]{:S(2)}) collective-permute-start(bf16[72,1088]{1,0:T(8,128)(2,1)S(1)} %select_convert_fusion.10), channel_id=1, source_target_pairs={{0,4},{1,5},{2,6},{3,7},{4,0},{5,1},{6,2},{7,3},{8,12},{9,13},{10,... | collective-permute-start | bytes 470024 | tf_op jit(solution)/shard_map/ppermute | solution.py:296
  236.0 17.5 %collective-permute-start.25 = (bf16[72,2176]{1,0:T(8,128)(2,1)S(1)}, bf16[72,2176]{1,0:T(8,128)(2,1)S(1)}, u32[]{:S(2)}, u32[]{:S(2)}) collective-permute-start(bf16[72,2176]{1,0:T(8,128)(2,1)S(1)} %add_convert_fusion.7), channel_id=1, source_target_pairs={{0,8},{1,9},{2,10},{3,11},{4,12},{5,13},{6,14},{7,15},{8,0},{9,1},... | collective-permute-start | bytes 940040 | tf_op jit(solution)/shard_map/ppermute | solution.py:296
  237.1 21.7 %collective-permute-start.23 = (bf16[3264,512]{1,0:T(8,128)(2,1)S(1)}, bf16[3264,512]{1,0:T(8,128)(2,1)S(1)}, u32[]{:S(2)}, u32[]{:S(2)}) collective-permute-start(bf16[3264,512]{1,0:T(8,128)(2,1)S(1)} %constant_dynamic-update-slice_fusion), channel_id=1, source_target_pairs={{0,16},{16,0},{1,17},{17,1},{2,18},{18,2},{3,19},{19,3},{4,20},{20... | collective-permute-start | bytes 10027016 | tf_op jit(solution)/shard_map/ppermute | solution.py:241
  248.2 6.2 %collective-permute-start.24 = (bf16[40,1088]{1,0:T(8,128)(2,1)S(1)}, bf16[40,1088]{1,0:T(8,128)(2,1)S(1)}, u32[]{:S(2)}, u32[]{:S(2)}) collective-permute-start(bf16[40,1088]{1,0:T(8,128)(2,1)S(1)} %select_convert_fusion.11), channel_id=1, source_target_pairs={{0,8},{1,9},{2,10},{3,11},{4,12},{5,13},{6,14},{7,15},{8,0},{9,1},... | collective-permute-start | bytes 261128 | tf_op jit(solution)/shard_map/ppermute | solution.py:296
  254.4 13.1 %collective-permute-start.27 = (bf16[40,1088]{1,0:T(8,128)(2,1)S(1)}, bf16[40,1088]{1,0:T(8,128)(2,1)S(1)}, u32[]{:S(2)}, u32[]{:S(2)}) collective-permute-start(bf16[40,1088]{1,0:T(8,128)(2,1)S(1)} %add_convert_fusion.9), channel_id=1, source_target_pairs={{0,8},{1,9},{2,10},{3,11},{4,12},{5,13},{6,14},{7,15},{8,0},{9,1},... | collective-permute-start | bytes 261128 | tf_op jit(solution)/shard_map/ppermute | solution.py:296
  256.7 21.0 %collective-permute-start.29 = (bf16[72,4352]{1,0:T(8,128)(2,1)}, bf16[72,4352]{1,0:T(8,128)(2,1)}, u32[]{:S(2)}, u32[]{:S(2)}) collective-permute-start(bf16[72,4352]{1,0:T(8,128)(2,1)} %select_convert_fusion.3), channel_id=1, source_target_pairs={{0,4},{1,5},{2,6},{3,7},{4,0},{5,1},{6,2},{7,3},{8,12},{9,13},{10,... | collective-permute-start | bytes 1880072 | tf_op jit(solution)/shard_map/ppermute | solution.py:296
  274.1 23.9 %collective-permute-start.28 = (bf16[136,2176]{1,0:T(8,128)(2,1)}, bf16[136,2176]{1,0:T(8,128)(2,1)S(1)}, u32[]{:S(2)}, u32[]{:S(2)}) collective-permute-start(bf16[136,2176]{1,0:T(8,128)(2,1)} %pad_maximum_fusion.11), channel_id=1, source_target_pairs={{0,4},{1,5},{2,6},{3,7},{4,0},{5,1},{6,2},{7,3},{8,12},{9,13},{10,... | collective-permute-start | bytes 1775624 | tf_op jit(solution)/shard_map/ppermute | solution.py:296
  274.2 26.9 %collective-permute-start.37 = (bf16[72,1088]{1,0:T(8,128)(2,1)S(1)}, bf16[72,1088]{1,0:T(8,128)(2,1)S(1)}, u32[]{:S(2)}, u32[]{:S(2)}) collective-permute-start(bf16[72,1088]{1,0:T(8,128)(2,1)S(1)} %copy-done.30), channel_id=1, source_target_pairs={{0,4},{1,5},{2,6},{3,7},{4,0},{5,1},{6,2},{7,3},{8,12},{9,13},{10,... | collective-permute-start | bytes 470024 | tf_op jit(solution)/shard_map/ppermute | solution.py:296
  276.2 23.0 %collective-permute-start.26 = (bf16[272,3264]{1,0:T(8,128)(2,1)S(1)}, bf16[272,3264]{1,0:T(8,128)(2,1)S(1)}, u32[]{:S(2)}, u32[]{:S(2)}) collective-permute-start(bf16[272,3264]{1,0:T(8,128)(2,1)S(1)} %fusion.10), channel_id=1, source_target_pairs={{0,2},{1,3},{2,0},{3,1},{4,6},{5,7},{6,4},{7,5},{8,10},{9,11},{10,... | collective-permute-start | bytes 5326856 | tf_op jit(solution)/shard_map/ppermute | solution.py:296
  279.1 24.8 %collective-permute-start.36 = (bf16[40,4352]{1,0:T(8,128)(2,1)S(1)}, bf16[40,4352]{1,0:T(8,128)(2,1)S(1)}, u32[]{:S(2)}, u32[]{:S(2)}) collective-permute-start(bf16[40,4352]{1,0:T(8,128)(2,1)S(1)} %select_convert_fusion.6), channel_id=1, source_target_pairs={{0,8},{1,9},{2,10},{3,11},{4,12},{5,13},{6,14},{7,15},{8,0},{9,1},... | collective-permute-start | bytes 1044488 | tf_op jit(solution)/shard_map/ppermute | solution.py:296
  281.5 18.3 %collective-permute-start.33 = (f32[12,544]{1,0:T(8,128)S(1)}, f32[12,544]{1,0:T(8,128)S(1)}, u32[]{:S(2)}, u32[]{:S(2)}) collective-permute-start(f32[12,544]{1,0:T(8,128)S(1)} %add.267), channel_id=1, source_target_pairs={{0,2},{1,3},{2,0},{3,1},{4,6},{5,7},{6,4},{7,5},{8,10},{9,11},{10,... | collective-permute-start | bytes 78344 | tf_op jit(solution)/shard_map/ppermute | solution.py:419
  304.0 20.7 %collective-permute-start.39 = (bf16[40,4352]{1,0:T(8,128)(2,1)S(1)}, bf16[40,4352]{1,0:T(8,128)(2,1)S(1)}, u32[]{:S(2)}, u32[]{:S(2)}) collective-permute-start(bf16[40,4352]{1,0:T(8,128)(2,1)S(1)} %add_convert_fusion.6), channel_id=1, source_target_pairs={{0,8},{1,9},{2,10},{3,11},{4,12},{5,13},{6,14},{7,15},{8,0},{9,1},... | collective-permute-start | bytes 1044488 | tf_op jit(solution)/shard_map/ppermute | solution.py:296
  305.8 18.9 %collective-permute-start.40 = (f32[12,544]{1,0:T(8,128)S(1)}, f32[12,544]{1,0:T(8,128)S(1)}, u32[]{:S(2)}, u32[]{:S(2)}) collective-permute-start(f32[12,544]{1,0:T(8,128)S(1)} %add.271), channel_id=1, source_target_pairs={{0,8},{1,9},{2,10},{3,11},{4,12},{5,13},{6,14},{7,15},{8,0},{9,1},... | collective-permute-start | bytes 78344 | tf_op jit(solution)/shard_map/ppermute | solution.py:419
  307.0 26.3 %collective-permute-start.35 = (bf16[272,2176]{1,0:T(8,128)(2,1)S(1)}, bf16[272,2176]{1,0:T(8,128)(2,1)S(1)}, u32[]{:S(2)}, u32[]{:S(2)}) collective-permute-start(bf16[272,2176]{1,0:T(8,128)(2,1)S(1)} %pad_maximum_fusion.4), channel_id=1, source_target_pairs={{0,2},{1,3},{2,0},{3,1},{4,6},{5,7},{6,4},{7,5},{8,10},{9,11},{10,... | collective-permute-start | bytes 3551240 | tf_op jit(solution)/shard_map/ppermute | solution.py:296
  307.7 23.0 %collective-permute-start.32 = (bf16[136,3264]{1,0:T(8,128)(2,1)S(1)}, bf16[136,3264]{1,0:T(8,128)(2,1)S(1)}, u32[]{:S(2)}, u32[]{:S(2)}) collective-permute-start(bf16[136,3264]{1,0:T(8,128)(2,1)S(1)} %select_convert_fusion.2), channel_id=1, source_target_pairs={{0,1},{1,0},{2,3},{3,2},{4,5},{5,4},{6,7},{7,6},{8,9},{9,8},{10,11... | collective-permute-start | bytes 2663432 | tf_op jit(solution)/shard_map/ppermute | solution.py:296
  331.1 14.0 %collective-permute-start.34 = (bf16[72,3264]{1,0:T(8,128)(2,1)S(1)}, bf16[72,3264]{1,0:T(8,128)(2,1)S(1)}, u32[]{:S(2)}, u32[]{:S(2)}) collective-permute-start(bf16[72,3264]{1,0:T(8,128)(2,1)S(1)} %select_convert_fusion.5), channel_id=1, source_target_pairs={{0,4},{1,5},{2,6},{3,7},{4,0},{5,1},{6,2},{7,3},{8,12},{9,13},{10,... | collective-permute-start | bytes 1410056 | tf_op jit(solution)/shard_map/ppermute | solution.py:296
  331.8 24.7 %collective-permute-start.42 = (bf16[72,4352]{1,0:T(8,128)(2,1)S(1)}, bf16[72,4352]{1,0:T(8,128)(2,1)S(1)}, u32[]{:S(2)}, u32[]{:S(2)}) collective-permute-start(bf16[72,4352]{1,0:T(8,128)(2,1)S(1)} %pad_maximum_fusion.9), channel_id=1, source_target_pairs={{0,4},{1,5},{2,6},{3,7},{4,0},{5,1},{6,2},{7,3},{8,12},{9,13},{10,... | collective-permute-start | bytes 1880072 | tf_op jit(solution)/shard_map/ppermute | solution.py:296
  356.7 13.1 %collective-permute-start.41 = (bf16[40,3264]{1,0:T(8,128)(2,1)S(1)}, bf16[40,3264]{1,0:T(8,128)(2,1)S(1)}, u32[]{:S(2)}, u32[]{:S(2)}) collective-permute-start(bf16[40,3264]{1,0:T(8,128)(2,1)S(1)} %select_convert_fusion.9), channel_id=1, source_target_pairs={{0,8},{1,9},{2,10},{3,11},{4,12},{5,13},{6,14},{7,15},{8,0},{9,1},... | collective-permute-start | bytes 783368 | tf_op jit(solution)/shard_map/ppermute | solution.py:296
  358.6 16.3 %collective-permute-start.44 = (bf16[136,4352]{1,0:T(8,128)(2,1)S(1)}, bf16[136,4352]{1,0:T(8,128)(2,1)S(1)}, u32[]{:S(2)}, u32[]{:S(2)}) collective-permute-start(bf16[136,4352]{1,0:T(8,128)(2,1)S(1)} %pad_maximum_fusion.5), channel_id=1, source_target_pairs={{0,1},{1,0},{2,3},{3,2},{4,5},{5,4},{6,7},{7,6},{8,9},{9,8},{10,11... | collective-permute-start | bytes 3551240 | tf_op jit(solution)/shard_map/ppermute | solution.py:296
  369.9 14.2 %collective-permute-start.43 = (bf16[40,3264]{1,0:T(8,128)(2,1)S(1)}, bf16[40,3264]{1,0:T(8,128)(2,1)S(1)}, u32[]{:S(2)}, u32[]{:S(2)}) collective-permute-start(bf16[40,3264]{1,0:T(8,128)(2,1)S(1)} %add_convert_fusion.8), channel_id=1, source_target_pairs={{0,8},{1,9},{2,10},{3,11},{4,12},{5,13},{6,14},{7,15},{8,0},{9,1},... | collective-permute-start | bytes 783368 | tf_op jit(solution)/shard_map/ppermute | solution.py:296
  384.2 11.8 %collective-permute-start.45 = (bf16[72,3264]{1,0:T(8,128)(2,1)S(1)}, bf16[72,3264]{1,0:T(8,128)(2,1)S(1)}, u32[]{:S(2)}, u32[]{:S(2)}) collective-permute-start(bf16[72,3264]{1,0:T(8,128)(2,1)S(1)} %pad_maximum_fusion.12), channel_id=1, source_target_pairs={{0,4},{1,5},{2,6},{3,7},{4,0},{5,1},{6,2},{7,3},{8,12},{9,13},{10,... | collective-permute-start | bytes 1410056 | tf_op jit(solution)/shard_map/ppermute | solution.py:296
  384.7 95.2 %collective-permute-start.51 = (bf16[544,2176]{1,0:T(8,128)(2,1)S(1)}, bf16[544,2176]{1,0:T(8,128)(2,1)}, u32[]{:S(2)}, u32[]{:S(2)}) collective-permute-start(bf16[544,2176]{1,0:T(8,128)(2,1)S(1)} %pad_maximum_fusion.1.refs_1_), channel_id=1, source_target_pairs={{0,1},{1,0},{2,3},{3,2},{4,5},{5,4},{6,7},{7,6},{8,9},{9,8},{10,11... | collective-permute-start | bytes 7102472 | tf_op jit(solution)/shard_map/ppermute | solution.py:296
  396.2 49.5 %collective-permute-start.46 = (bf16[136,3264]{1,0:T(8,128)(2,1)S(1)}, bf16[136,3264]{1,0:T(8,128)(2,1)S(1)}, u32[]{:S(2)}, u32[]{:S(2)}) collective-permute-start(bf16[136,3264]{1,0:T(8,128)(2,1)S(1)} %pad_maximum_fusion.6), channel_id=1, source_target_pairs={{0,1},{1,0},{2,3},{3,2},{4,5},{5,4},{6,7},{7,6},{8,9},{9,8},{10,11... | collective-permute-start | bytes 2663432 | tf_op jit(solution)/shard_map/ppermute | solution.py:296
  398.3 87.4 %collective-permute-start.50 = (bf16[272,4352]{1,0:T(8,128)(2,1)}, bf16[272,4352]{1,0:T(8,128)(2,1)}, u32[]{:S(2)}, u32[]{:S(2)}) collective-permute-start(bf16[272,4352]{1,0:T(8,128)(2,1)} %pad_maximum_fusion.refs_1_), channel_id=1, source_target_pairs={{0,2},{1,3},{2,0},{3,1},{4,6},{5,7},{6,4},{7,5},{8,10},{9,11},{10,... | collective-permute-start | bytes 7102472 | tf_op jit(solution)/shard_map/ppermute | solution.py:296
  447.3 44.8 %collective-permute-start.47 = (bf16[272,3264]{1,0:T(8,128)(2,1)}, bf16[272,3264]{1,0:T(8,128)(2,1)}, u32[]{:S(2)}, u32[]{:S(2)}) collective-permute-start(bf16[272,3264]{1,0:T(8,128)(2,1)} %pad_maximum_fusion.3.refs_1_), channel_id=1, source_target_pairs={{0,2},{1,3},{2,0},{3,1},{4,6},{5,7},{6,4},{7,5},{8,10},{9,11},{10,... | collective-permute-start | bytes 5326856 | tf_op jit(solution)/shard_map/ppermute | solution.py:296
  447.6 10.8 %collective-permute-start.48 = (bf16[136,1088]{1,0:T(8,128)(2,1)S(1)}, bf16[136,1088]{1,0:T(8,128)(2,1)S(1)}, u32[]{:S(2)}, u32[]{:S(2)}) collective-permute-start(bf16[136,1088]{1,0:T(8,128)(2,1)S(1)} %pad_maximum_fusion.13), channel_id=1, source_target_pairs={{0,1},{1,0},{2,3},{3,2},{4,5},{5,4},{6,7},{7,6},{8,9},{9,8},{10,11... | collective-permute-start | bytes 887816 | tf_op jit(solution)/shard_map/ppermute | solution.py:296
  458.6 18.7 %collective-permute-start.49 = (bf16[272,1088]{1,0:T(8,128)(2,1)S(1)}, bf16[272,1088]{1,0:T(8,128)(2,1)}, u32[]{:S(2)}, u32[]{:S(2)}) collective-permute-start(bf16[272,1088]{1,0:T(8,128)(2,1)S(1)} %pad_maximum_fusion.10.refs_1_), channel_id=1, source_target_pairs={{0,2},{1,3},{2,0},{3,1},{4,6},{5,7},{6,4},{7,5},{8,10},{9,11},{10,... | collective-permute-start | bytes 1775624 | tf_op jit(solution)/shard_map/ppermute | solution.py:296
  (64 other events, 248.1 us)
Sparse Core Ops, SparseCore 0:
  9.6 13.8 all-gather.3
  25.0 23.0 all-gather.5
  49.7 23.8 all-gather.7

commit v3 on v2

--- a/solution.py
+++ b/solution.py
@@ -1,3 +1,5 @@
+import functools
+
 import jax
 import jax.numpy as jnp
 from jax import lax
@@ -248,6 +250,10 @@
     return jnp.where(first, lower, upper), jnp.where(first, upper, lower)
 
 
+class State:
+    pass
+
+
 class Line:
     def __init__(self):
         self.standing = []
@@ -384,7 +390,7 @@
         + [pl.BlockSpec(block.shape, lambda i: (0, 0)) for block in blocks],
         out_specs=pl.BlockSpec((rows, sum(lanes[0])), lambda i: (i, 0)),
         out_shape=jax.ShapeDtypeStruct((2 * rows * len(groups), sum(lanes[0])), single),
-        compiler_params=pltpu.CompilerParams(vmem_limit_bytes=40 * 2**20),
+        compiler_params=pltpu.CompilerParams(vmem_limit_bytes=56 * 2**20),
         cost_estimate=NO_COST,
         name="assemble",
     )(lows, *blocks)
@@ -442,10 +448,10 @@
 def grad_pre_of(full_down, cotangent, pre_active):
     width, ff = full_down.shape
     length = cotangent.shape[1]
-    tile = 256
+    tile = 640
     return pl.pallas_call(
         grad_pre_kernel,
-        grid=(ff // tile,),
+        grid=(-(-ff // tile),),
         in_specs=[
             pl.BlockSpec((width, tile), lambda i: (0, i)),
             pl.BlockSpec((width, length), lambda i: (0, 0)),
@@ -459,7 +465,7 @@
             jax.ShapeDtypeStruct((ff, length), bfloat),
             jax.ShapeDtypeStruct((ff, 1), single),
         ],
-        compiler_params=pltpu.CompilerParams(vmem_limit_bytes=24 * 2**20),
+        compiler_params=pltpu.CompilerParams(vmem_limit_bytes=56 * 2**20),
         cost_estimate=NO_COST,
         name="grad_pre",
     )(full_down, cotangent, pre_active)
@@ -527,39 +533,48 @@
         ]
         + [jax.ShapeDtypeStruct((width, 1), single)] * 3,
         scratch_shapes=[pltpu.VMEM((width, length), single)],
-        compiler_params=pltpu.CompilerParams(vmem_limit_bytes=40 * 2**20),
+        compiler_params=pltpu.CompilerParams(vmem_limit_bytes=56 * 2**20),
         cost_estimate=NO_COST,
         name="grad_middle",
     )(full_up, grad_pre, normal, scale, gain, cotangent)
 
 
+NAMES = (
+    "gact", "DAs", "DAk", "UAs", "gn2", "gheads", "DA", "abackA", "UAk", "UBs", "abackB",
+    "joinA", "OAs", "UBk", "joinB", "UB", "OAk", "gproj", "OA", "gn1", "UA", "QBs", "QAs",
+    "QBk", "QB", "QAk", "QA", "smalls", "S", "asmD", "asmO", "out", "asmU", "asmQ",
+)
+
 ORDER = (
-    "out", "Dsend", "Dkeep", "gact", "gn2", "DA", "Usend", "Ukeep", "DA", "gheads", "Osend",
-    "Okeep", "abackA", "DA", "OA", "abackB", "UA", "OA", "DA", "joinA", "joinB", "gproj",
-    "OA", "gn1", "UA", "DA", "OA", "Qsend", "Qkeep", "OA", "smalls", "S", "UA", "S", "DA",
-    "QA", "S", "OA", "S", "UA", "S", "OA", "QA", "DA", "UA", "OA", "QA", "UA", "DA", "QA",
-    "UA", "QA", "QA", "UA", "QA", "QA",
+    0, 1, 2, 3, 4, 5, 6, 7, 8, 6, 9, 10, 11, 6, 12, 13, 14, 15, 16, 17, 6, 18, 19, 15, 18,
+    20, 6, 21, 22, 15, 20, 18, 23, 6, 20, 24, 15, 18, 25, 26, 24, 6, 20, 26, 15, 27, 18, 24,
+    20, 26, 28, 18, 15, 20, 24, 26, 29, 18, 28, 15, 24, 28, 26, 30, 24, 20, 26, 28, 24, 28,
+    26, 31, 32, 33,
 )
 
 ROUTES = {
     "DA": ((0, 1), (1, 0), (2, 2), (3, 3)),
-    "UA": ((1, 0), (0, 1), (2, 2), (3, 3)),
+    "UA": ((2, 2), (0, 1), (1, 0), (3, 3)),
+    "UB": ((0, 1), (1, 2), (2, 0), (3, 3)),
     "OA": ((1, 0), (0, 1), (2, 2), (3, 3)),
     "QA": ((1, 0), (0, 1), (2, 2), (3, 3)),
+    "QB": ((0, 1), (1, 0), (2, 2), (3, 3)),
 }
 
 CUTS = {
     "DA": ((0, 1088), (0, 2176)),
-    "UA": ((0, 544), (0, 4352)),
+    "UA": ((0, 544), (0, 2176)),
+    "UB": ((0, 544), (2176, 4352)),
     "OA": ((0, 544), (0, 1088)),
-    "QA": ((0, 544), (0, 3264)),
+    "QA": ((0, 544), (0, 1664)),
+    "QB": ((0, 544), (1664, 3264)),
 }
 
 LAYOUTS = {
     "D": [['DA']],
-    "U": [['UA']],
+    "U": [['UA', 'UB']],
     "O": [['OA']],
-    "Q": [['QA']],
+    "Q": [['QA', 'QB']],
 }
 
 
@@ -643,7 +658,6 @@
     col_up = ordered(bias_up, other_up_bias, 0).astype(single)[:, None]
 
     grad_rows = cotangent[0].T
-    other_grad_rows = swapped(grad_rows)
     width = grad_rows.shape[0]
 
     rows = tokens[0].T.astype(single)
@@ -654,11 +668,12 @@
     col_qkv = jnp.concatenate([col_query, jnp.zeros_like(col_query), col_value], axis=0)
     qkv = (project + col_qkv).astype(bfloat)
     early_kv = lax.ppermute(qkv[width:, SKIP:], "shard", [(0, 1)])
+
+    qkv, early_kv, early_docs, grad_rows, normed_one_theirs = lax.optimization_barrier(
+        (qkv, early_kv, early_docs, grad_rows, normed_one_theirs)
+    )
+    other_grad_rows = swapped(grad_rows)
     normed_one_arrived = swapped(normed_one_theirs)
-
-    qkv, early_kv, early_docs, normed_one_arrived, other_grad_rows = lax.optimization_barrier(
-        (qkv, early_kv, early_docs, normed_one_arrived, other_grad_rows)
-    )
     heads, lse = attend(flag, docs, early_docs, qkv, early_kv)
     heads_mine, heads_theirs = halves(heads, at)
     heads_arrived = swapped(heads_theirs)
@@ -666,117 +681,108 @@
     normal_two, scale_two = normalize(middle)
     normed_two = (normal_two * col_gain_two + col_shift_two).astype(bfloat)
     normed_two_mine, normed_two_theirs = halves(normed_two, at)
-    normed_two_arrived = swapped(normed_two_theirs)
-    normed_two, heads_arrived = lax.optimization_barrier((normed_two, heads_arrived))
+    normed_two, heads_arrived, other_grad_rows, normed_one_arrived = lax.optimization_barrier(
+        (normed_two, heads_arrived, other_grad_rows, normed_one_arrived)
+    )
     pre_active = dot(full_up, normed_two, 0, 0) + col_up
     active = tanh_gelu(pre_active).astype(bfloat)
     active_mine, active_theirs = halves(active, at)
+    active, active_mine, active_theirs, normed_two_theirs, pre_active, grad_rows = (
+        lax.optimization_barrier(
+            (active, active_mine, active_theirs, normed_two_theirs, pre_active, grad_rows)
+        )
+    )
     active_arrived = swapped(active_theirs)
+    normed_two_arrived = swapped(normed_two_theirs)
     line = Line()
     sums = {name: Sum(line, order) for name, order in ROUTES.items()}
     sums["S"] = SmallSum(line)
-    s = {}
+    s = State()
     half = width // 2
     ff = pre_active.shape[0]
 
     def stage_out():
         active_now, middle_now = line.enter(active, middle)
         out = (middle_now + dot(full_down, active_now, 1, 0) + col_down).astype(bfloat)
-        line.leave(s, output=out)
-
-    def send_matrix(matrix, pairs):
-        names = [name for row in LAYOUTS[matrix] for name in row]
-        sent = []
-        for name in names:
-            rows, lanes = [slice(*at) for at in CUTS[name]]
-            sent.append(
-                sums[name].send([(former[rows], latter[lanes]) for former, latter in pairs])
-            )
-        formers, latters = zip(*pairs)
-        sent = line.leave(
-            s, sent, **{matrix + str(i): one for i, one in enumerate(formers + latters)}
-        )
-        for name, value in zip(names, sent):
-            if not sums[name].plain:
-                sums[name].pass_on(value, sums[name].order[0])
-
-    def keep(matrix):
-        names = [name for row in LAYOUTS[matrix] for name in row]
-        if sums[names[0]].plain:
-            return
-        count = 2
-        values = line.enter(*[s[matrix + str(i)] for i in range(2 * count)])
-        for name in names:
-            rows, lanes = [slice(*at) for at in CUTS[name]]
-            pairs = [(a[rows], b[lanes]) for a, b in zip(values[:count], values[count:])]
+        line.leave(s.__dict__, output=out)
+
+    operands = {
+        "D": ("cot", "cot_other", "active", "active_other"),
+        "U": ("normed_two", "normed_two_other", "grad_pre", "grad_pre_other"),
+        "O": ("heads", "heads_other", "grad_branch", "grad_branch_other"),
+        "Q": ("normed_one", "normed_one_other", "grad_project", "grad_project_other"),
+    }
+    s.__dict__.update(cot=grad_rows, cot_other=other_grad_rows, active=active_mine)
+    s.__dict__.update(active_other=active_arrived, normed_two=normed_two_mine)
+    s.__dict__.update(normed_two_other=normed_two_arrived, heads=heads_mine, heads_other=heads_arrived)
+    s.__dict__.update(normed_one=normed_one_mine, normed_one_other=normed_one_arrived)
+
+    def pairs_of(name):
+        keys = operands[name[0]]
+        values = line.enter(*[s.__dict__[key] for key in keys])
+        rows, lanes = [slice(*at) for at in CUTS[name]]
+        pairs = [(values[i][rows], values[i + 2][lanes]) for i in range(2)]
+        return dict(zip(keys, values)), pairs
+
+    def send(name):
+        values, pairs = pairs_of(name)
+        (sent,) = line.leave(s.__dict__, [sums[name].send(pairs)], **values)
+        if not sums[name].plain:
+            sums[name].pass_on(sent, sums[name].order[0])
+
+    def keep(name):
+        if not sums[name].plain:
+            _, pairs = pairs_of(name)
             line.leave(sums[name].__dict__, total=sums[name].keep(pairs))
-
-    def stage_down_send():
-        mine, arrived, s["normed_two_arrived"], own, other = line.enter(
-            active_mine, active_arrived, normed_two_arrived, grad_rows, other_grad_rows
-        )
-        send_matrix("D", [(own, mine), (other, arrived)])
 
     def stage_grad_active():
         (cot,) = line.enter(grad_rows)
         grad_pre, bias_sum = grad_pre_of(full_down, cot, pre_active)
-        line.leave(s, grad_pre=grad_pre, grad_bias_up=bias_sum)
-        s["grad_pre_other"] = swapped(s["grad_pre"])
+        line.leave(s.__dict__, grad_pre=grad_pre, grad_bias_up=bias_sum)
+        s.grad_pre_other = swapped(s.grad_pre)
 
     def stage_normed_two():
-        (grad_pre,) = line.enter(s["grad_pre"])
+        grad_pre, s.normed_two_other = line.enter(s.grad_pre, s.normed_two_other)
         names = "grad_middle", "grad_branch", "grad_gain_two", "grad_shift_two", "grad_bias_out"
         results = grad_middle_of(
             full_up, grad_pre, normal_two, scale_two, col_gain_two, grad_rows
         )
-        line.leave(s, **dict(zip(names, results)))
-        s["grad_branch_other"] = swapped(s["grad_branch"])
-
-    def stage_up_send():
-        mine, arrived, own, other = line.enter(
-            normed_two_mine, s["normed_two_arrived"], s["grad_pre"], s["grad_pre_other"]
-        )
-        send_matrix("U", [(mine, own), (arrived, other)])
-
-    def stage_out_send():
-        mine, arrived, own, other = line.enter(
-            heads_mine, heads_arrived, s["grad_branch"], s["grad_branch_other"]
-        )
-        send_matrix("O", [(mine, own), (arrived, other)])
+        line.leave(s.__dict__, **dict(zip(names, results)))
+        s.grad_branch_other = swapped(s.grad_branch)
 
     def stage_grad_heads():
-        grad_branch, s["grad_branch_other"] = line.enter(s["grad_branch"], s["grad_branch_other"])
-        line.leave(s, grad_heads=dot(full_out, grad_branch, 1, 0).astype(bfloat))
+        grad_branch, s.grad_branch_other = line.enter(s.grad_branch, s.grad_branch_other)
+        line.leave(s.__dict__, grad_heads=dot(full_out, grad_branch, 1, 0).astype(bfloat))
 
     heads_count = width // HDIM
     ranges = {"A": (0, heads_count // 2), "B": (heads_count // 2, heads_count)}
 
     def stage_attend_back(name):
-        (grad_heads,) = line.enter(s["grad_heads"])
+        (grad_heads,) = line.enter(s.grad_heads)
         results = attend_back(
             flag, docs, early_docs, qkv, early_kv, grad_heads, heads, lse, *ranges[name]
         )
         back = jnp.concatenate(results[3:], axis=0)
         kept = {name + str(i): one for i, one in enumerate(results[:3])}
-        (back,) = line.leave(s, [back], **kept)
-        s["back" + name] = lax.ppermute(back, "shard", [(1, 0)])
+        (back,) = line.leave(s.__dict__, [back], **kept)
+        s.__dict__["back" + name] = lax.ppermute(back, "shard", [(1, 0)])
 
     def joined(own, back):
         return (own + jnp.pad(back.astype(single), ((0, 0), (SKIP, 0)))).astype(bfloat)
 
     def stage_join(name):
-        query, key, value, back = line.enter(*[s[name + str(i)] for i in range(3)], s["back" + name])
+        query, key, value, back = line.enter(*[s.__dict__[name + str(i)] for i in range(3)], s.__dict__["back" + name])
         middle_row = back.shape[0] // 2
         key, value = joined(key, back[:middle_row]), joined(value, back[middle_row:])
-        line.leave(s, **{name + "q": query, name + "k": key, name + "v": value})
+        line.leave(s.__dict__, **{name + "q": query, name + "k": key, name + "v": value})
 
     def stage_project():
-        pieces = line.enter(*[s[name + part] for part in "qkv" for name in "AB"])
-        line.leave(s, grad_project=jnp.concatenate(pieces, axis=0))
-        s["grad_project_other"] = swapped(s["grad_project"])
+        pieces = line.enter(*[s.__dict__[name + part] for part in "qkv" for name in "AB"])
+        line.leave(s.__dict__, grad_project=jnp.concatenate(pieces, axis=0))
+        s.grad_project_other = swapped(s.grad_project)
 
     def stage_normed_one():
-        (grad_project,) = line.enter(s["grad_project"])
+        (grad_project,) = line.enter(s.grad_project)
         grad_normed_one = ordered(
             dot(w_qkv, grad_project, 1, 0), dot(other_qkv, grad_project, 1, 0), 0
         )
@@ -784,25 +790,25 @@
             grad_normed_one, normal_one, scale_one, col_gain_one
         )
         line.leave(
-            s,
-            input_grad=(s["grad_middle"] + part_one).astype(bfloat),
+            s.__dict__,
+            input_grad=(s.grad_middle + part_one).astype(bfloat),
             grad_gain_one=gain_sum,
             grad_shift_one=shift_sum,
         )
 
     def stage_small():
         bias_out, gain_two_sum, shift_two_sum, bias_up_sum, cot, grad_project = line.enter(
-            s["grad_bias_out"],
-            s["grad_gain_two"],
-            s["grad_shift_two"],
-            s["grad_bias_up"],
+            s.grad_bias_out,
+            s.grad_gain_two,
+            s.grad_shift_two,
+            s.grad_bias_up,
             grad_rows,
-            s["grad_project"],
+            s.grad_project,
         )
         small = jnp.stack(
             [
-                s["grad_gain_one"],
-                s["grad_shift_one"],
+                s.grad_gain_one,
+                s.grad_shift_one,
                 jnp.sum(grad_project[:width].astype(single), axis=1),
                 jnp.sum(grad_project[2 * width :].astype(single), axis=1),
                 bias_out[:, 0],
@@ -817,22 +823,15 @@
         upper = jnp.concatenate([small[:, half:], up_parts[1]], axis=0)
         sums["S"].send(jnp.where(first, lower, upper), jnp.where(first, upper, lower))
 
-    def stage_qkv_send():
-        mine, arrived, own, other = line.enter(
-            normed_one_mine, normed_one_arrived, s["grad_project"], s["grad_project_other"]
-        )
-        send_matrix("Q", [(mine, own), (arrived, other)])
+    grads = {}
+
+    def assemble(matrix):
+        grads[matrix] = assembled(line, [[sums[name] for name in row] for row in LAYOUTS[matrix]])
 
     stages = {
         "out": stage_out,
-        "Dsend": stage_down_send,
-        "Dkeep": lambda: keep("D"),
         "gact": stage_grad_active,
         "gn2": stage_normed_two,
-        "Usend": stage_up_send,
-        "Ukeep": lambda: keep("U"),
-        "Osend": stage_out_send,
-        "Okeep": lambda: keep("O"),
         "gheads": stage_grad_heads,
         "abackA": lambda: stage_attend_back("A"),
         "abackB": lambda: stage_attend_back("B"),
@@ -841,37 +840,32 @@
         "gproj": stage_project,
         "gn1": stage_normed_one,
         "smalls": stage_small,
-        "Qsend": stage_qkv_send,
-        "Qkeep": lambda: keep("Q"),
     }
-    grads = {}
-
-    def gather():
-        for name, layout in LAYOUTS.items():
-            rows_of = [[sums[one] for one in row] for row in layout]
-            sent = not waiting or not rows_of[0][0].plain
-            if name not in grads and sent and all(
-                one.finished() for row in rows_of for one in row
-            ):
-                grads[name] = assembled(line, rows_of)
-
-    waiting = set(stages)
-    for name in ORDER:
+    for name in CUTS:
+        stages[name + "s"] = functools.partial(send, name)
+        stages[name + "k"] = functools.partial(keep, name)
+    last = []
+    for name in [NAMES[i] for i in ORDER]:
         if name in stages:
             stages[name]()
-            waiting.remove(name)
+        elif name in sums:
+            sums[name].step()
         else:
-            sums[name].step()
-        if name not in stages:
-            gather()
-    while len(grads) < len(LAYOUTS) or not sums["S"].finished():
-        for one in sums.values():
-            one.step()
-        gather()
+            last.append(name[-1])
+            for one in sums.values():
+                while len(last) == len(LAYOUTS) and not one.finished():
+                    one.step()
+            if all(sums[one].finished() for row in LAYOUTS[last[-1]] for one in row):
+                assemble(last[-1])
+    for matrix in LAYOUTS:
+        if matrix not in grads:
+            assemble(matrix)
+    while not sums["S"].finished():
+        sums["S"].step()
     small = sums["S"].total
     return (
-        s["output"].T[None],
-        s["input_grad"].T[None],
+        s.output.T[None],
+        s.input_grad.T[None],
         grads["Q"],
         grads["O"],
         grads["U"],

time: 513 us -> 462 us (0.901)
  waiting for transfers between devices: 193 us -> 101 us
  starting transfers between devices: 56.4 us -> 73.7 us
  other arithmetic: 33.2 us -> 47.5 us
    ppermute x32 -> x48, waiting for transfers between devices: 167 us -> 77.4 us  [pass_on(): self.arrived = lax.ppermute(block, ('shard', 'replica'), route)]
    ppermute x32 -> x48, starting transfers between devices: 41.4 us -> 61.6 us  [pass_on(): self.arrived = lax.ppermute(block, ('shard', 'replica'), route)]
    ppermute x4, waiting for transfers between devices: 19.6 us -> 4.53 us  [step(): self.arrived = lax.ppermute(self.total, 'replica', route)]
    ppermute x12, waiting for transfers between devices: 4.07 us -> 17.8 us  [swapped(): return lax.ppermute(block, 'shard', [(0, 1), (1, 0)])]
    dot_general x24 -> x32, matrix products: 89.6 us -> 94.2 us  [dot(): lax.dot_general(former, latter, (((former_axis,), (latter_axis,)), ((), (...]
    unnamed x119 -> x125, local copies, waits for them, and re-layouts: 14.1 us -> 12.3 us
  transfers between devices with their start and end apart: 55 -> 71, of which waited for: 23 -> 19; matrix products, arithmetic and copies ran while one was open for 25% -> 32% of each run, Pallas kernels for 17% -> 17%
where the time goes in v3:
time: 462 us; the launch traced here: 453 us
  waiting for transfers between devices  101 us (22%)
  Pallas kernels  97.6 us (21%)
  matrix products  94.2 us (20%)
  starting transfers between devices  73.7 us (16%)
  other arithmetic  47.5 us (10%)
  local copies, waits for them, and re-layouts  23.2 us (5%)
  between operations  16.1 us (3%)
    dot_general x32, matrix products, dot(): lax.dot_general(former, latter, (((former_axis,), (latter_axis,)), ((), (...  94.2 us
    ppermute x48, waiting for transfers between devices, pass_on(): self.arrived = lax.ppermute(block, ('shard', 'replica'), route)  77.4 us
    ppermute x48, starting transfers between devices, pass_on(): self.arrived = lax.ppermute(block, ('shard', 'replica'), route)  61.6 us
    pallas_call x2, Pallas kernels, attend_back(): pl.pallas_call(attend_back_kernel, grid=(end - begin,), in_specs=inputs +...  24.2 us
    pallas_call x1, Pallas kernels, attend(): pl.pallas_call(attend_kernel, grid=(heads,), in_specs=inputs, out_specs=[...  21.5 us
    pallas_call x4, Pallas kernels, assembled(): pl.pallas_call(lambda *refs: assemble_kernel(lanes, *refs), grid=(2 * len...  21.5 us
    ppermute x12, waiting for transfers between devices, swapped(): return lax.ppermute(block, 'shard', [(0, 1), (1, 0)])  17.8 us
    pallas_call x1, Pallas kernels, grad_pre_of(): pl.pallas_call(grad_pre_kernel, grid=(-(-ff // tile),), in_specs=[pl.Bloc...  16.2 us
  transfers between devices with their start and end apart: 71, of which 19 were waited for; matrix products, arithmetic and copies ran while one was open for 32% of the time, Pallas kernels for 17%

profile of v3, /device:TPU:0, one launch (start us, length us, event | category | flops | bytes accessed | tf_op | source)
XLA Modules:
  0.0 453.4 jit_solution(12823607737751482606)
XLA Ops:
  11.5 3.7 collective-permute-done
  15.5 3.3 fusion.166
  21.4 5.0 %fusion.169 = f32[512,3264]{0,1:T(8,128)S(1)} fusion(bf16[544,512]{1,0:T(8,128)(2,1)S(1)} %get-tuple-element.665, bf16[544,3264]{1,0:T(8,128)(2,1)} %param.19), kind=kOutput, calls=%fused_computation.365 | convolution fusion | flops 1818230784 | bytes 10792960 | tf_op jit(solution)/shard_map/dot_general | solution.py:19
  26.5 5.0 %fusion.8.q_ref.k_ref.v_ref = bf16[3264,512]{1,0:T(8,128)(2,1)S(1)} fusion(f32[512,3264]{0,1:T(8,128)S(1)} %fusion.169, bf16[544,512]{1,0:T(8,128)(2,1)} %get-tuple-element.415, bf16[544,3264]{1,0:T(8,128)(2,1)} %collective-permute-done.1, f32[3264]{0:T(1024)S(1)} %reduce.6), kind=kOutput, calls=%fused_computation.11 | convolution fusion | flops 1823244288 | bytes 14148352 | tf_op jit(solution)/shard_map/dot_general | solution.py:19
  32.9 3.3 collective-permute-start.2
  36.2 2.6 collective-permute-start.3
  42.6 21.5 %attend.1 = (bf16[1088,512]{1,0:T(8,128)(2,1)S(1)}, f32[17,1,512]{2,1,0:T(1,128)S(1)}) custom-call(s32[1]{0:T(128)} %bitcast.3.flag_ref, s32[1,512]{1,0:T(1,128)S(1)} %copy-done.11, s32[512,1]{1,0:T(8,128)S(1)} %copy-done.5, s32[512,1]{1,0:T(8,128)S(1)} %copy-done.8, bf16[3264,512]{1,0:T(8,128)(2,1)S(1)} %fusion.8.q_ref.k_ref.v_ref, ...), custom_call_target="tpu_custom_call" | custom-call | flops 12000000000 | bytes 6000000 | tf_op jit(solution)/shard_map/attend/pallas_call | solution.py:171
  66.7 4.2 fusion.168
  75.2 13.3 %fusion.7 = (bf16[4352,512]{1,0:T(8,128)(2,1)S(1)}, f32[4352,512]{1,0:T(8,128)}) fusion(f32[4352]{0:T(1024)S(1)} %maximum_convert_fusion.1, bf16[1088,512]{1,0:T(8,128)(2,1)} %copy-done.24, bf16[1088,4352]{1,0:T(8,128)(2,1)} %all-gather.6.cloned.1.call-done.w_ref), kind=kOutput, calls=%fused_computation.8 | convolution fusion | flops 4870897664 | bytes 23970816 | tf_op jit(solution)/shard_map/dot_general | solution.py:19
  91.9 16.2 %grad_pre.1 = (bf16[4352,512]{1,0:T(8,128)(2,1)}, f32[4352,1]{1,0:T(8,128)}) custom-call(bf16[1088,4352]{1,0:T(8,128)(2,1)} %all-gather.8.cloned.1.call-done.w_ref, bf16[1088,512]{1,0:T(8,128)(2,1)} %bitcast.8.cot_ref, f32[4352,512]{1,0:T(8,128)} %get-tuple-element.422.pre_ref), custom_call_target="tpu_custom_call" | custom-call | tf_op jit(solution)/shard_map/grad_pre/pallas_call | solution.py:452
  109.1 11.0 %collective-permute-done.8 = bf16[2176,512]{1,0:T(8,128)(2,1)} collective-permute-done((bf16[2176,512]{1,0:T(8,128)(2,1)}, bf16[2176,512]{1,0:T(8,128)(2,1)}, u32[]{:S(2)}, u32[]{:S(2)}) %collective-permute-start.8) | collective-permute-done | bytes 2228256 | tf_op jit(solution)/shard_map/ppermute | solution.py:243
  120.1 3.6 fusion.69
  123.8 4.2 fusion.9
  127.9 2.7 collective-permute-start.9
  130.6 2.9 fusion.65
  133.5 5.7 %convolution_add_fusion = f32[544,2176]{1,0:T(8,128)} fusion(f32[544,2176]{1,0:T(8,128)S(1)} %fusion.65, bf16[2176,512]{1,0:T(8,128)(2,1)} %collective-permute-done.8, bf16[1088,512]{1,0:T(8,128)(2,1)} %collective-permute-done.5, pred[]{:T(512)} %eq.17), kind=kOutput, calls=%fused_computation.12 | convolution fusion | flops 1213616128 | bytes 12812289 | tf_op jit(solution)/shard_map/dot_general | solution.py:19
  139.2 2.7 fusion.46
  143.8 14.2 %grad_middle.1 = (f32[1088,512]{1,0:T(8,128)}, bf16[1088,512]{1,0:T(8,128)(2,1)}, f32[1088,1]{1,0:T(8,128)}, f32[1088,1]{1,0:T(8,128)}, f32[1088,1]{1,0:T(8,128)}) custom-call(bf16[1088,4352]{1,0:T(8,128)(2,1)} %all-gather.6.cloned.1.call-done.w_ref, bf16[4352,512]{1,0:T(8,128)(2,1)} %get-tuple-element.540.grad_ref, ...), custom_call_target="tpu_custom_call" | custom-call | tf_op jit(solution)/shard_map/grad_middle/pallas_call | solution.py:518
  158.1 3.0 collective-permute-done.12
  161.1 4.6 %fusion.17.g_ref = bf16[1088,512]{1,0:T(8,128)(2,1)} fusion(bf16[1088,1088]{1,0:T(8,128)(2,1)} %all-gather.4.cloned.1.call-done, bf16[1088,512]{1,0:T(8,128)(2,1)} %get-tuple-element.564), kind=kOutput, calls=%fused_computation.38 | convolution fusion | flops 1212710912 | bytes 4595712 | tf_op jit(solution)/shard_map/dot_general | solution.py:19
  165.7 3.5 convert_add_fusion
  180.8 11.6 %attend_back.2 = (bf16[512,512]{1,0:T(8,128)(2,1)S(1)}, f32[512,512]{1,0:T(8,128)S(1)}, f32[512,512]{1,0:T(8,128)S(1)}, bf16[512,384]{1,0:T(8,128)(2,1)S(1)}, bf16[512,384]{1,0:T(8,128)(2,1)S(1)}) custom-call(s32[1]{0:T(128)} %bitcast.3.flag_ref, s32[1,512]{1,0:T(1,128)S(1)} %copy-done.11, s32[512,1]{1,0:T(8,128)S(1)} %copy-done.6, s32[512,1]{1,0:T(8,128)S(1)} %copy-done.9, ...), custom_call_target="tpu_custom_call" | custom-call | tf_op jit(solution)/shard_map/attend_back/pallas_call | solution.py:206
  192.5 2.5 fusion.44
  195.1 2.6 convolution_add_fusion.4
  202.3 2.7 fusion.11
  205.0 12.6 %attend_back.3 = (bf16[576,512]{1,0:T(8,128)(2,1)S(1)}, f32[576,512]{1,0:T(8,128)S(1)}, f32[576,512]{1,0:T(8,128)S(1)}, bf16[576,384]{1,0:T(8,128)(2,1)S(1)}, bf16[576,384]{1,0:T(8,128)(2,1)S(1)}) custom-call(s32[1]{0:T(128)} %bitcast.3.flag_ref, s32[1,512]{1,0:T(1,128)S(1)} %copy-done.11, s32[512,1]{1,0:T(8,128)S(1)} %copy-done.7, s32[512,1]{1,0:T(8,128)S(1)} %copy-done.10, ...), custom_call_target="tpu_custom_call" | custom-call | tf_op jit(solution)/shard_map/attend_back/pallas_call | solution.py:206
  220.4 2.6 collective-permute-start.16
  230.7 5.5 %collective-permute-done.17 = bf16[272,2176]{1,0:T(8,128)(2,1)S(1)} collective-permute-done((bf16[272,2176]{1,0:T(8,128)(2,1)S(1)}, bf16[272,2176]{1,0:T(8,128)(2,1)S(1)}, u32[]{:S(2)}, u32[]{:S(2)}) %collective-permute-start.17) | collective-permute-done | bytes 1183776 | tf_op jit(solution)/shard_map/ppermute | solution.py:302
  239.7 4.9 %collective-permute-start.20 = (bf16[72,2176]{1,0:T(8,128)(2,1)S(1)}, bf16[72,2176]{1,0:T(8,128)(2,1)S(1)}, u32[]{:S(2)}, u32[]{:S(2)}) collective-permute-start(bf16[72,2176]{1,0:T(8,128)(2,1)S(1)} %add_convert_fusion.6), channel_id=1, source_target_pairs={{0,8},{1,9},{2,10},{3,11},{4,12},{5,13},{6,14},{7,15},{8,0},{9,1},... | collective-permute-start | bytes 940040 | tf_op jit(solution)/shard_map/ppermute | solution.py:302
  248.5 4.1 select_bitcast_fusion.1
  269.4 3.6 collective-permute-done.28
  280.9 7.7 %collective-permute-done.32 = bf16[136,2176]{1,0:T(8,128)(2,1)S(1)} collective-permute-done((bf16[136,2176]{1,0:T(8,128)(2,1)S(1)}, bf16[136,2176]{1,0:T(8,128)(2,1)S(1)}, u32[]{:S(2)}, u32[]{:S(2)}) %collective-permute-start.32) | collective-permute-done | bytes 591904 | tf_op jit(solution)/shard_map/ppermute | solution.py:302
  288.7 11.0 %collective-permute-done.33 = bf16[72,2176]{1,0:T(8,128)(2,1)S(1)} collective-permute-done((bf16[72,2176]{1,0:T(8,128)(2,1)S(1)}, bf16[72,2176]{1,0:T(8,128)(2,1)S(1)}, u32[]{:S(2)}, u32[]{:S(2)}) %collective-permute-start.33) | collective-permute-done | bytes 313376 | tf_op jit(solution)/shard_map/ppermute | solution.py:302
  311.1 11.9 %collective-permute-done.35 = bf16[136,1600]{1,0:T(8,128)(2,1)S(1)} collective-permute-done((bf16[136,1600]{1,0:T(8,128)(2,1)S(1)}, bf16[136,1600]{1,0:T(8,128)(2,1)S(1)}, u32[]{:S(2)}, u32[]{:S(2)}) %collective-permute-start.35) | collective-permute-done | bytes 435232 | tf_op jit(solution)/shard_map/ppermute | solution.py:302
  328.6 3.4 collective-permute-start.40
  349.8 4.8 %collective-permute-done.38 = bf16[72,1664]{1,0:T(8,128)(2,1)S(1)} collective-permute-done((bf16[72,1664]{1,0:T(8,128)(2,1)S(1)}, bf16[72,1664]{1,0:T(8,128)(2,1)S(1)}, u32[]{:S(2)}, u32[]{:S(2)}) %collective-permute-start.38) | collective-permute-done | bytes 239648 | tf_op jit(solution)/shard_map/ppermute | solution.py:302
  354.7 3.2 collective-permute-start.45
  360.3 4.4 collective-permute-done.46
  365.8 6.9 %collective-permute-done.43 = bf16[40,1664]{1,0:T(8,128)(2,1)S(1)} collective-permute-done((bf16[40,1664]{1,0:T(8,128)(2,1)S(1)}, bf16[40,1664]{1,0:T(8,128)(2,1)S(1)}, u32[]{:S(2)}, u32[]{:S(2)}) %collective-permute-start.43) | collective-permute-done | bytes 133152 | tf_op jit(solution)/shard_map/ppermute | solution.py:302
  373.5 6.5 %collective-permute-done.51 = bf16[136,2176]{1,0:T(8,128)(2,1)S(1)} collective-permute-done((bf16[136,2176]{1,0:T(8,128)(2,1)S(1)}, bf16[136,2176]{1,0:T(8,128)(2,1)S(1)}, u32[]{:S(2)}, u32[]{:S(2)}) %collective-permute-start.51) | collective-permute-done | bytes 591904 | tf_op jit(solution)/shard_map/ppermute | solution.py:302
  380.9 4.1 collective-permute-start.49
  391.9 10.1 %collective-permute-done.57.refs_2_ = bf16[272,1088]{1,0:T(8,128)(2,1)S(1)} collective-permute-done((bf16[272,1088]{1,0:T(8,128)(2,1)S(1)}, bf16[272,1088]{1,0:T(8,128)(2,1)S(1)}, u32[]{:S(2)}, u32[]{:S(2)}) %collective-permute-start.57) | collective-permute-done | bytes 591904 | tf_op jit(solution)/shard_map/ppermute | solution.py:302
  402.9 3.1 assemble.5
  406.0 6.6 %assemble.7 = f32[1088,2176]{1,0:T(8,128)} custom-call(s32[1]{0:T(128)S(6)} %convert_element_type.330.refs_0_, bf16[544,2176]{1,0:T(8,128)(2,1)} %pad_maximum_fusion.refs_1_, bf16[544,2176]{1,0:T(8,128)(2,1)} %collective-permute-done.50.refs_2_), custom_call_target="tpu_custom_call" | custom-call | tf_op jit(solution)/shard_map/assemble/pallas_call | solution.py:386
  417.2 4.5 collective-permute-done.65
  425.5 7.8 %fusion.15 = bf16[1088,512]{1,0:T(8,128)(2,1)} fusion(f32[1088,512]{1,0:T(8,128)S(1)} %bitcast.140, bf16[1088,4352]{1,0:T(8,128)(2,1)S(1)} %bitcast.138, bf16[4352,512]{1,0:T(8,128)(2,1)} %copy-done.25, f32[1088]{0:T(1024)S(1)} %copy-done.42), kind=kOutput, calls=%fused_computation.27 | convolution fusion | flops 4850286592 | bytes 17273088 | tf_op jit(solution)/shard_map/dot_general | solution.py:19
  434.0 6.5 %assemble.6 = f32[544,4352]{1,0:T(8,128)} custom-call(s32[2]{0:T(128)} %add_convert_fusion.13.refs_0_, bf16[272,2176]{1,0:T(8,128)(2,1)} %copy-done.23, bf16[272,2176]{1,0:T(8,128)(2,1)} %collective-permute-done.60.refs_2_, bf16[272,2176]{1,0:T(8,128)(2,1)} %copy-done.22, bf16[272,2176]{1,0:T(8,128)(2,1)} %collective-permute-done.61.refs_4_), custom_call_target="tpu_custom_call" | custom-call | tf_op jit(solution)/shard_map/assemble/pallas_call | solution.py:386
  441.1 5.3 %assemble.4 = f32[544,3264]{1,0:T(8,128)} custom-call(s32[2]{0:T(128)} %add_convert_fusion.12.refs_0_, bf16[272,1664]{1,0:T(8,128)(2,1)} %pad_maximum_fusion.6.refs_1_, bf16[272,1664]{1,0:T(8,128)(2,1)} %collective-permute-done.66.refs_2_, bf16[272,1600]{1,0:T(8,128)(2,1)} %pad_maximum_fusion.5.refs_3_, bf16[272,1600]{1,0:T(8,128)(2,1)} %collective-permute-done.67.refs_4_), custom_call_target="tpu_custom_call" | custom-call | tf_op jit(solution)/shard_map/assemble/pallas_call | solution.py:386
  (450 shorter events, 140.4 us)
Async XLA Ops:
  7.2 59.5 %all-gather.4.cloned.1.call-start = ((), (), s32[]{:S(2)}) async-start(), calls=%async_computation | async-start | bytes 3760128 | tf_op jit(solution)/shard_map/all_gather | solution.py:638
  8.0 67.2 %all-gather.6.cloned.1.call-start = ((), (), s32[]{:S(2)}) async-start(), calls=%async_computation.1 | async-start | bytes 14204928 | tf_op jit(solution)/shard_map/all_gather | solution.py:639
  8.7 83.2 %all-gather.8.cloned.1.call-start = ((), (), s32[]{:S(2)}) async-start(), calls=%async_computation.2 | async-start | bytes 14204928 | tf_op jit(solution)/shard_map/all_gather | solution.py:640
  8.8 17.7 %collective-permute-start.1 = (bf16[544,3264]{1,0:T(8,128)(2,1)}, bf16[544,3264]{1,0:T(8,128)(2,1)}, u32[]{:S(2)}, u32[]{:S(2)}) collective-permute-start(bf16[544,3264]{1,0:T(8,128)(2,1)} %param.19), channel_id=1, source_target_pairs={{0,16},{16,0},{1,17},{17,1},{2,18},{18,2},{3,19},{19,3},{4,20},{20... | collective-permute-start | bytes 10653704 | tf_op jit(solution)/shard_map/ppermute | solution.py:243
  108.2 31.0 %collective-permute-start.11 = (bf16[4352,512]{1,0:T(8,128)(2,1)}, bf16[4352,512]{1,0:T(8,128)(2,1)}, u32[]{:S(2)}, u32[]{:S(2)}) collective-permute-start(bf16[4352,512]{1,0:T(8,128)(2,1)} %get-tuple-element.540.grad_ref), channel_id=1, source_target_pairs={{0,16},{16,0},{1,17},{17,1},{2,18},{18,2},{3,19},{19,3},{4,20},{20... | collective-permute-start | bytes 13369352 | tf_op jit(solution)/shard_map/ppermute | solution.py:243
  108.6 11.5 %collective-permute-start.8 = (bf16[2176,512]{1,0:T(8,128)(2,1)}, bf16[2176,512]{1,0:T(8,128)(2,1)}, u32[]{:S(2)}, u32[]{:S(2)}) collective-permute-start(bf16[2176,512]{1,0:T(8,128)(2,1)} %get-tuple-element.421), channel_id=1, source_target_pairs={{0,16},{16,0},{1,17},{17,1},{2,18},{18,2},{3,19},{19,3},{4,20},{20... | collective-permute-start | bytes 6684680 | tf_op jit(solution)/shard_map/ppermute | solution.py:243
  108.8 30.4 %collective-permute-start.10 = (bf16[544,512]{1,0:T(8,128)(2,1)}, bf16[544,512]{1,0:T(8,128)(2,1)S(1)}, u32[]{:S(2)}, u32[]{:S(2)}) collective-permute-start(bf16[544,512]{1,0:T(8,128)(2,1)} %get-tuple-element.430), channel_id=1, source_target_pairs={{0,16},{16,0},{1,17},{17,1},{2,18},{18,2},{3,19},{19,3},{4,20},{20... | collective-permute-start | bytes 1671176 | tf_op jit(solution)/shard_map/ppermute | solution.py:243
  127.9 37.8 %collective-permute-start.9 = (bf16[544,2176]{1,0:T(8,128)(2,1)}, bf16[544,2176]{1,0:T(8,128)(2,1)}, u32[]{:S(2)}, u32[]{:S(2)}) collective-permute-start(bf16[544,2176]{1,0:T(8,128)(2,1)} %fusion.9), channel_id=1, source_target_pairs={{0,1},{1,0},{2,3},{3,2},{4,5},{5,4},{6,7},{7,6},{8,9},{9,8},{10,11... | collective-permute-start | bytes 7102472 | tf_op jit(solution)/shard_map/ppermute | solution.py:302
  172.1 27.1 %collective-permute-start.13 = (bf16[272,2176]{1,0:T(8,128)(2,1)}, bf16[272,2176]{1,0:T(8,128)(2,1)}, u32[]{:S(2)}, u32[]{:S(2)}) collective-permute-start(bf16[272,2176]{1,0:T(8,128)(2,1)} %select_convert_fusion), channel_id=1, source_target_pairs={{0,2},{1,3},{2,0},{3,1},{4,6},{5,7},{6,4},{7,5},{8,10},{9,11},{10,... | collective-permute-start | bytes 3551240 | tf_op jit(solution)/shard_map/ppermute | solution.py:302
  174.8 83.1 %collective-permute-start.22 = (bf16[272,2176]{1,0:T(8,128)(2,1)}, bf16[272,2176]{1,0:T(8,128)(2,1)S(1)}, u32[]{:S(2)}, u32[]{:S(2)}) collective-permute-start(bf16[272,2176]{1,0:T(8,128)(2,1)} %fusion.10), channel_id=1, source_target_pairs={{0,4},{1,5},{2,6},{3,7},{4,0},{5,1},{6,2},{7,3},{8,12},{9,13},{10,... | collective-permute-start | bytes 3551240 | tf_op jit(solution)/shard_map/ppermute | solution.py:302
  197.7 20.0 %collective-permute-start.15 = (bf16[1024,384]{1,0:T(8,128)(2,1)S(1)}, bf16[1024,384]{1,0:T(8,128)(2,1)S(1)}, u32[]{:S(2)}, u32[]{:S(2)}) collective-permute-start(bf16[1024,384]{1,0:T(8,128)(2,1)S(1)} %pad_maximum_fusion.8), channel_id=1, source_target_pairs={{16,0},{17,1},{18,2},{19,3},{20,4},{21,5},{22,6},{23,7},{24,8},{25... | collective-permute-start | bytes 2359304 | tf_op jit(solution)/shard_map/ppermute | solution.py:768
  200.9 19.2 %collective-permute-start.14 = (bf16[136,2176]{1,0:T(8,128)(2,1)S(1)}, bf16[136,2176]{1,0:T(8,128)(2,1)S(1)}, u32[]{:S(2)}, u32[]{:S(2)}) collective-permute-start(bf16[136,2176]{1,0:T(8,128)(2,1)S(1)} %select_convert_fusion.3), channel_id=1, source_target_pairs={{0,4},{1,5},{2,6},{3,7},{4,0},{5,1},{6,2},{7,3},{8,12},{9,13},{10,... | collective-permute-start | bytes 1775624 | tf_op jit(solution)/shard_map/ppermute | solution.py:302
  218.1 18.1 %collective-permute-start.17 = (bf16[272,2176]{1,0:T(8,128)(2,1)S(1)}, bf16[272,2176]{1,0:T(8,128)(2,1)S(1)}, u32[]{:S(2)}, u32[]{:S(2)}) collective-permute-start(bf16[272,2176]{1,0:T(8,128)(2,1)S(1)} %fusion.11), channel_id=1, source_target_pairs={{0,1},{1,0},{2,3},{3,2},{4,5},{5,4},{6,7},{7,6},{8,9},{9,8},{10,11... | collective-permute-start | bytes 3551240 | tf_op jit(solution)/shard_map/ppermute | solution.py:302
  218.7 11.6 %collective-permute-start.18 = (bf16[1152,384]{1,0:T(8,128)(2,1)S(1)}, bf16[1152,384]{1,0:T(8,128)(2,1)S(1)}, u32[]{:S(2)}, u32[]{:S(2)}) collective-permute-start(bf16[1152,384]{1,0:T(8,128)(2,1)S(1)} %pad_maximum_fusion.7), channel_id=1, source_target_pairs={{16,0},{17,1},{18,2},{19,3},{20,4},{21,5},{22,6},{23,7},{24,8},{25... | collective-permute-start | bytes 2654216 | tf_op jit(solution)/shard_map/ppermute | solution.py:768
  220.4 19.2 %collective-permute-start.16 = (bf16[72,2176]{1,0:T(8,128)(2,1)S(1)}, bf16[72,2176]{1,0:T(8,128)(2,1)S(1)}, u32[]{:S(2)}, u32[]{:S(2)}) collective-permute-start(bf16[72,2176]{1,0:T(8,128)(2,1)S(1)} %select_convert_fusion.9), channel_id=1, source_target_pairs={{0,8},{1,9},{2,10},{3,11},{4,12},{5,13},{6,14},{7,15},{8,0},{9,1},... | collective-permute-start | bytes 940040 | tf_op jit(solution)/shard_map/ppermute | solution.py:302
  229.0 15.6 %collective-permute-start.21 = (bf16[272,1088]{1,0:T(8,128)(2,1)S(1)}, bf16[272,1088]{1,0:T(8,128)(2,1)S(1)}, u32[]{:S(2)}, u32[]{:S(2)}) collective-permute-start(bf16[272,1088]{1,0:T(8,128)(2,1)S(1)} %fusion.22), channel_id=1, source_target_pairs={{0,2},{1,3},{2,0},{3,1},{4,6},{5,7},{6,4},{7,5},{8,10},{9,11},{10,... | collective-permute-start | bytes 1775624 | tf_op jit(solution)/shard_map/ppermute | solution.py:302
  239.5 24.0 %collective-permute-start.19 = (bf16[3264,512]{1,0:T(8,128)(2,1)S(1)}, bf16[3264,512]{1,0:T(8,128)(2,1)S(1)}, u32[]{:S(2)}, u32[]{:S(2)}) collective-permute-start(bf16[3264,512]{1,0:T(8,128)(2,1)S(1)} %constant_dynamic-update-slice_fusion), channel_id=1, source_target_pairs={{0,16},{16,0},{1,17},{17,1},{2,18},{18,2},{3,19},{19,3},{4,20},{20... | collective-permute-start | bytes 10027016 | tf_op jit(solution)/shard_map/ppermute | solution.py:243
  239.7 19.8 %collective-permute-start.20 = (bf16[72,2176]{1,0:T(8,128)(2,1)S(1)}, bf16[72,2176]{1,0:T(8,128)(2,1)S(1)}, u32[]{:S(2)}, u32[]{:S(2)}) collective-permute-start(bf16[72,2176]{1,0:T(8,128)(2,1)S(1)} %add_convert_fusion.6), channel_id=1, source_target_pairs={{0,8},{1,9},{2,10},{3,11},{4,12},{5,13},{6,14},{7,15},{8,0},{9,1},... | collective-permute-start | bytes 940040 | tf_op jit(solution)/shard_map/ppermute | solution.py:302
  244.9 12.8 %collective-permute-start.23 = (bf16[136,1088]{1,0:T(8,128)(2,1)S(1)}, bf16[136,1088]{1,0:T(8,128)(2,1)S(1)}, u32[]{:S(2)}, u32[]{:S(2)}) collective-permute-start(bf16[136,1088]{1,0:T(8,128)(2,1)S(1)} %select_convert_fusion.8), channel_id=1, source_target_pairs={{0,1},{1,0},{2,3},{3,2},{4,5},{5,4},{6,7},{7,6},{8,9},{9,8},{10,11... | collective-permute-start | bytes 887816 | tf_op jit(solution)/shard_map/ppermute | solution.py:302
  245.0 12.5 %collective-permute-start.24 = (bf16[136,2176]{1,0:T(8,128)(2,1)S(1)}, bf16[136,2176]{1,0:T(8,128)(2,1)S(1)}, u32[]{:S(2)}, u32[]{:S(2)}) collective-permute-start(bf16[136,2176]{1,0:T(8,128)(2,1)S(1)} %select_convert_fusion.2), channel_id=1, source_target_pairs={{0,2},{1,3},{2,0},{3,1},{4,6},{5,7},{6,4},{7,5},{8,10},{9,11},{10,... | collective-permute-start | bytes 1775624 | tf_op jit(solution)/shard_map/ppermute | solution.py:302
  260.3 13.0 %collective-permute-start.27 = (bf16[72,1088]{1,0:T(8,128)(2,1)S(1)}, bf16[72,1088]{1,0:T(8,128)(2,1)S(1)}, u32[]{:S(2)}, u32[]{:S(2)}) collective-permute-start(bf16[72,1088]{1,0:T(8,128)(2,1)S(1)} %select_convert_fusion.14), channel_id=1, source_target_pairs={{0,4},{1,5},{2,6},{3,7},{4,0},{5,1},{6,2},{7,3},{8,12},{9,13},{10,... | collective-permute-start | bytes 470024 | tf_op jit(solution)/shard_map/ppermute | solution.py:302
  261.7 26.8 %collective-permute-start.32 = (bf16[136,2176]{1,0:T(8,128)(2,1)S(1)}, bf16[136,2176]{1,0:T(8,128)(2,1)S(1)}, u32[]{:S(2)}, u32[]{:S(2)}) collective-permute-start(bf16[136,2176]{1,0:T(8,128)(2,1)S(1)} %pad_maximum_fusion.10), channel_id=1, source_target_pairs={{0,4},{1,5},{2,6},{3,7},{4,0},{5,1},{6,2},{7,3},{8,12},{9,13},{10,... | collective-permute-start | bytes 1775624 | tf_op jit(solution)/shard_map/ppermute | solution.py:302
  273.4 35.6 %collective-permute-start.25 = (bf16[272,1664]{1,0:T(8,128)(2,1)S(1)}, bf16[272,1664]{1,0:T(8,128)(2,1)S(1)}, u32[]{:S(2)}, u32[]{:S(2)}) collective-permute-start(bf16[272,1664]{1,0:T(8,128)(2,1)S(1)} %fusion.21), channel_id=1, source_target_pairs={{0,2},{1,3},{2,0},{3,1},{4,6},{5,7},{6,4},{7,5},{8,10},{9,11},{10,... | collective-permute-start | bytes 2715656 | tf_op jit(solution)/shard_map/ppermute | solution.py:302
  275.2 29.6 %collective-permute-start.29 = (bf16[40,1088]{1,0:T(8,128)(2,1)S(1)}, bf16[40,1088]{1,0:T(8,128)(2,1)S(1)}, u32[]{:S(2)}, u32[]{:S(2)}) collective-permute-start(bf16[40,1088]{1,0:T(8,128)(2,1)S(1)} %select_convert_fusion.17), channel_id=1, source_target_pairs={{0,8},{1,9},{2,10},{3,11},{4,12},{5,13},{6,14},{7,15},{8,0},{9,1},... | collective-permute-start | bytes 261128 | tf_op jit(solution)/shard_map/ppermute | solution.py:302
  275.9 26.9 %collective-permute-start.30 = (bf16[40,2176]{1,0:T(8,128)(2,1)S(1)}, bf16[40,2176]{1,0:T(8,128)(2,1)S(1)}, u32[]{:S(2)}, u32[]{:S(2)}) collective-permute-start(bf16[40,2176]{1,0:T(8,128)(2,1)S(1)} %select_convert_fusion.13), channel_id=1, source_target_pairs={{0,8},{1,9},{2,10},{3,11},{4,12},{5,13},{6,14},{7,15},{8,0},{9,1},... | collective-permute-start | bytes 522248 | tf_op jit(solution)/shard_map/ppermute | solution.py:302
  278.1 23.2 %collective-permute-start.31 = (bf16[272,1600]{1,0:T(8,128)(2,1)S(1)}, bf16[272,1600]{1,0:T(8,128)(2,1)S(1)}, u32[]{:S(2)}, u32[]{:S(2)}) collective-permute-start(bf16[272,1600]{1,0:T(8,128)(2,1)S(1)} %fusion.20), channel_id=1, source_target_pairs={{0,1},{1,0},{2,3},{3,2},{4,5},{5,4},{6,7},{7,6},{8,9},{9,8},{10,11... | collective-permute-start | bytes 2611208 | tf_op jit(solution)/shard_map/ppermute | solution.py:302
  299.8 25.7 %collective-permute-start.37 = (bf16[272,2176]{1,0:T(8,128)(2,1)S(1)}, bf16[272,2176]{1,0:T(8,128)(2,1)S(1)}, u32[]{:S(2)}, u32[]{:S(2)}) collective-permute-start(bf16[272,2176]{1,0:T(8,128)(2,1)S(1)} %pad_maximum_fusion.2), channel_id=1, source_target_pairs={{0,2},{1,3},{2,0},{3,1},{4,6},{5,7},{6,4},{7,5},{8,10},{9,11},{10,... | collective-permute-start | bytes 3551240 | tf_op jit(solution)/shard_map/ppermute | solution.py:302
  301.3 27.3 %collective-permute-start.36 = (bf16[40,2176]{1,0:T(8,128)(2,1)S(1)}, bf16[40,2176]{1,0:T(8,128)(2,1)S(1)}, u32[]{:S(2)}, u32[]{:S(2)}) collective-permute-start(bf16[40,2176]{1,0:T(8,128)(2,1)S(1)} %select_convert_fusion.12), channel_id=1, source_target_pairs={{0,8},{1,9},{2,10},{3,11},{4,12},{5,13},{6,14},{7,15},{8,0},{9,1},... | collective-permute-start | bytes 522248 | tf_op jit(solution)/shard_map/ppermute | solution.py:302
  302.9 32.5 %collective-permute-start.39 = (bf16[40,2176]{1,0:T(8,128)(2,1)S(1)}, bf16[40,2176]{1,0:T(8,128)(2,1)S(1)}, u32[]{:S(2)}, u32[]{:S(2)}) collective-permute-start(bf16[40,2176]{1,0:T(8,128)(2,1)S(1)} %add_convert_fusion.8), channel_id=1, source_target_pairs={{0,8},{1,9},{2,10},{3,11},{4,12},{5,13},{6,14},{7,15},{8,0},{9,1},... | collective-permute-start | bytes 522248 | tf_op jit(solution)/shard_map/ppermute | solution.py:302
  305.5 37.6 %collective-permute-start.42 = (bf16[40,1088]{1,0:T(8,128)(2,1)}, bf16[40,1088]{1,0:T(8,128)(2,1)}, u32[]{:S(2)}, u32[]{:S(2)}) collective-permute-start(bf16[40,1088]{1,0:T(8,128)(2,1)} %add_convert_fusion.11), channel_id=1, source_target_pairs={{0,8},{1,9},{2,10},{3,11},{4,12},{5,13},{6,14},{7,15},{8,0},{9,1},... | collective-permute-start | bytes 261128 | tf_op jit(solution)/shard_map/ppermute | solution.py:302
  309.0 14.0 %collective-permute-start.35 = (bf16[136,1600]{1,0:T(8,128)(2,1)S(1)}, bf16[136,1600]{1,0:T(8,128)(2,1)S(1)}, u32[]{:S(2)}, u32[]{:S(2)}) collective-permute-start(bf16[136,1600]{1,0:T(8,128)(2,1)S(1)} %select_convert_fusion.5), channel_id=1, source_target_pairs={{0,2},{1,3},{2,0},{3,1},{4,6},{5,7},{6,4},{7,5},{8,10},{9,11},{10,... | collective-permute-start | bytes 1305608 | tf_op jit(solution)/shard_map/ppermute | solution.py:302
  327.3 61.0 %collective-permute-start.50 = (bf16[544,2176]{1,0:T(8,128)(2,1)}, bf16[544,2176]{1,0:T(8,128)(2,1)}, u32[]{:S(2)}, u32[]{:S(2)}) collective-permute-start(bf16[544,2176]{1,0:T(8,128)(2,1)} %pad_maximum_fusion.refs_1_), channel_id=1, source_target_pairs={{0,1},{1,0},{2,3},{3,2},{4,5},{5,4},{6,7},{7,6},{8,9},{9,8},{10,11... | collective-permute-start | bytes 7102472 | tf_op jit(solution)/shard_map/ppermute | solution.py:302
  328.6 20.1 %collective-permute-start.40 = (bf16[40,2176]{1,0:T(8,128)(2,1)S(1)}, bf16[40,2176]{1,0:T(8,128)(2,1)}, u32[]{:S(2)}, u32[]{:S(2)}) collective-permute-start(bf16[40,2176]{1,0:T(8,128)(2,1)S(1)} %add_convert_fusion.7), channel_id=1, source_target_pairs={{0,8},{1,9},{2,10},{3,11},{4,12},{5,13},{6,14},{7,15},{8,0},{9,1},... | collective-permute-start | bytes 522248 | tf_op jit(solution)/shard_map/ppermute | solution.py:302
  332.0 15.2 %collective-permute-start.41 = (bf16[72,1600]{1,0:T(8,128)(2,1)}, bf16[72,1600]{1,0:T(8,128)(2,1)}, u32[]{:S(2)}, u32[]{:S(2)}) collective-permute-start(bf16[72,1600]{1,0:T(8,128)(2,1)} %select_convert_fusion.11), channel_id=1, source_target_pairs={{0,4},{1,5},{2,6},{3,7},{4,0},{5,1},{6,2},{7,3},{8,12},{9,13},{10,... | collective-permute-start | bytes 691208 | tf_op jit(solution)/shard_map/ppermute | solution.py:302
  345.1 13.1 %collective-permute-start.47 = (bf16[72,2176]{1,0:T(8,128)(2,1)S(1)}, bf16[72,2176]{1,0:T(8,128)(2,1)S(1)}, u32[]{:S(2)}, u32[]{:S(2)}) collective-permute-start(bf16[72,2176]{1,0:T(8,128)(2,1)S(1)} %copy-done.29), channel_id=1, source_target_pairs={{0,4},{1,5},{2,6},{3,7},{4,0},{5,1},{6,2},{7,3},{8,12},{9,13},{10,... | collective-permute-start | bytes 940040 | tf_op jit(solution)/shard_map/ppermute | solution.py:302
  358.0 15.1 %collective-permute-start.52 = (f32[12,544]{1,0:T(8,128)S(1)}, f32[12,544]{1,0:T(8,128)S(1)}, u32[]{:S(2)}, u32[]{:S(2)}) collective-permute-start(f32[12,544]{1,0:T(8,128)S(1)} %add.314), channel_id=1, source_target_pairs={{0,1},{1,0},{2,3},{3,2},{4,5},{5,4},{6,7},{7,6},{8,9},{9,8},{10,11... | collective-permute-start | bytes 78344 | tf_op jit(solution)/shard_map/ppermute | solution.py:425
  358.1 14.6 %collective-permute-start.53 = (bf16[136,1088]{1,0:T(8,128)(2,1)S(1)}, bf16[136,1088]{1,0:T(8,128)(2,1)S(1)}, u32[]{:S(2)}, u32[]{:S(2)}) collective-permute-start(bf16[136,1088]{1,0:T(8,128)(2,1)S(1)} %pad_maximum_fusion.17), channel_id=1, source_target_pairs={{0,1},{1,0},{2,3},{3,2},{4,5},{5,4},{6,7},{7,6},{8,9},{9,8},{10,11... | collective-permute-start | bytes 887816 | tf_op jit(solution)/shard_map/ppermute | solution.py:302
  365.5 14.5 %collective-permute-start.51 = (bf16[136,2176]{1,0:T(8,128)(2,1)S(1)}, bf16[136,2176]{1,0:T(8,128)(2,1)S(1)}, u32[]{:S(2)}, u32[]{:S(2)}) collective-permute-start(bf16[136,2176]{1,0:T(8,128)(2,1)S(1)} %pad_maximum_fusion.11), channel_id=1, source_target_pairs={{0,2},{1,3},{2,0},{3,1},{4,6},{5,7},{6,4},{7,5},{8,10},{9,11},{10,... | collective-permute-start | bytes 1775624 | tf_op jit(solution)/shard_map/ppermute | solution.py:302
  372.7 15.1 %collective-permute-start.58 = (bf16[136,2176]{1,0:T(8,128)(2,1)S(1)}, bf16[136,2176]{1,0:T(8,128)(2,1)S(1)}, u32[]{:S(2)}, u32[]{:S(2)}) collective-permute-start(bf16[136,2176]{1,0:T(8,128)(2,1)S(1)} %pad_maximum_fusion.12), channel_id=1, source_target_pairs={{0,1},{1,0},{2,3},{3,2},{4,5},{5,4},{6,7},{7,6},{8,9},{9,8},{10,11... | collective-permute-start | bytes 1775624 | tf_op jit(solution)/shard_map/ppermute | solution.py:302
  373.1 11.9 %collective-permute-start.54 = (f32[12,544]{1,0:T(8,128)S(1)}, f32[12,544]{1,0:T(8,128)S(1)}, u32[]{:S(2)}, u32[]{:S(2)}) collective-permute-start(f32[12,544]{1,0:T(8,128)S(1)} %add.317), channel_id=1, source_target_pairs={{0,2},{1,3},{2,0},{3,1},{4,6},{5,7},{6,4},{7,5},{8,10},{9,11},{10,... | collective-permute-start | bytes 78344 | tf_op jit(solution)/shard_map/ppermute | solution.py:425
  385.0 17.1 %collective-permute-start.57 = (bf16[272,1088]{1,0:T(8,128)(2,1)S(1)}, bf16[272,1088]{1,0:T(8,128)(2,1)S(1)}, u32[]{:S(2)}, u32[]{:S(2)}) collective-permute-start(bf16[272,1088]{1,0:T(8,128)(2,1)S(1)} %pad_maximum_fusion.9.refs_1_), channel_id=1, source_target_pairs={{0,2},{1,3},{2,0},{3,1},{4,6},{5,7},{6,4},{7,5},{8,10},{9,11},{10,... | collective-permute-start | bytes 1775624 | tf_op jit(solution)/shard_map/ppermute | solution.py:302
  386.5 46.8 %collective-permute-start.61 = (bf16[272,2176]{1,0:T(8,128)(2,1)S(1)}, bf16[272,2176]{1,0:T(8,128)(2,1)}, u32[]{:S(2)}, u32[]{:S(2)}) collective-permute-start(bf16[272,2176]{1,0:T(8,128)(2,1)S(1)} %pad_maximum_fusion.3.refs_3_), channel_id=1, source_target_pairs={{0,1},{1,0},{2,3},{3,2},{4,5},{5,4},{6,7},{7,6},{8,9},{9,8},{10,11... | collective-permute-start | bytes 3551240 | tf_op jit(solution)/shard_map/ppermute | solution.py:302
  387.8 25.3 %collective-permute-start.63 = (f32[12,544]{1,0:T(8,128)S(1)}, f32[12,544]{1,0:T(8,128)S(1)}, u32[]{:S(2)}, u32[]{:S(2)}) collective-permute-start(f32[12,544]{1,0:T(8,128)S(1)} %add.318), channel_id=1, source_target_pairs={{0,4},{1,5},{2,6},{3,7},{4,0},{5,1},{6,2},{7,3},{8,12},{9,13},{10,... | collective-permute-start | bytes 78344 | tf_op jit(solution)/shard_map/ppermute | solution.py:425
  388.3 24.9 %collective-permute-start.64 = (bf16[136,1600]{1,0:T(8,128)(2,1)}, bf16[136,1600]{1,0:T(8,128)(2,1)}, u32[]{:S(2)}, u32[]{:S(2)}) collective-permute-start(bf16[136,1600]{1,0:T(8,128)(2,1)} %pad_maximum_fusion.13), channel_id=1, source_target_pairs={{0,2},{1,3},{2,0},{3,1},{4,6},{5,7},{6,4},{7,5},{8,10},{9,11},{10,... | collective-permute-start | bytes 1305608 | tf_op jit(solution)/shard_map/ppermute | solution.py:302
  389.7 22.9 %collective-permute-start.56 = (bf16[72,1664]{1,0:T(8,128)(2,1)S(1)}, bf16[72,1664]{1,0:T(8,128)(2,1)S(1)}, u32[]{:S(2)}, u32[]{:S(2)}) collective-permute-start(bf16[72,1664]{1,0:T(8,128)(2,1)S(1)} %pad_maximum_fusion.19), channel_id=1, source_target_pairs={{0,4},{1,5},{2,6},{3,7},{4,0},{5,1},{6,2},{7,3},{8,12},{9,13},{10,... | collective-permute-start | bytes 718856 | tf_op jit(solution)/shard_map/ppermute | solution.py:302
  402.1 31.3 %collective-permute-start.60 = (bf16[272,2176]{1,0:T(8,128)(2,1)S(1)}, bf16[272,2176]{1,0:T(8,128)(2,1)}, u32[]{:S(2)}, u32[]{:S(2)}) collective-permute-start(bf16[272,2176]{1,0:T(8,128)(2,1)S(1)} %pad_maximum_fusion.4.refs_1_), channel_id=1, source_target_pairs={{0,4},{1,5},{2,6},{3,7},{4,0},{5,1},{6,2},{7,3},{8,12},{9,13},{10,... | collective-permute-start | bytes 3551240 | tf_op jit(solution)/shard_map/ppermute | solution.py:302
  415.7 25.4 %collective-permute-start.67 = (bf16[272,1600]{1,0:T(8,128)(2,1)}, bf16[272,1600]{1,0:T(8,128)(2,1)}, u32[]{:S(2)}, u32[]{:S(2)}) collective-permute-start(bf16[272,1600]{1,0:T(8,128)(2,1)} %pad_maximum_fusion.5.refs_3_), channel_id=1, source_target_pairs={{0,1},{1,0},{2,3},{3,2},{4,5},{5,4},{6,7},{7,6},{8,9},{9,8},{10,11... | collective-permute-start | bytes 2611208 | tf_op jit(solution)/shard_map/ppermute | solution.py:302
  424.1 17.0 %collective-permute-start.66 = (bf16[272,1664]{1,0:T(8,128)(2,1)}, bf16[272,1664]{1,0:T(8,128)(2,1)}, u32[]{:S(2)}, u32[]{:S(2)}) collective-permute-start(bf16[272,1664]{1,0:T(8,128)(2,1)} %pad_maximum_fusion.6.refs_1_), channel_id=1, source_target_pairs={{0,2},{1,3},{2,0},{3,1},{4,6},{5,7},{6,4},{7,5},{8,10},{9,11},{10,... | collective-permute-start | bytes 2715656 | tf_op jit(solution)/shard_map/ppermute | solution.py:302
  (83 other events, 489.8 us)
Sparse Core Ops, SparseCore 0:
  9.6 13.8 all-gather.3
  25.0 23.0 all-gather.5
  49.7 26.2 all-gather.7
